TPU v7x, 256 devices: a whole 4x4x8 slice. The times are simulated.
256 devices in a mesh: segment: 8 (over z_hi, x), dp: 32 (over z_lo, y, core).
Axes of the slice: x: 4, y: 4, z: 8 (z_hi: 2, z_lo: 4; z = z_hi * 4 + z_lo), core: 2. Of those that a mesh axis runs over, the one named last changes fastest.
Arguments:
- fine_inflow: bfloat16 [8, 32, 16, 16, 256], P('segment', 'dp'), may hold values from -250 to 250
- coarse_inflow: bfloat16 [8, 32, 8, 8, 512], P('segment', 'dp'), may hold values from -250 to 250
- fine_entries: bfloat16 [3, 32, 16, 16, 256], P(None, 'dp'), may hold values from -250 to 250
- fine_pending: bfloat16 [8, 6, 32, 16, 16, 256], P('segment', None, 'dp'), may hold values from -250 to 250, as said below
- coarse_pending: bfloat16 [8, 2, 32, 8, 8, 512], P('segment', None, 'dp'), may hold values from -250 to 250, as said below
- fine_kernels: bfloat16 [8, 2, 3, 3, 256, 256], P('segment'), may hold values from -0.125 to 0.125
- fine_mixing: bfloat16 [8, 256, 256], P('segment'), may hold values from -0.375 to 0.375
- fine_gains: float32 [8, 2, 256], P('segment'), may hold values from 0.5 to 1.5
- fine_shifts: float32 [8, 2, 256], P('segment'), may hold values from -3 to 3
- coarse_kernel: bfloat16 [8, 3, 3, 512, 512], P('segment'), may hold values from -0.09375 to 0.09375
- coarse_mixing: bfloat16 [8, 512, 512], P('segment'), may hold values from -0.25 to 0.25
- coarse_gains: float32 [8, 512], P('segment'), may hold values from 0.5 to 1.5
- coarse_shifts: float32 [8, 512], P('segment'), may hold values from -3 to 3
- descent_kernel: bfloat16 [2, 2, 256, 512], replicated, may hold values from -0.1875 to 0.1875
- upsample_kernel: bfloat16 [512, 2, 2, 256], replicated, may hold values from -0.25 to 0.25
Outputs:
- fine_stash: bfloat16 [8, 4, 32, 16, 16, 256], P('segment', None, 'dp')
- coarse_stash: bfloat16 [8, 4, 32, 8, 8, 512], P('segment', None, 'dp')
- fine_backlog: bfloat16 [8, 6, 32, 16, 16, 256], P('segment', None, 'dp')
- coarse_backlog: bfloat16 [8, 2, 32, 8, 8, 512], P('segment', None, 'dp')
Inputs may be any that keep to these rules, and one draw needn't show every extreme that they name: `fine_pending`: at segments 4 and above only the first 6 slots are read. `coarse_pending`: at segments below 4 only the first 2 slots are read.
All inputs are finite; a program needn't handle non-finite values.
Results may differ from a plain program's by a relative error of at most 0.017.
Values may be sent and summed in bfloat16 or wider, within the bound.
No kernel may reach another device: no remote copies, remote signals or barrier semaphores. Data moves between devices by JAX's collectives and lax.ppermute only.
A program may use at most 64 MiB of HBM per device.

v0:
```python
import jax
import jax.numpy as jnp
from jax import lax
from jax.sharding import PartitionSpec as P

EPSILON = 1e-05


def copy_for_each(x, axis):
    size = lax.axis_size(axis)
    return lax.all_to_all(jnp.broadcast_to(x[None], (size, *x.shape)), axis, 0, 0, tiled=True)


def taken_together(x, axis):
    everything = copy_for_each(x, axis)
    return jnp.sum(everything, axis=0)


def shifted(block, axis, distance):
    devices = range(lax.axis_size(axis))
    route = [(i - distance, i) for i in devices if i - distance in devices]
    return lax.ppermute(block, axis, route)


def for_sending(x):

    def short(part):
        return part.astype(jnp.bfloat16) if part.dtype == jnp.float32 else part

    return jax.tree.map(short, x)


def passed_along(x, axis, by):
    size = lax.axis_size(axis)
    return lax.ppermute(x, axis, [(i, (i + by) % size) for i in range(size)])


def convolve(images, kernel):
    return lax.conv_general_dilated(
        images,
        kernel,
        (1, 1),
        "SAME",
        dimension_numbers=("NHWC", "HWIO", "NHWC"),
        preferred_element_type=jnp.float32,
    )


def project(images, matrix):
    flat = images.reshape(-1, images.shape[-1])
    result = jnp.dot(flat, matrix, preferred_element_type=jnp.float32)
    return result.reshape(images.shape[:-1] + (matrix.shape[1],))


def descend(images, kernel):
    lowered = lax.conv_general_dilated(
        images,
        kernel,
        (2, 2),
        "VALID",
        dimension_numbers=("NHWC", "HWIO", "NHWC"),
        preferred_element_type=jnp.float32,
    )
    return lowered.astype(jnp.bfloat16)


def upsample(images, kernel):
    batches, height, breadth, coarse = images.shape
    fine_ch = kernel.shape[-1]
    spread = project(images, kernel.reshape(coarse, 4 * fine_ch))
    spread = spread.reshape(batches, height, breadth, 2, 2, fine_ch).transpose(0, 1, 3, 2, 4, 5)
    return spread.reshape(batches, 2 * height, 2 * breadth, fine_ch).astype(jnp.bfloat16)


def normalize(activations, gain_list, shift_list, dp_count):
    widths_list = [member.shape[-1] for member in activations]
    starts = [sum(widths_list[:member_index]) for member_index in range(len(widths_list))]
    inverse = jnp.concatenate(
        [
            jnp.full(
                (member.shape[-1],),
                1.0 / (dp_count * member.shape[1] * member.shape[2]),
                jnp.float32,
            )
            for member in activations
        ]
    )
    totals = jnp.concatenate([jnp.sum(member, axis=(0, 1, 2)) for member in activations])
    squares = jnp.concatenate(
        [jnp.sum(jnp.square(member), axis=(0, 1, 2)) for member in activations]
    )
    joined = taken_together(jnp.concatenate([totals, squares]), "dp")
    centers = joined[: totals.shape[0]] * inverse
    spreads = joined[totals.shape[0] :] * inverse - jnp.square(centers)
    results = []
    for member_index, member in enumerate(activations):
        lower_edge = starts[member_index]
        upper_edge = lower_edge + widths_list[member_index]
        scaled = (member - centers[lower_edge:upper_edge]) * lax.rsqrt(
            spreads[lower_edge:upper_edge] + EPSILON
        ) * gain_list[member_index] + shift_list[member_index]
        results.append(jnp.maximum(scaled, 0.0).astype(jnp.bfloat16))
    return results


def on_device(
    fine_inflow,
    coarse_inflow,
    fine_entries,
    fine_pending,
    coarse_pending,
    fine_kernels,
    fine_mixing,
    fine_gains,
    fine_shifts,
    coarse_kernel,
    coarse_mixing,
    coarse_gains,
    coarse_shifts,
    descent_kernel,
    upsample_kernel,
):
    segment_count = lax.axis_size("segment")
    half_depth = segment_count // 2
    dp_count = lax.axis_size("dp")
    position = lax.axis_index("segment")
    is_lower = position < half_depth
    tick_count = fine_entries.shape[0] + 1
    hold_fine = fine_pending.shape[1]
    recv_fine = 3 * half_depth - hold_fine
    hold_coarse = coarse_pending.shape[1]
    recv_coarse = half_depth - hold_coarse
    fine_slots = [fine_pending[0, slot_index] for slot_index in range(hold_fine)]
    coarse_slots = [coarse_pending[0, slot_index] for slot_index in range(hold_coarse)]
    fine_now = fine_inflow[0]
    coarse_now = coarse_inflow[0]
    zero_fine = jnp.zeros_like(fine_now)
    zero_coarse = jnp.zeros_like(coarse_now)
    fine_made = []
    coarse_made = []
    fine_arrived = []
    coarse_arrived = []
    fine_store = []
    coarse_store = []
    first_count = min(tick_count, hold_fine)
    early_tiles = shifted(jnp.stack(fine_slots[:first_count]), "segment", half_depth)
    fine_arrived = [early_tiles[slot_index] for slot_index in range(first_count)]
    for tick_now in range(tick_count):
        if tick_now > 0:
            fine_send, coarse_send = lax.cond(
                position == half_depth - 1,
                lambda: (
                    upsample(coarse_store[-1], upsample_kernel),
                    descend(fine_store[-1], descent_kernel),
                ),
                lambda: (fine_store[-1], coarse_store[-1]),
            )
            fine_recv = shifted(fine_send, "segment", 1)
            coarse_recv = jax.tree.map(
                lambda part, own: part.astype(own.dtype),
                passed_along(for_sending(coarse_send), "segment", 1),
                coarse_send,
            )
            fine_now = jnp.where(position == 0, fine_entries[tick_now - 1], fine_recv)
            coarse_now = coarse_recv
        fine_outgoing = fine_slots[tick_now]
        coarse_outgoing = (
            coarse_slots[tick_now]
            if tick_now < hold_coarse
            else coarse_made[tick_now - hold_coarse]
        )
        coarse_arrived.append(shifted(coarse_outgoing, "segment", -half_depth))
        fine_taken = fine_slots[tick_now]
        coarse_taken = (
            coarse_slots[tick_now]
            if tick_now < recv_coarse
            else coarse_arrived[tick_now - recv_coarse]
        )
        fine_input = lax.cond(
            is_lower,
            lambda: fine_now,
            lambda: (project(fine_now, fine_mixing[0]) + fine_taken.astype(jnp.float32)).astype(
                jnp.bfloat16
            ),
        )
        coarse_input = lax.cond(
            is_lower,
            lambda: (
                project(coarse_now, coarse_mixing[0]) + coarse_taken.astype(jnp.float32)
            ).astype(jnp.bfloat16),
            lambda: coarse_now,
        )
        fine_first, coarse_out = normalize(
            [convolve(fine_input, fine_kernels[0, 0]), convolve(coarse_input, coarse_kernel[0])],
            [fine_gains[0, 0], coarse_gains[0]],
            [fine_shifts[0, 0], coarse_shifts[0]],
            dp_count,
        )
        fine_out = normalize(
            [convolve(fine_first, fine_kernels[0, 1])],
            [fine_gains[0, 1]],
            [fine_shifts[0, 1]],
            dp_count,
        )[0]
        fine_made.append(
            lax.cond(
                is_lower,
                lambda: project(fine_out, fine_mixing[0]).astype(jnp.bfloat16),
                lambda: zero_fine,
            )
        )
        coarse_made.append(
            lax.cond(
                is_lower,
                lambda: zero_coarse,
                lambda: project(coarse_out, coarse_mixing[0]).astype(jnp.bfloat16),
            )
        )
        fine_store.append(fine_out)
        coarse_store.append(coarse_out)
    sender_fine = fine_slots + fine_made
    receiver_fine = fine_slots[:recv_fine] + fine_arrived
    sender_coarse = coarse_slots + coarse_made
    receiver_coarse = coarse_slots[:recv_coarse] + coarse_arrived
    fine_backlog = []
    for slot_index in range(hold_fine):
        kept_side = receiver_fine[tick_count + slot_index]
        fine_backlog.append(jnp.where(is_lower, sender_fine[tick_count + slot_index], kept_side))
    coarse_backlog = []
    for slot_index in range(hold_coarse):
        kept_side = receiver_coarse[tick_count + slot_index]
        coarse_backlog.append(
            jnp.where(is_lower, kept_side, sender_coarse[tick_count + slot_index])
        )
    fine_stash = jnp.stack(fine_store)[None]
    coarse_stash = jnp.stack(coarse_store)[None]
    return (
        fine_stash,
        coarse_stash,
        jnp.stack(fine_backlog)[None],
        jnp.stack(coarse_backlog)[None],
    )


def solution(mesh):
    placed = (
        P("segment", "dp", None, None, None),
        P("segment", "dp", None, None, None),
        P(None, "dp", None, None, None),
        P("segment", None, "dp", None, None, None),
        P("segment", None, "dp", None, None, None),
        P("segment", None, None, None, None, None),
        P("segment", None, None),
        P("segment", None, None),
        P("segment", None, None),
        P("segment", None, None, None, None),
        P("segment", None, None),
        P("segment", None),
        P("segment", None),
        P(),
        P(),
    )
    return jax.shard_map(
        on_device,
        mesh=mesh,
        in_specs=placed,
        out_specs=(
            P("segment", None, "dp", None, None, None),
            P("segment", None, "dp", None, None, None),
            P("segment", None, "dp", None, None, None),
            P("segment", None, "dp", None, None, None),
        ),
        check_vma=False,
    )
```

profile of v0, /device:TPU:32, one launch (start us, length us, event | category | flops | bytes accessed | tf_op | source)
XLA Modules:
  0.0 231.4 jit_solution(10500664118746317472)
XLA Ops:
  5.6 5.4 %fusion.279 = (f32[512]{0:T(512)S(1)}, f32[512]{0:T(512)S(1)}, f32[1,8,8,512]{3,0,2,1:T(1,128)}) fusion(bf16[1,8,8,512]{3,0,2,1:T(2,128)(2,1)S(1)} %get-tuple-element.490, bf16[1,3,3,512,512]{4,3,2,1,0:T(8,128)(2,1)} %param.62), kind=kOutput, calls=%fused_computation.397 | convolution fusion | flops 253852672 | bytes 4919296 | tf_op jit(solution)/shard_map/conv_general_dilated | solution.py:39
  12.6 8.8 %all-to-all-start = ((f32[32,1,1536]{2,1,0:T(1,128)}), f32[32,1,1536]{2,1,0:T(1,128)S(1)}, u32[]{:S(2)}, u32[]{:S(2)}) async-start(f32[32,1,1536]{2,1,0:T(1,128)} %broadcast_in_dim.44), calls=%async_computation | async-start | bytes 393216 | tf_op jit(solution)/shard_map/all_to_all | solution.py:11
  22.5 7.3 %all-to-all-done = f32[32,1,1536]{2,1,0:T(1,128)S(1)} async-done(((f32[32,1,1536]{2,1,0:T(1,128)}), f32[32,1,1536]{2,1,0:T(1,128)S(1)}, u32[]{:S(2)}, u32[]{:S(2)}) %all-to-all-start) | async-done | bytes 196640 | tf_op jit(solution)/shard_map/all_to_all | solution.py:11
  34.9 5.1 %all-to-all-start.1 = ((f32[32,1,512]{2,1,0:T(1,128)}), f32[32,1,512]{2,1,0:T(1,128)S(1)}, u32[]{:S(2)}, u32[]{:S(2)}) async-start(f32[32,1,512]{2,1,0:T(1,128)} %broadcast_in_dim.45), calls=%async_computation.1 | async-start | bytes 131072 | tf_op jit(solution)/shard_map/all_to_all | solution.py:11
  40.3 6.4 %all-to-all-done.1 = f32[32,1,512]{2,1,0:T(1,128)S(1)} async-done(((f32[32,1,512]{2,1,0:T(1,128)}), f32[32,1,512]{2,1,0:T(1,128)S(1)}, u32[]{:S(2)}, u32[]{:S(2)}) %all-to-all-start.1) | async-done | bytes 65568 | tf_op jit(solution)/shard_map/all_to_all | solution.py:11
  51.5 4.1 %collective-permute-start = (bf16[1,16,16,256]{3,2,1,0:T(8,128)(2,1)}, bf16[1,16,16,256]{3,2,1,0:T(8,128)(2,1)}, u32[]{:S(2)}, u32[]{:S(2)}) collective-permute-start(bf16[1,16,16,256]{3,2,1,0:T(8,128)(2,1)} %get-tuple-element.238), channel_id=1, source_target_pairs={{0,32},{32,64},{64,96},{96,128},{128,160},{160,192},{192,224},{1,3... | collective-permute-start | bytes 393224 | tf_op jit(solution)/shard_map/ppermute | solution.py:22
  55.5 6.3 %collective-permute-done.1 = bf16[1,8,8,512]{3,2,1,0:T(8,128)(2,1)S(1)} collective-permute-done((bf16[1,8,8,512]{3,2,1,0:T(8,128)(2,1)}, bf16[1,8,8,512]{3,2,1,0:T(8,128)(2,1)S(1)}, u32[]{:S(2)}, u32[]{:S(2)}) %collective-permute-start.1) | collective-permute-done | bytes 65568 | tf_op jit(solution)/shard_map/ppermute | solution.py:35
  63.0 5.9 %fusion.278 = (f32[512]{0:T(512)}, f32[512]{0:T(512)}, f32[1,8,8,512]{3,0,2,1:T(1,128)}) fusion(bf16[1,8,8,512]{3,0,2,1:T(2,128)(2,1)S(1)} %get-tuple-element.491, bf16[1,3,3,512,512]{4,3,2,1,0:T(8,128)(2,1)} %param.62), kind=kOutput, calls=%fused_computation.396 | convolution fusion | flops 253852672 | bytes 4919296 | tf_op jit(solution)/shard_map/conv_general_dilated | solution.py:39
  73.5 4.1 %all-to-all-start.2 = ((f32[32,1,1536]{2,1,0:T(1,128)}), f32[32,1,1536]{2,1,0:T(1,128)S(1)}, u32[]{:S(2)}, u32[]{:S(2)}) async-start(f32[32,1,1536]{2,1,0:T(1,128)} %broadcast_in_dim.46), calls=%async_computation.2 | async-start | bytes 393216 | tf_op jit(solution)/shard_map/all_to_all | solution.py:11
  82.2 11.4 %collective-permute-start.8 = (bf16[4,1,16,16,256]{4,3,2,1,0:T(8,128)(2,1)}, bf16[4,1,16,16,256]{4,3,2,1,0:T(8,128)(2,1)}, u32[]{:S(2)}, u32[]{:S(2)}) collective-permute-start(bf16[4,1,16,16,256]{4,3,2,1,0:T(8,128)(2,1)} %pad_maximum_fusion), channel_id=1, source_target_pairs={{0,128},{32,160},{64,192},{96,224},{1,129},{33,161},{65,193},{97,2... | collective-permute-start | bytes 1572872 | tf_op jit(solution)/shard_map/ppermute | solution.py:22
  99.9 7.7 %all-to-all-start.3 = ((f32[32,1,512]{2,1,0:T(1,128)}), f32[32,1,512]{2,1,0:T(1,128)S(1)}, u32[]{:S(2)}, u32[]{:S(2)}) async-start(f32[32,1,512]{2,1,0:T(1,128)} %broadcast_in_dim.47), calls=%async_computation.3 | async-start | bytes 131072 | tf_op jit(solution)/shard_map/all_to_all | solution.py:11
  107.9 8.9 %all-to-all-done.3 = f32[32,1,512]{2,1,0:T(1,128)S(1)} async-done(((f32[32,1,512]{2,1,0:T(1,128)}), f32[32,1,512]{2,1,0:T(1,128)S(1)}, u32[]{:S(2)}, u32[]{:S(2)}) %all-to-all-start.3) | async-done | bytes 65568 | tf_op jit(solution)/shard_map/all_to_all | solution.py:11
  125.7 4.9 %collective-permute-done.3 = bf16[1,8,8,512]{3,2,1,0:T(8,128)(2,1)} collective-permute-done((bf16[1,8,8,512]{3,2,1,0:T(8,128)(2,1)}, bf16[1,8,8,512]{3,2,1,0:T(8,128)(2,1)}, u32[]{:S(2)}, u32[]{:S(2)}) %collective-permute-start.3) | collective-permute-done | bytes 65568 | tf_op jit(solution)/shard_map/ppermute | solution.py:35
  132.4 5.9 %fusion.277 = (f32[512]{0:T(512)}, f32[512]{0:T(512)}, f32[1,8,8,512]{3,0,2,1:T(1,128)}) fusion(bf16[1,8,8,512]{3,0,2,1:T(2,128)(2,1)} %get-tuple-element.492, bf16[1,3,3,512,512]{4,3,2,1,0:T(8,128)(2,1)} %param.62), kind=kOutput, calls=%fused_computation.395 | convolution fusion | flops 253852672 | bytes 4919296 | tf_op jit(solution)/shard_map/conv_general_dilated | solution.py:39
  143.0 9.2 %all-to-all-start.4 = ((f32[32,1,1536]{2,1,0:T(1,128)}), f32[32,1,1536]{2,1,0:T(1,128)S(1)}, u32[]{:S(2)}, u32[]{:S(2)}) async-start(f32[32,1,1536]{2,1,0:T(1,128)} %broadcast_in_dim.48), calls=%async_computation.4 | async-start | bytes 393216 | tf_op jit(solution)/shard_map/all_to_all | solution.py:11
  156.7 4.0 %all-to-all-done.4 = f32[32,1,1536]{2,1,0:T(1,128)S(1)} async-done(((f32[32,1,1536]{2,1,0:T(1,128)}), f32[32,1,1536]{2,1,0:T(1,128)S(1)}, u32[]{:S(2)}, u32[]{:S(2)}) %all-to-all-start.4) | async-done | bytes 196640 | tf_op jit(solution)/shard_map/all_to_all | solution.py:11
  164.7 5.1 %all-to-all-start.5 = ((f32[32,1,512]{2,1,0:T(1,128)}), f32[32,1,512]{2,1,0:T(1,128)S(1)}, u32[]{:S(2)}, u32[]{:S(2)}) async-start(f32[32,1,512]{2,1,0:T(1,128)} %broadcast_in_dim.49), calls=%async_computation.5 | async-start | bytes 131072 | tf_op jit(solution)/shard_map/all_to_all | solution.py:11
  171.0 5.6 %all-to-all-done.5 = f32[32,1,512]{2,1,0:T(1,128)S(1)} async-done(((f32[32,1,512]{2,1,0:T(1,128)}), f32[32,1,512]{2,1,0:T(1,128)S(1)}, u32[]{:S(2)}, u32[]{:S(2)}) %all-to-all-start.5) | async-done | bytes 65568 | tf_op jit(solution)/shard_map/all_to_all | solution.py:11
  181.9 8.9 %collective-permute-done.6 = bf16[1,8,8,512]{3,2,1,0:T(8,128)(2,1)S(1)} collective-permute-done((bf16[1,8,8,512]{3,2,1,0:T(8,128)(2,1)S(1)}, bf16[1,8,8,512]{3,2,1,0:T(8,128)(2,1)S(1)}, u32[]{:S(2)}, u32[]{:S(2)}) %collective-permute-start.6) | collective-permute-done | bytes 65568 | tf_op jit(solution)/shard_map/ppermute | solution.py:35
  192.0 4.6 %fusion.276 = (f32[512]{0:T(512)S(1)}, f32[512]{0:T(512)S(1)}, f32[1,8,8,512]{3,0,2,1:T(1,128)S(1)}) fusion(bf16[1,8,8,512]{3,0,2,1:T(2,128)(2,1)S(1)} %get-tuple-element.493, bf16[1,3,3,512,512]{4,3,2,1,0:T(8,128)(2,1)} %param.62), kind=kOutput, calls=%fused_computation.394 | convolution fusion | flops 253852672 | bytes 4919296 | tf_op jit(solution)/shard_map/conv_general_dilated | solution.py:39
  200.6 4.1 %all-to-all-start.6 = ((f32[32,1,1536]{2,1,0:T(1,128)}), f32[32,1,1536]{2,1,0:T(1,128)S(1)}, u32[]{:S(2)}, u32[]{:S(2)}) async-start(f32[32,1,1536]{2,1,0:T(1,128)} %broadcast_in_dim.50), calls=%async_computation.6 | async-start | bytes 393216 | tf_op jit(solution)/shard_map/all_to_all | solution.py:11
  207.4 5.8 %all-to-all-done.6 = f32[32,1,1536]{2,1,0:T(1,128)S(1)} async-done(((f32[32,1,1536]{2,1,0:T(1,128)}), f32[32,1,1536]{2,1,0:T(1,128)S(1)}, u32[]{:S(2)}, u32[]{:S(2)}) %all-to-all-start.6) | async-done | bytes 196640 | tf_op jit(solution)/shard_map/all_to_all | solution.py:11
  216.4 5.1 %all-to-all-start.7 = ((f32[32,1,512]{2,1,0:T(1,128)}), f32[32,1,512]{2,1,0:T(1,128)S(1)}, u32[]{:S(2)}, u32[]{:S(2)}) async-start(f32[32,1,512]{2,1,0:T(1,128)} %broadcast_in_dim.52), calls=%async_computation.7 | async-start | bytes 131072 | tf_op jit(solution)/shard_map/all_to_all | solution.py:11
  223.9 4.4 %all-to-all-done.7 = f32[32,1,512]{2,1,0:T(1,128)S(1)} async-done(((f32[32,1,512]{2,1,0:T(1,128)}), f32[32,1,512]{2,1,0:T(1,128)S(1)}, u32[]{:S(2)}, u32[]{:S(2)}) %all-to-all-start.7) | async-done | bytes 65568 | tf_op jit(solution)/shard_map/all_to_all | solution.py:11
  (274 shorter events, 91.1 us)
Async XLA Ops:
  12.6 17.2 %all-to-all-start = ((f32[32,1,1536]{2,1,0:T(1,128)}), f32[32,1,1536]{2,1,0:T(1,128)S(1)}, u32[]{:S(2)}, u32[]{:S(2)}) async-start(f32[32,1,1536]{2,1,0:T(1,128)} %broadcast_in_dim.44), calls=%async_computation | async-start | bytes 393216 | tf_op jit(solution)/shard_map/all_to_all | solution.py:11
  34.9 11.9 %all-to-all-start.1 = ((f32[32,1,512]{2,1,0:T(1,128)}), f32[32,1,512]{2,1,0:T(1,128)S(1)}, u32[]{:S(2)}, u32[]{:S(2)}) async-start(f32[32,1,512]{2,1,0:T(1,128)} %broadcast_in_dim.45), calls=%async_computation.1 | async-start | bytes 131072 | tf_op jit(solution)/shard_map/all_to_all | solution.py:11
  50.0 11.8 %collective-permute-start.1 = (bf16[1,8,8,512]{3,2,1,0:T(8,128)(2,1)}, bf16[1,8,8,512]{3,2,1,0:T(8,128)(2,1)S(1)}, u32[]{:S(2)}, u32[]{:S(2)}) collective-permute-start(bf16[1,8,8,512]{3,2,1,0:T(8,128)(2,1)} %get-tuple-element.239), channel_id=1, source_target_pairs={{0,32},{32,64},{64,96},{96,128},{128,160},{160,192},{192,224},{224... | collective-permute-start | bytes 196616 | tf_op jit(solution)/shard_map/ppermute | solution.py:35
  51.5 17.4 %collective-permute-start = (bf16[1,16,16,256]{3,2,1,0:T(8,128)(2,1)}, bf16[1,16,16,256]{3,2,1,0:T(8,128)(2,1)}, u32[]{:S(2)}, u32[]{:S(2)}) collective-permute-start(bf16[1,16,16,256]{3,2,1,0:T(8,128)(2,1)} %get-tuple-element.238), channel_id=1, source_target_pairs={{0,32},{32,64},{64,96},{96,128},{128,160},{160,192},{192,224},{1,3... | collective-permute-start | bytes 393224 | tf_op jit(solution)/shard_map/ppermute | solution.py:22
  70.0 25.3 %copy-start.28 = (f32[1,1,256]{2,1,0:T(1,128)S(1)}, f32[1,1,256]{2,1,0:T(1,128)}, u32[]{:S(2)}) copy-start(f32[1,1,256]{2,1,0:T(1,128)} %copy-done.27) | copy-start | bytes 3076
  70.0 25.3 %copy-start.32 = (f32[1,1,256]{2,1,0:T(1,128)S(1)}, f32[1,1,256]{2,1,0:T(1,128)}, u32[]{:S(2)}) copy-start(f32[1,1,256]{2,1,0:T(1,128)} %copy-done.31) | copy-start | bytes 3076
  70.0 25.3 %copy-start.38 = (pred[8,3]{0,1:T(4,128)(4,1)S(1)}, pred[8,3]{0,1:T(4,128)(4,1)}, u32[]{:S(2)}) copy-start(pred[8,3]{0,1:T(4,128)(4,1)} %constant.110) | copy-start | bytes 76
  73.5 21.6 %all-to-all-start.2 = ((f32[32,1,1536]{2,1,0:T(1,128)}), f32[32,1,1536]{2,1,0:T(1,128)S(1)}, u32[]{:S(2)}, u32[]{:S(2)}) async-start(f32[32,1,1536]{2,1,0:T(1,128)} %broadcast_in_dim.46), calls=%async_computation.2 | async-start | bytes 393216 | tf_op jit(solution)/shard_map/all_to_all | solution.py:11
  77.7 46.0 %collective-permute-start.4 = (bf16[1,8,8,512]{3,2,1,0:T(8,128)(2,1)}, bf16[1,8,8,512]{3,2,1,0:T(8,128)(2,1)}, u32[]{:S(2)}, u32[]{:S(2)}) collective-permute-start(bf16[1,8,8,512]{3,2,1,0:T(8,128)(2,1)} %get-tuple-element.543), channel_id=1, source_target_pairs={{128,0},{160,32},{192,64},{224,96},{129,1},{161,33},{193,65},{225,... | collective-permute-start | bytes 196616 | tf_op jit(solution)/shard_map/ppermute | solution.py:22
  79.0 102.9 %collective-permute-start.7 = (bf16[1,8,8,512]{3,2,1,0:T(8,128)(2,1)}, bf16[1,8,8,512]{3,2,1,0:T(8,128)(2,1)}, u32[]{:S(2)}, u32[]{:S(2)}) collective-permute-start(bf16[1,8,8,512]{3,2,1,0:T(8,128)(2,1)} %get-tuple-element.542), channel_id=1, source_target_pairs={{128,0},{160,32},{192,64},{224,96},{129,1},{161,33},{193,65},{225,... | collective-permute-start | bytes 196616 | tf_op jit(solution)/shard_map/ppermute | solution.py:22
  82.2 70.1 %collective-permute-start.8 = (bf16[4,1,16,16,256]{4,3,2,1,0:T(8,128)(2,1)}, bf16[4,1,16,16,256]{4,3,2,1,0:T(8,128)(2,1)}, u32[]{:S(2)}, u32[]{:S(2)}) collective-permute-start(bf16[4,1,16,16,256]{4,3,2,1,0:T(8,128)(2,1)} %pad_maximum_fusion), channel_id=1, source_target_pairs={{0,128},{32,160},{64,192},{96,224},{1,129},{33,161},{65,193},{97,2... | collective-permute-start | bytes 1572872 | tf_op jit(solution)/shard_map/ppermute | solution.py:22
  96.5 20.3 %copy-start.20 = (f32[1,1,256]{2,1,0:T(1,128)S(1)}, f32[1,1,256]{2,1,0:T(1,128)}, u32[]{:S(2)}) copy-start(f32[1,1,256]{2,1,0:T(1,128)} %get-tuple-element.562) | copy-start | bytes 3076
  96.5 20.3 %copy-start.24 = (f32[1,1,256]{2,1,0:T(1,128)S(1)}, f32[1,1,256]{2,1,0:T(1,128)}, u32[]{:S(2)}) copy-start(f32[1,1,256]{2,1,0:T(1,128)} %get-tuple-element.560) | copy-start | bytes 3076
  99.9 16.8 %all-to-all-start.3 = ((f32[32,1,512]{2,1,0:T(1,128)}), f32[32,1,512]{2,1,0:T(1,128)S(1)}, u32[]{:S(2)}, u32[]{:S(2)}) async-start(f32[32,1,512]{2,1,0:T(1,128)} %broadcast_in_dim.47), calls=%async_computation.3 | async-start | bytes 131072 | tf_op jit(solution)/shard_map/all_to_all | solution.py:11
  120.0 10.6 %collective-permute-start.3 = (bf16[1,8,8,512]{3,2,1,0:T(8,128)(2,1)}, bf16[1,8,8,512]{3,2,1,0:T(8,128)(2,1)}, u32[]{:S(2)}, u32[]{:S(2)}) collective-permute-start(bf16[1,8,8,512]{3,2,1,0:T(8,128)(2,1)} %get-tuple-element.241), channel_id=1, source_target_pairs={{0,32},{32,64},{64,96},{96,128},{128,160},{160,192},{192,224},{224... | collective-permute-start | bytes 196616 | tf_op jit(solution)/shard_map/ppermute | solution.py:35
  122.2 82.5 %collective-permute-start.9 = (bf16[1,8,8,512]{3,2,1,0:T(8,128)(2,1)}, bf16[1,8,8,512]{3,2,1,0:T(8,128)(2,1)}, u32[]{:S(2)}, u32[]{:S(2)}) collective-permute-start(bf16[1,8,8,512]{3,2,1,0:T(8,128)(2,1)} %get-tuple-element.608), channel_id=1, source_target_pairs={{128,0},{160,32},{192,64},{224,96},{129,1},{161,33},{193,65},{225,... | collective-permute-start | bytes 196616 | tf_op jit(solution)/shard_map/ppermute | solution.py:22
  123.7 14.6 %collective-permute-start.2 = (bf16[1,16,16,256]{3,2,1,0:T(8,128)(2,1)}, bf16[1,16,16,256]{3,2,1,0:T(8,128)(2,1)}, u32[]{:S(2)}, u32[]{:S(2)}) collective-permute-start(bf16[1,16,16,256]{3,2,1,0:T(8,128)(2,1)} %get-tuple-element.240), channel_id=1, source_target_pairs={{0,32},{32,64},{64,96},{96,128},{128,160},{160,192},{192,224},{1,3... | collective-permute-start | bytes 393224 | tf_op jit(solution)/shard_map/ppermute | solution.py:22
  143.0 17.7 %all-to-all-start.4 = ((f32[32,1,1536]{2,1,0:T(1,128)}), f32[32,1,1536]{2,1,0:T(1,128)S(1)}, u32[]{:S(2)}, u32[]{:S(2)}) async-start(f32[32,1,1536]{2,1,0:T(1,128)} %broadcast_in_dim.48), calls=%async_computation.4 | async-start | bytes 393216 | tf_op jit(solution)/shard_map/all_to_all | solution.py:11
  154.5 67.1 %collective-permute-start.10 = (bf16[1,8,8,512]{3,2,1,0:T(8,128)(2,1)}, bf16[1,8,8,512]{3,2,1,0:T(8,128)(2,1)}, u32[]{:S(2)}, u32[]{:S(2)}) collective-permute-start(bf16[1,8,8,512]{3,2,1,0:T(8,128)(2,1)} %get-tuple-element.610), channel_id=1, source_target_pairs={{128,0},{160,32},{192,64},{224,96},{129,1},{161,33},{193,65},{225,... | collective-permute-start | bytes 196616 | tf_op jit(solution)/shard_map/ppermute | solution.py:22
  164.7 11.9 %all-to-all-start.5 = ((f32[32,1,512]{2,1,0:T(1,128)}), f32[32,1,512]{2,1,0:T(1,128)S(1)}, u32[]{:S(2)}, u32[]{:S(2)}) async-start(f32[32,1,512]{2,1,0:T(1,128)} %broadcast_in_dim.49), calls=%async_computation.5 | async-start | bytes 131072 | tf_op jit(solution)/shard_map/all_to_all | solution.py:11
  176.9 13.9 %collective-permute-start.6 = (bf16[1,8,8,512]{3,2,1,0:T(8,128)(2,1)S(1)}, bf16[1,8,8,512]{3,2,1,0:T(8,128)(2,1)S(1)}, u32[]{:S(2)}, u32[]{:S(2)}) collective-permute-start(bf16[1,8,8,512]{3,2,1,0:T(8,128)(2,1)S(1)} %get-tuple-element.243), channel_id=1, source_target_pairs={{0,32},{32,64},{64,96},{96,128},{128,160},{160,192},{192,224},{224... | collective-permute-start | bytes 196616 | tf_op jit(solution)/shard_map/ppermute | solution.py:35
  179.9 16.7 %collective-permute-start.5 = (bf16[1,16,16,256]{3,2,1,0:T(8,128)(2,1)S(1)}, bf16[1,16,16,256]{3,2,1,0:T(8,128)(2,1)S(1)}, u32[]{:S(2)}, u32[]{:S(2)}) collective-permute-start(bf16[1,16,16,256]{3,2,1,0:T(8,128)(2,1)S(1)} %get-tuple-element.242), channel_id=1, source_target_pairs={{0,32},{32,64},{64,96},{96,128},{128,160},{160,192},{192,224},{1,3... | collective-permute-start | bytes 393224 | tf_op jit(solution)/shard_map/ppermute | solution.py:22
  200.6 12.6 %all-to-all-start.6 = ((f32[32,1,1536]{2,1,0:T(1,128)}), f32[32,1,1536]{2,1,0:T(1,128)S(1)}, u32[]{:S(2)}, u32[]{:S(2)}) async-start(f32[32,1,1536]{2,1,0:T(1,128)} %broadcast_in_dim.50), calls=%async_computation.6 | async-start | bytes 393216 | tf_op jit(solution)/shard_map/all_to_all | solution.py:11
  216.4 11.9 %all-to-all-start.7 = ((f32[32,1,512]{2,1,0:T(1,128)}), f32[32,1,512]{2,1,0:T(1,128)S(1)}, u32[]{:S(2)}, u32[]{:S(2)}) async-start(f32[32,1,512]{2,1,0:T(1,128)} %broadcast_in_dim.52), calls=%async_computation.7 | async-start | bytes 131072 | tf_op jit(solution)/shard_map/all_to_all | solution.py:11
  (43 other events, 440.0 us)
where the time goes:
time: 236 us; the launch traced here: 231 us
  starting transfers between devices  76.8 us (33%)
  waiting for transfers between devices  62.6 us (27%)
  matrix products  44.1 us (19%)
  local copies, waits for them, and re-layouts  23.3 us (10%)
  other arithmetic  22.4 us (9%)
    all_to_all x8, starting transfers between devices, copy_for_each(): lax.all_to_all(jnp.broadcast_to(x[None], (size, *x.shape)), axis, 0, 0, t...  49.4 us
    all_to_all x8, waiting for transfers between devices, copy_for_each(): lax.all_to_all(jnp.broadcast_to(x[None], (size, *x.shape)), axis, 0, 0, t...  42.4 us
    conv_general_dilated x12, matrix products, convolve(): lax.conv_general_dilated(images, kernel, (1, 1), 'SAME', dimension_number...  39.2 us
    ppermute x8, starting transfers between devices, shifted(): return lax.ppermute(block, axis, route)  24.5 us
    ppermute x3, waiting for transfers between devices, passed_along(): return lax.ppermute(x, axis, [(i, (i + by) % size) for i in range(size)])  20.1 us
    convert_element_type x12, other arithmetic, normalize(): results.append(jnp.maximum(scaled, 0.0).astype(jnp.bfloat16))  6.54 us
    broadcast_in_dim x8, local copies, waits for them, and re-layouts, copy_for_each(): jnp.broadcast_to(x[None], (size, *x.shape))  5.78 us
    unnamed x4, other arithmetic  5.53 us
  transfers between devices with their start and end apart: 19, of which 10 were waited for; matrix products, arithmetic and copies ran while one was open for 27% of the time, Pallas kernels for 0%

commit v1 on v0

v1 whole, which is shorter than its diff:
```python
import functools

import jax
import jax.numpy as jnp
from jax import lax
from jax.experimental import pallas as pl
from jax.experimental.pallas import tpu as pltpu
from jax.sharding import PartitionSpec as P

EPSILON = 1e-05
BF16 = jnp.bfloat16
F32 = jnp.float32
LIMIT = 24 * 1024 * 1024

SIDE, CSIDE = 16, 8
CELLS, CCELLS = SIDE * SIDE, CSIDE * CSIDE
FCH, CCH = 256, 512
N_DP = 32
HALF = 4
LAST = 2 * HALF - 1
TICKS = 4


def call(body, outs, in_specs, scratch=(), flops=0, moved=0, aliases=None):
    kernel = pl.pallas_call(
        body,
        out_shape=[space(*rest) if len(rest) == 2 else space(*rest, BF16) for space, *rest in outs],
        in_specs=in_specs,
        out_specs=[VM if space is pltpu.VMEM else ANY for space, *_ in outs],
        scratch_shapes=list(scratch),
        input_output_aliases=aliases or {},
        compiler_params=pltpu.CompilerParams(vmem_limit_bytes=LIMIT),
        cost_estimate=pl.CostEstimate(flops=flops, bytes_accessed=moved, transcendentals=0),
    )
    spaces = {id(VM): pltpu.VMEM, id(ANY): pltpu.HBM}

    def placed(spec, x):
        return pltpu.with_memory_space_constraint(x, spaces[id(spec)]) if id(spec) in spaces else x

    return lambda *args: kernel(*[placed(spec, arg) for spec, arg in zip(in_specs, args, strict=True)])


VM = pl.BlockSpec(memory_space=pltpu.VMEM)
SM = pl.BlockSpec(memory_space=pltpu.SMEM)
ANY = pl.BlockSpec(memory_space=pl.ANY)


def dot(a, b):
    return jnp.dot(a, b, preferred_element_type=F32)


def lanes(rows):
    return jnp.concatenate([rows[i : i + 1] for i in range(rows.shape[0])], axis=1)


def rows_of(line):
    return [line[:, i : i + 128] for i in range(0, line.shape[1], 128)]


def with_neighbours(x, width):
    count = x.shape[0]
    column = lax.broadcasted_iota(jnp.int32, x.shape, 0) & (width - 1)
    left = jnp.where(column == 0, 0.0, pltpu.roll(x, 1, 0))
    right = jnp.where(column == width - 1, 0.0, pltpu.roll(x, count - 1, 0))
    return left, x, right


class Streamed:
    def __init__(self, source, held, sems):
        self.held = held
        self.copies = [
            pltpu.make_async_copy(source.at[i], held.at[i], sems.at[i]) for i in range(held.shape[0])
        ]

    def start(self):
        for copy in self.copies:
            copy.start()
        return self

    def __getitem__(self, i):
        self.copies[i].wait()
        return self.held[i]


def fine_convolution(x, padded, kernel):
    edge = jnp.zeros((SIDE, 3 * FCH), BF16)
    padded[0:SIDE, :] = edge
    padded[SIDE + CELLS : 2 * SIDE + CELLS, :] = edge
    for i, piece in enumerate(with_neighbours(x, SIDE)):
        padded[SIDE : SIDE + CELLS, i * FCH : (i + 1) * FCH] = piece.astype(BF16)
    total = dot(padded[0:CELLS, :], kernel[0])
    total += dot(padded[SIDE : SIDE + CELLS, :], kernel[1])
    total += dot(padded[2 * SIDE : 2 * SIDE + CELLS, :], kernel[2])
    return total


def local_moments(h):
    mean = jnp.sum(h, axis=0, keepdims=True) * (1.0 / h.shape[0])
    away = h - mean
    return mean, jnp.sum(away * away, axis=0, keepdims=True)


def merged(pieces, cells_each):
    count = len(pieces)
    k = pieces[0].shape[0] // 2
    total = functools.reduce(jnp.add, pieces)
    mean = total * (1.0 / count)
    drift = functools.reduce(jnp.add, [jnp.square(piece - mean) for piece in pieces])
    spread = (total[k:] + cells_each * drift[:k]) * (1.0 / (count * cells_each))
    return lanes(mean[:k]), lanes(spread)


def activated(h, mean, spread, gain, shift):
    return jnp.maximum((h - mean) * lax.rsqrt(spread + EPSILON) * gain + shift, 0.0)


def fine_first(tick, *refs):
    if tick == 0:
        place, inflow, pending, mixing, kernels, cpending = refs[:6]
        refs = refs[6:]
    else:
        place, arrived, raised_in, entries, raising, pending, mixing, kernels = refs[:8]
        refs = refs[8:]
    h_ref, pay_ref = refs[:2]
    x_ref, padded, skip_ref, mix_ref, held, sems = refs[(3 if tick == 0 else 2) :][:6]
    segment = place[0]
    kernel = Streamed(kernels.at[0], held, sems.at[pl.ds(0, 3)])
    skip = pltpu.make_async_copy(pending.at[tick], skip_ref, sems.at[3])
    mix = pltpu.make_async_copy(mixing, mix_ref, sems.at[4])

    if tick == 0:
        x = pltpu.make_async_copy(inflow, x_ref, sems.at[5])
        x.start()
    else:
        spread_ref, up_ref, up_sems = refs[8:]
        up = Streamed(raising, up_ref, up_sems)

        @pl.when(segment == HALF)
        def _():
            up.start()

        @pl.when(segment == 0)
        def _():
            pltpu.make_async_copy(entries.at[tick - 1], x_ref, sems.at[5]).start()

    @pl.when(segment >= HALF)
    def _():
        mix.start()
        skip.start()

    kernel.start()
    if tick == 0:
        packed, staged, pack_sems = refs[2], refs[9], refs[10]
        loads = [pltpu.make_async_copy(pending.at[slot], staged.at[slot], pack_sems.at[slot]) for slot in range(4)]
        cloads = [
            pltpu.make_async_copy(
                cpending.at[slot, :, pl.ds(side * FCH, FCH)],
                staged.at[0, pl.ds((2 * slot + side) * CCELLS, CCELLS)],
                pack_sems.at[2 * slot + side],
            )
            for slot in range(2)
            for side in range(2)
        ]
        store = pltpu.make_async_copy(staged, packed, pack_sems.at[4])
        cstore = pltpu.make_async_copy(staged.at[0], packed.at[0], pack_sems.at[4])

        @pl.when(segment < HALF)
        def _():
            for copy in loads:
                copy.start()

        @pl.when(segment >= HALF)
        def _():
            for copy in cloads:
                copy.start()

    if tick == 0:
        x.wait()
    else:

        @pl.when(segment == 0)
        def _():
            pltpu.make_async_copy(entries.at[tick - 1], x_ref, sems.at[5]).wait()

        @pl.when((segment != 0) & (segment != HALF))
        def _():
            x_ref[...] = arrived[...]

        @pl.when(segment == HALF)
        def _():
            for part in range(4):
                raised = dot(raised_in[...], up[part])
                for i in range(CSIDE):
                    start = (2 * i + part // 2) * SIDE + part % 2
                    for p in range(FCH // 128):
                        spread_ref[p, pl.ds(start, CSIDE, stride=2), :] = raised[
                            i * CSIDE : (i + 1) * CSIDE, p * 128 : (p + 1) * 128
                        ]
            for p in range(FCH // 128):
                x_ref[:, p * 128 : (p + 1) * 128] = spread_ref[p].astype(BF16)

    @pl.when(segment >= HALF)
    def _():
        skip.wait()
        mix.wait()
        x_ref[...] = (dot(x_ref[...], mix_ref[...]) + skip_ref[...].astype(F32)).astype(BF16)

    if tick == 0:

        @pl.when(segment < HALF)
        def _():
            for copy in loads:
                copy.wait()
            store.start()

        @pl.when(segment >= HALF)
        def _():
            for copy in cloads:
                copy.wait()
            cstore.start()

    h = fine_convolution(x_ref[...].astype(F32), padded, kernel)
    h_ref[...] = h
    mean, spread = local_moments(h)
    pay = jnp.concatenate(rows_of(mean) + rows_of(spread), axis=0)
    pay_ref[...] = jnp.broadcast_to(pay[None], pay_ref.shape)
    if tick == 0:

        @pl.when(segment < HALF)
        def _():
            store.wait()

        @pl.when(segment >= HALF)
        def _():
            cstore.wait()


def coarse_first(tick, *refs):
    place, arrived, pending, mixing, kernels = refs[:5]
    h_ref, mine_ref, other_ref, x_ref, padded, mix_ref, held, sems, skip_ref = refs[5:]
    kernel = Streamed(kernels, held, sems.at[pl.ds(3, 3)])
    if tick < 2:
        skips = [pltpu.make_async_copy(pending.at[tick], skip_ref, sems.at[1])]
    else:
        skips = [
            pltpu.make_async_copy(
                pending.at[1, 0, pl.ds((2 * (tick - 2) + side) * CCELLS, CCELLS)],
                skip_ref.at[:, pl.ds(side * FCH, FCH)],
                sems.at[(1, 6)[side]],
            )
            for side in range(2)
        ]
    segment = place[0]
    mix = pltpu.make_async_copy(mixing, mix_ref, sems.at[0])

    @pl.when(segment < HALF)
    def _():
        mix.start()
        for skip in skips:
            skip.start()

    if tick == 0:
        fetch = pltpu.make_async_copy(arrived, x_ref, sems.at[2])
        fetch.start()
    kernel.start()
    if tick == 0:
        fetch.wait()
    else:
        x_ref[...] = arrived[...]
    @pl.when(segment < HALF)
    def _():
        mix.wait()
        for skip in skips:
            skip.wait()
        x_ref[...] = (dot(x_ref[...], mix_ref[...]) + skip_ref[...].astype(F32)).astype(BF16)

    edge = jnp.zeros((CSIDE, CCH), F32)
    for i, piece in enumerate(with_neighbours(x_ref[...].astype(F32), CSIDE)):
        columns = slice(i * CCH, (i + 1) * CCH)
        padded[0, :, columns] = jnp.concatenate([edge, piece[: CCELLS - CSIDE]], axis=0).astype(BF16)
        padded[1, :, columns] = piece.astype(BF16)
        padded[2, :, columns] = jnp.concatenate([piece[CSIDE:], edge], axis=0).astype(BF16)
    h = dot(padded[0], kernel[0])
    h += dot(padded[1], kernel[1])
    h += dot(padded[2], kernel[2])
    h_ref[...] = h
    mean, spread = local_moments(h)
    mean, spread = rows_of(mean), rows_of(spread)
    first = jnp.concatenate(mean[:2] + spread[:2], axis=0)
    second = jnp.concatenate(mean[2:] + spread[2:], axis=0)
    is_first = place[1] == 0
    mine_ref[...] = jnp.where(is_first, first, second)
    other_ref[...] = jnp.where(is_first, second, first)


def fine_second(gathered, h_ref, gains, shifts, kernels, mine, theirs, out_ref, pay_ref, padded, held, sems):
    kernel = Streamed(kernels.at[1], held, sems).start()
    mean, spread = merged([gathered[i] for i in range(N_DP)], float(CELLS))
    x = activated(h_ref[...], mean, spread, gains[0:1], shifts[0:1]).astype(BF16)
    h = fine_convolution(x.astype(F32), padded, kernel)
    out_ref[...] = h
    mean, spread = local_moments(h)
    a, b = mine[...], theirs[...]
    pair_mean = (a[:2] + b[:2]) * 0.5
    pair_spread = a[2:] + b[2:] + jnp.square(a[:2] - b[:2]) * (0.5 * CCELLS)
    pay = jnp.concatenate(rows_of(mean) + rows_of(spread) + [pair_mean, pair_spread], axis=0)
    pay_ref[...] = jnp.broadcast_to(pay[None], pay_ref.shape)


def finish(tick, place, gathered, h_ref, hc_ref, gains, shifts, cgains, cshifts, *refs):
    if tick == TICKS - 1:
        fine_ref, coarse_ref = refs
    else:
        descent, fine_ref, coarse_ref, going, fine32, packed, down_ref, sem = refs
        fetch = pltpu.make_async_copy(descent, down_ref, sem)

        @pl.when(place[0] == HALF - 1)
        def _():
            fetch.start()

    mean, spread = merged([gathered[i, 0:4] for i in range(N_DP)], float(CELLS))
    fine = activated(h_ref[...], mean, spread, gains[1:2], shifts[1:2]).astype(BF16)
    mean0, spread0 = merged([gathered[i, 4:8] for i in range(0, N_DP, 2)], 2.0 * CCELLS)
    mean1, spread1 = merged([gathered[i, 4:8] for i in range(1, N_DP, 2)], 2.0 * CCELLS)
    mean = jnp.concatenate([mean0, mean1], axis=1)
    spread = jnp.concatenate([spread0, spread1], axis=1)
    coarse = activated(hc_ref[...], mean, spread, cgains[...], cshifts[...]).astype(BF16)
    fine_ref[...] = fine
    coarse_ref[...] = coarse
    if tick < TICKS - 1:
        segment = place[0]

        @pl.when(segment != HALF - 1)
        def _():
            going[...] = coarse

        @pl.when(segment == HALF - 1)
        def _():
            for p in range(FCH // 128):
                fine32[...] = fine[:, p * 128 : (p + 1) * 128].astype(F32)
                for a in range(2):
                    for c in range(2):
                        taken = [
                            fine32[pl.ds((2 * i + a) * SIDE + c, CSIDE, stride=2), :] for i in range(CSIDE)
                        ]
                        column = (2 * a + c) * FCH + p * 128
                        packed[:, column : column + 128] = jnp.concatenate(taken, axis=0).astype(BF16)
            fetch.wait()
            going[...] = dot(packed[...], down_ref[...]).astype(BF16)


def keep(tick, *refs):
    place, fine, coarse, mixing, cmixing = refs[:5]
    refs = refs[5:]
    if tick != 1:
        extra, refs = refs[0], refs[1:]
    fstash, cstash, fback, ctarget, term, cterm, mix_ref, cmix_ref, staged, sems = refs[(0, 4, 3, 4)[tick] :]
    segment = place[0]
    copies = [
        pltpu.make_async_copy(fine, fstash.at[tick], sems.at[0]),
        pltpu.make_async_copy(coarse, cstash.at[tick], sems.at[1]),
    ]
    for copy in copies:
        copy.start()
    if tick == 0:
        load = pltpu.make_async_copy(extra.at[4:6], staged.at[0:2], sems.at[2])
        load.start()

    @pl.when(segment < HALF)
    def _():
        fetch = pltpu.make_async_copy(mixing, mix_ref, sems.at[3])
        fetch.start()
        if tick == 3:
            ccopy = pltpu.make_async_copy(extra, ctarget, sems.at[5])
            ccopy.start()
        fetch.wait()
        term[...] = dot(fine[...], mix_ref[...]).astype(BF16)
        copy = pltpu.make_async_copy(term, fback.at[2 + tick], sems.at[4])
        copy.start()
        if tick == 3:
            ccopy.wait()
        copy.wait()

    @pl.when(segment >= HALF)
    def _():
        fetch = pltpu.make_async_copy(cmixing, cmix_ref, sems.at[3])
        fetch.start()
        if tick == 2:
            received = pltpu.make_async_copy(extra.at[0], staged, sems.at[4])
            received.start()
        fetch.wait()
        cterm[...] = dot(coarse[...], cmix_ref[...]).astype(BF16)
        copy = pltpu.make_async_copy(cterm, ctarget.at[tick % 2], sems.at[5])
        copy.start()
        if tick == 2:
            received.wait()
            stored = pltpu.make_async_copy(staged, fback.at[2:6], sems.at[4])
            stored.start()
            stored.wait()
        copy.wait()

    if tick == 0:
        load.wait()
        store = pltpu.make_async_copy(staged.at[0:2], fback.at[0:2], sems.at[2])
        store.start()
        store.wait()
    for copy in copies:
        copy.wait()


def kept_after(tick, common, added, kept):
    stashes = [
        (pltpu.HBM, (TICKS, CELLS, FCH)),
        (pltpu.HBM, (TICKS, CCELLS, CCH)),
        (pltpu.HBM, (6, CELLS, FCH)),
        (pltpu.HBM, (2, CCELLS, CCH)),
    ]
    earlier = () if tick == 0 else tuple(kept[:3]) if tick == 2 else tuple(kept)
    start = len(common) + len(added)
    return call(
        functools.partial(keep, tick),
        stashes,
        [SM, VM, VM, ANY, ANY] + [VM if tick == 3 else ANY] * len(added) + [ANY] * len(earlier),
        (
            pltpu.VMEM((CELLS, FCH), BF16),
            pltpu.VMEM((CCELLS, CCH), BF16),
            pltpu.VMEM((FCH, FCH), BF16),
            pltpu.VMEM((CCH, CCH), BF16),
            pltpu.VMEM((4, CELLS, FCH), BF16),
            pltpu.SemaphoreType.DMA((6,)),
        ),
        40_000_000,
        1_000_000,
        {start + i: i for i in range(len(earlier))},
    )(*common, *added, *earlier)


def tied(*values):
    return lax.optimization_barrier(values)


def on_device(
    fine_inflow,
    coarse_inflow,
    fine_entries,
    fine_pending,
    coarse_pending,
    fine_kernels,
    fine_mixing,
    fine_gains,
    fine_shifts,
    coarse_kernel,
    coarse_mixing,
    coarse_gains,
    coarse_shifts,
    descent_kernel,
    upsample_kernel,
):
    place = jnp.stack([lax.axis_index("segment"), lax.axis_index("dp") % 2]).astype(jnp.int32)
    inflow = fine_inflow.reshape(CELLS, FCH)
    cinflow = coarse_inflow.reshape(CCELLS, CCH)
    entries = fine_entries.reshape(TICKS - 1, CELLS, FCH)
    pending = fine_pending.reshape(6, CELLS, FCH)
    cpending = coarse_pending.reshape(2, CCELLS, CCH)
    kernels = fine_kernels.reshape(2, 3, 3 * FCH, FCH)
    ckernel = coarse_kernel.reshape(3, 3 * CCH, CCH)
    mixing = fine_mixing.reshape(FCH, FCH)
    cmixing = coarse_mixing.reshape(CCH, CCH)
    gains, shifts = fine_gains.reshape(2, FCH), fine_shifts.reshape(2, FCH)
    cgains, cshifts = coarse_gains.reshape(1, CCH), coarse_shifts.reshape(1, CCH)
    descent = descent_kernel.reshape(4 * FCH, CCH)
    upsampling = upsample_kernel.transpose(1, 2, 0, 3).reshape(4, CCH, FCH)

    fine_route = [(0, 1), (1, 2), (2, 3), (4, 5), (5, 6), (6, 7)]
    up_route = [(HALF - 1, HALF)]
    coarse_route = [(p, (p + 1) % (2 * HALF)) for p in range(2 * HALF)]
    pairs = [[p, p + HALF] for p in range(HALF)]
    cores = [(i, i ^ 1) for i in range(N_DP)]

    ftile, ctile = (CELLS, FCH), (CCELLS, CCH)
    fine_bf, coarse_bf = pltpu.VMEM(ftile, BF16), pltpu.VMEM(ctile, BF16)
    padded = pltpu.VMEM((CELLS + 2 * SIDE, 3 * FCH), BF16)
    held = pltpu.VMEM((3, 3 * FCH, FCH), BF16)
    conv_flops = 2 * CELLS * 9 * FCH * FCH
    vmem, hbm = pltpu.VMEM, pltpu.HBM

    arrived = raised = carrived = kept = None
    for tick in range(TICKS):
        sending = tick < TICKS - 1
        if tick == 0:
            sources, specs = (inflow, pending, mixing, kernels, cpending), [SM, ANY, ANY, ANY, ANY, ANY]
            more = (pltpu.VMEM((4, CELLS, FCH), BF16), pltpu.SemaphoreType.DMA((5,)))
        else:
            sources = (arrived, raised, entries, upsampling, pending, mixing, kernels)
            specs = [SM, VM, VM, ANY, ANY, ANY, ANY, ANY]
            more = (
                pltpu.VMEM((2, CELLS, 128), F32),
                pltpu.VMEM((4, CCH, FCH), BF16),
                pltpu.SemaphoreType.DMA((4,)),
            )
        h1, pay, *packed = call(
            functools.partial(fine_first, tick),
            [(vmem, ftile, F32), (vmem, (N_DP, 4, 128), F32)] + [(hbm, (4, CELLS, FCH))] * (tick == 0),
            specs,
            (fine_bf, padded, fine_bf, pltpu.VMEM((FCH, FCH), BF16), held, pltpu.SemaphoreType.DMA((6,)), *more),
            conv_flops,
            1_000_000,
        )(place, *sources)

        if tick == 0:
            carrived = cinflow
            pay, later = tied(pay, place)
            skips = lax.all_gather(packed[0], "segment", axis_index_groups=pairs)
        else:
            pay, carrived = tied(pay, carrived)
            later = place
        gathered = lax.all_to_all(pay, "dp", 0, 0, tiled=True)
        hc, mine, other = call(
            functools.partial(coarse_first, tick),
            [(vmem, ctile, F32), (vmem, (4, 128), F32), (vmem, (4, 128), F32)],
            [SM, VM if tick else ANY, ANY, ANY, ANY],
            (
                coarse_bf,
                pltpu.VMEM((3, CCELLS, 3 * CCH), BF16),
                pltpu.VMEM((CCH, CCH), BF16),
                pltpu.VMEM((3, 3 * CCH, CCH), BF16),
                pltpu.SemaphoreType.DMA((7,)),
                coarse_bf,
            ),
            2 * CCELLS * 9 * CCH * CCH,
            1_500_000,
        )(later, carrived, cpending if tick < 2 else skips, cmixing, ckernel)
        theirs = lax.ppermute(other, "dp", cores)
        h2, pay2 = call(
            fine_second,
            [(vmem, ftile, F32), (vmem, (N_DP, 8, 128), F32)],
            [VM, VM, VM, VM, ANY, VM, VM],
            (padded, held, pltpu.SemaphoreType.DMA((3,))),
            conv_flops,
            1_000_000,
        )(gathered, h1, gains, shifts, kernels, mine, theirs)
        if tick > 0:
            pay2, own, cown = tied(pay2, own, cown)
        gathered2 = lax.all_to_all(pay2, "dp", 0, 0, tiled=True)
        if tick == 0:
            gathered2, upsampling = tied(gathered2, upsampling)
        else:
            added = ((pending,), (), (skips,))[tick - 1]
            kept = kept_after(tick - 1, (place, own, cown, mixing, cmixing), added, kept)
            gathered2, *kept = tied(gathered2, *kept)
            if tick == 2:
                fresh = lax.ppermute(kept[3], "segment", [(p + HALF, p) for p in range(HALF)])
        own, cown, *going = call(
            functools.partial(finish, tick),
            [(vmem, ftile), (vmem, ctile)] + ([(vmem, ctile)] if sending else []),
            [SM] + [VM] * 7 + [ANY] * sending,
            (
                pltpu.VMEM((CELLS, 128), F32),
                pltpu.VMEM((CCELLS, 4 * FCH), BF16),
                pltpu.VMEM((4 * FCH, CCH), BF16),
                pltpu.SemaphoreType.DMA,
            ) if sending else (),
            100_000_000,
            1_000_000,
        )(place, gathered2, h2, hc, gains, shifts, cgains, cshifts, *((descent,) if sending else ()))
        if sending:
            raised = lax.ppermute(cown, "segment", up_route)
            arrived = lax.ppermute(own, "segment", fine_route)
            carrived = lax.ppermute(going[0], "segment", coarse_route)
    fstash, cstash, fback, cback = kept_after(
        TICKS - 1, (place, own, cown, mixing, cmixing), (fresh,), kept
    )
    return (
        fstash.reshape(1, TICKS, 1, SIDE, SIDE, FCH),
        cstash.reshape(1, TICKS, 1, CSIDE, CSIDE, CCH),
        fback.reshape(1, 6, 1, SIDE, SIDE, FCH),
        cback.reshape(1, 2, 1, CSIDE, CSIDE, CCH),
    )


def solution(mesh):
    placed = (
        P("segment", "dp", None, None, None),
        P("segment", "dp", None, None, None),
        P(None, "dp", None, None, None),
        P("segment", None, "dp", None, None, None),
        P("segment", None, "dp", None, None, None),
        P("segment", None, None, None, None, None),
        P("segment", None, None),
        P("segment", None, None),
        P("segment", None, None),
        P("segment", None, None, None, None),
        P("segment", None, None),
        P("segment", None),
        P("segment", None),
        P(),
        P(),
    )
    return jax.shard_map(
        on_device,
        mesh=mesh,
        in_specs=placed,
        out_specs=(P("segment", None, "dp", None, None, None),) * 4,
        check_vma=False,
    )
```

time: 236 us -> 213 us (0.903); the launches traced: 231 us -> 212 us
  Pallas kernels: 0 us -> 52.2 us
  matrix products: 44.1 us -> 0 us
  other arithmetic: 22.4 us -> 0.08 us
  local copies, waits for them, and re-layouts: 23.3 us -> 1.14 us
  waiting for transfers between devices: 62.6 us -> 78.2 us
  between operations: 1.98 us -> 14.4 us
  starting transfers between devices: 76.8 us -> 66.2 us
    pallas_call x0 -> x20, Pallas kernels: none -> 52.2 us  [call(): kernel(*[placed(spec, arg) for spec, arg in zip(in_specs, args, strict=Tr...]
    conv_general_dilated x12 -> x0, matrix products: 39.2 us -> none  [convolve(): lax.conv_general_dilated(images, kernel, (1, 1), 'SAME', dimension_number...]
    ppermute x11 -> x14, waiting for transfers between devices: 20.2 us -> 44.5 us  [the longest x1 22 us: on_device(): lax.ppermute(kept[3], 'segment', [(p + HALF, p) for p in range(HALF)])]
    all_to_all x8, waiting for transfers between devices: 42.4 us -> 33 us  [the longest x4 18.5 us: on_device(): gathered2 = lax.all_to_all(pay2, 'dp', 0, 0, tiled=True)]
    broadcast_in_dim x12 -> x0, local copies, waits for them, and re-layouts: 7.05 us -> none  [the longest x8 5.78 us: copy_for_each(): jnp.broadcast_to(x[None], (size, *x.shape))]
    convert_element_type x12 -> x0, other arithmetic: 6.54 us -> none  [normalize(): results.append(jnp.maximum(scaled, 0.0).astype(jnp.bfloat16))]
    another operation x10 -> x0, local copies, waits for them, and re-layouts: 6.1 us -> none
    unnamed x4 -> x0, other arithmetic: 5.53 us -> none
  transfers between devices with their start and end apart: 19 -> 23, of which waited for: 10 -> 18; matrix products, arithmetic and copies ran while one was open for 27% -> 1% of each run, Pallas kernels for 0% -> 18%
where the time goes in v1:
time: 213 us; the launch traced here: 212 us
  waiting for transfers between devices  78.2 us (37%)
  starting transfers between devices  66.2 us (31%)
  Pallas kernels  52.2 us (25%)
  between operations  14.4 us (7%)
    pallas_call x20, Pallas kernels, call(): kernel(*[placed(spec, arg) for spec, arg in zip(in_specs, args, strict=Tr...  52.2 us
    all_to_all x4, starting transfers between devices, on_device(): gathered2 = lax.all_to_all(pay2, 'dp', 0, 0, tiled=True)  22.9 us
    ppermute x1, waiting for transfers between devices, on_device(): lax.ppermute(kept[3], 'segment', [(p + HALF, p) for p in range(HALF)])  22 us
    all_to_all x4, starting transfers between devices, on_device(): gathered = lax.all_to_all(pay, 'dp', 0, 0, tiled=True)  21.2 us
    all_to_all x4, waiting for transfers between devices, on_device(): gathered2 = lax.all_to_all(pay2, 'dp', 0, 0, tiled=True)  18.5 us
    ppermute x3, waiting for transfers between devices, on_device(): carrived = lax.ppermute(going[0], 'segment', coarse_route)  15 us
    all_to_all x4, waiting for transfers between devices, on_device(): gathered = lax.all_to_all(pay, 'dp', 0, 0, tiled=True)  14.6 us
    ppermute x3, starting transfers between devices, on_device(): arrived = lax.ppermute(own, 'segment', fine_route)  10.5 us
  transfers between devices with their start and end apart: 23, of which 18 were waited for; matrix products, arithmetic and copies ran while one was open for 1% of the time, Pallas kernels for 18%

profile of v1, /device:TPU:32, one launch (start us, length us, event | category | flops | bytes accessed | tf_op | source)
XLA Modules:
  0.0 212.3 jit_solution(6779307047627547850)
XLA Ops:
  7.3 3.6 %shard_map.174 = (f32[256,256]{1,0:T(8,128)S(1)}, f32[32,4,128]{2,1,0:T(4,128)}, bf16[4,256,256]{2,1,0:T(8,128)(2,1)}) custom-call(s32[2]{0:T(128)S(1)} %pad_add_fusion.refs_0_.place, bf16[256,256]{1,0:T(8,128)(2,1)} %bitcast.98, bf16[6,256,256]{2,1,0:T(8,128)(2,1)} %bitcast.65, bf16[256,256]{1,0:T(8,128)(2,1)} %bitcast.79, ...), custom_call_target="tpu_custom_call" | custom-call | flops 301989888 | bytes 1000000 | tf_op jit(solution)/shard_map/pallas_call | solution.py:40
  10.9 8.9 %all-to-all-start = ((f32[32,4,128]{2,1,0:T(4,128)}), f32[32,4,128]{2,1,0:T(4,128)S(1)}, u32[]{:S(2)}, u32[]{:S(2)}) async-start(f32[32,4,128]{2,1,0:T(4,128)} %get-tuple-element.95), calls=%async_computation | async-start | bytes 131072 | tf_op jit(solution)/shard_map/all_to_all | solution.py:517
  19.8 3.7 %shard_map.175 = (f32[64,512]{1,0:T(8,128)S(1)}, f32[4,128]{1,0:T(4,128)S(1)}, f32[4,128]{1,0:T(4,128)S(1)}) custom-call(s32[2]{0:T(128)S(1)} %pad_add_fusion.refs_0_.place, bf16[64,512]{1,0:T(8,128)(2,1)} %bitcast.99, bf16[2,64,512]{2,1,0:T(8,128)(2,1)} %bitcast.94, bf16[512,512]{1,0:T(8,128)(2,1)} %bitcast.57, bf16[3,1536,512]{2,1,0:T(8,128)(2,1)} %bitcast.53), custom_call_target="tpu_custom_call" | custom-call | flops 301989888 | bytes 1500000 | tf_op jit(solution)/shard_map/pallas_call | solution.py:40
  29.2 6.0 %all-to-all-start.1 = ((f32[32,8,128]{2,1,0:T(8,128)}), f32[32,8,128]{2,1,0:T(8,128)S(1)}, u32[]{:S(2)}, u32[]{:S(2)}) async-start(f32[32,8,128]{2,1,0:T(8,128)} %get-tuple-element.100), calls=%async_computation.1 | async-start | bytes 262144 | tf_op jit(solution)/shard_map/all_to_all | solution.py:544
  37.1 5.5 %all-to-all-done.1.gathered = f32[32,8,128]{2,1,0:T(8,128)S(1)} async-done(((f32[32,8,128]{2,1,0:T(8,128)}), f32[32,8,128]{2,1,0:T(8,128)S(1)}, u32[]{:S(2)}, u32[]{:S(2)}) %all-to-all-start.1) | async-done | bytes 131104 | tf_op jit(solution)/shard_map/all_to_all | solution.py:544
  53.9 6.2 %collective-permute-done.3.refs_1_ = bf16[64,512]{1,0:T(8,128)(2,1)S(1)} collective-permute-done((bf16[64,512]{1,0:T(8,128)(2,1)S(1)}, bf16[64,512]{1,0:T(8,128)(2,1)S(1)}, u32[]{:S(2)}, u32[]{:S(2)}) %collective-permute-start.3) | collective-permute-done | bytes 65568 | tf_op jit(solution)/shard_map/ppermute | solution.py:569
  60.2 3.6 %all-to-all-start.2 = ((f32[32,4,128]{2,1,0:T(4,128)}), f32[32,4,128]{2,1,0:T(4,128)S(1)}, u32[]{:S(2)}, u32[]{:S(2)}) async-start(f32[32,4,128]{2,1,0:T(4,128)} %get-tuple-element.109), calls=%async_computation.2 | async-start | bytes 131072 | tf_op jit(solution)/shard_map/all_to_all | solution.py:517
  63.8 3.7 %shard_map.179 = (f32[64,512]{1,0:T(8,128)S(1)}, f32[4,128]{1,0:T(4,128)S(1)}, f32[4,128]{1,0:T(4,128)S(1)}) custom-call(s32[2]{0:T(128)S(1)} %pad_add_fusion.refs_0_.place, bf16[64,512]{1,0:T(8,128)(2,1)S(1)} %collective-permute-done.3.refs_1_, bf16[2,64,512]{2,1,0:T(8,128)(2,1)} %bitcast.95, bf16[512,512]{1,0:T(8,128)(2,1)} %bitcast.58, ...), custom_call_target="tpu_custom_call" | custom-call | flops 301989888 | bytes 1500000 | tf_op jit(solution)/shard_map/pallas_call | solution.py:40
  68.7 9.3 %all-to-all-done.2.gathered = f32[32,4,128]{2,1,0:T(4,128)S(1)} async-done(((f32[32,4,128]{2,1,0:T(4,128)}), f32[32,4,128]{2,1,0:T(4,128)S(1)}, u32[]{:S(2)}, u32[]{:S(2)}) %all-to-all-start.2) | async-done | bytes 65568 | tf_op jit(solution)/shard_map/all_to_all | solution.py:517
  80.7 4.9 %all-to-all-start.3 = ((f32[32,8,128]{2,1,0:T(8,128)}), f32[32,8,128]{2,1,0:T(8,128)S(1)}, u32[]{:S(2)}, u32[]{:S(2)}) async-start(f32[32,8,128]{2,1,0:T(8,128)} %get-tuple-element.115), calls=%async_computation.3 | async-start | bytes 262144 | tf_op jit(solution)/shard_map/all_to_all | solution.py:544
  88.8 4.3 %all-to-all-done.3.gathered = f32[32,8,128]{2,1,0:T(8,128)S(1)} async-done(((f32[32,8,128]{2,1,0:T(8,128)}), f32[32,8,128]{2,1,0:T(8,128)S(1)}, u32[]{:S(2)}, u32[]{:S(2)}) %all-to-all-start.3) | async-done | bytes 131104 | tf_op jit(solution)/shard_map/all_to_all | solution.py:544
  93.8 3.9 %collective-permute-start.5 = (bf16[256,256]{1,0:T(8,128)(2,1)S(1)}, bf16[256,256]{1,0:T(8,128)(2,1)S(1)}, u32[]{:S(2)}, u32[]{:S(2)}) collective-permute-start(bf16[256,256]{1,0:T(8,128)(2,1)S(1)} %get-tuple-element.137.refs_1_), channel_id=1, source_target_pairs={{0,32},{32,64},{64,96},{128,160},{160,192},{192,224},{1,33},{33,65... | collective-permute-start | bytes 393224 | tf_op jit(solution)/shard_map/ppermute | solution.py:568
  104.9 5.1 %collective-permute-done.7.refs_1_ = bf16[64,512]{1,0:T(8,128)(2,1)S(1)} collective-permute-done((bf16[64,512]{1,0:T(8,128)(2,1)S(1)}, bf16[64,512]{1,0:T(8,128)(2,1)S(1)}, u32[]{:S(2)}, u32[]{:S(2)}) %collective-permute-start.7) | collective-permute-done | bytes 65568 | tf_op jit(solution)/shard_map/ppermute | solution.py:569
  110.1 4.3 %all-to-all-start.4 = ((f32[32,4,128]{2,1,0:T(4,128)}), f32[32,4,128]{2,1,0:T(4,128)S(1)}, u32[]{:S(2)}, u32[]{:S(2)}) async-start(f32[32,4,128]{2,1,0:T(4,128)} %get-tuple-element.129), calls=%async_computation.4 | async-start | bytes 131072 | tf_op jit(solution)/shard_map/all_to_all | solution.py:517
  114.4 3.7 %shard_map.184 = (f32[64,512]{1,0:T(8,128)S(1)}, f32[4,128]{1,0:T(4,128)S(1)}, f32[4,128]{1,0:T(4,128)S(1)}) custom-call(s32[2]{0:T(128)S(1)} %pad_add_fusion.refs_0_.place, bf16[64,512]{1,0:T(8,128)(2,1)S(1)} %collective-permute-done.7.refs_1_, bf16[2,4,256,256]{3,2,1,0:T(8,128)(2,1)} %bitcast.73, bf16[512,512]{1,0:T(8,128)(2,1)} %bitcast.60, ...), custom_call_target="tpu_custom_call" | custom-call | flops 301989888 | bytes 1500000 | tf_op jit(solution)/shard_map/pallas_call | solution.py:40
  123.8 6.0 %all-to-all-start.5 = ((f32[32,8,128]{2,1,0:T(8,128)}), f32[32,8,128]{2,1,0:T(8,128)S(1)}, u32[]{:S(2)}, u32[]{:S(2)}) async-start(f32[32,8,128]{2,1,0:T(8,128)} %get-tuple-element.136), calls=%async_computation.5 | async-start | bytes 262144 | tf_op jit(solution)/shard_map/all_to_all | solution.py:544
  132.2 5.0 %all-to-all-done.5.gathered = f32[32,8,128]{2,1,0:T(8,128)S(1)} async-done(((f32[32,8,128]{2,1,0:T(8,128)}), f32[32,8,128]{2,1,0:T(8,128)S(1)}, u32[]{:S(2)}, u32[]{:S(2)}) %all-to-all-start.5) | async-done | bytes 131104 | tf_op jit(solution)/shard_map/all_to_all | solution.py:544
  141.7 4.5 %collective-permute-start.11 = (bf16[64,512]{1,0:T(8,128)(2,1)S(1)}, bf16[64,512]{1,0:T(8,128)(2,1)S(1)}, u32[]{:S(2)}, u32[]{:S(2)}) collective-permute-start(bf16[64,512]{1,0:T(8,128)(2,1)S(1)} %get-tuple-element.153), channel_id=1, source_target_pairs={{0,32},{32,64},{64,96},{96,128},{128,160},{160,192},{192,224},{224... | collective-permute-start | bytes 196616 | tf_op jit(solution)/shard_map/ppermute | solution.py:569
  149.6 3.7 %collective-permute-done.11.refs_1_ = bf16[64,512]{1,0:T(8,128)(2,1)S(1)} collective-permute-done((bf16[64,512]{1,0:T(8,128)(2,1)S(1)}, bf16[64,512]{1,0:T(8,128)(2,1)S(1)}, u32[]{:S(2)}, u32[]{:S(2)}) %collective-permute-start.11) | collective-permute-done | bytes 65568 | tf_op jit(solution)/shard_map/ppermute | solution.py:569
  153.2 4.3 %all-to-all-start.6 = ((f32[32,4,128]{2,1,0:T(4,128)}), f32[32,4,128]{2,1,0:T(4,128)S(1)}, u32[]{:S(2)}, u32[]{:S(2)}) async-start(f32[32,4,128]{2,1,0:T(4,128)} %get-tuple-element.154), calls=%async_computation.6 | async-start | bytes 131072 | tf_op jit(solution)/shard_map/all_to_all | solution.py:517
  157.5 3.7 %shard_map.189 = (f32[64,512]{1,0:T(8,128)S(1)}, f32[4,128]{1,0:T(4,128)S(1)}, f32[4,128]{1,0:T(4,128)S(1)}) custom-call(s32[2]{0:T(128)S(1)} %pad_add_fusion.refs_0_.place, bf16[64,512]{1,0:T(8,128)(2,1)S(1)} %collective-permute-done.11.refs_1_, bf16[2,4,256,256]{3,2,1,0:T(8,128)(2,1)} %bitcast.74, bf16[512,512]{1,0:T(8,128)(2,1)} %bitcast.62, ...), custom_call_target="tpu_custom_call" | custom-call | flops 301989888 | bytes 1500000 | tf_op jit(solution)/shard_map/pallas_call | solution.py:40
  166.9 6.0 %all-to-all-start.7 = ((f32[32,8,128]{2,1,0:T(8,128)}), f32[32,8,128]{2,1,0:T(8,128)S(1)}, u32[]{:S(2)}, u32[]{:S(2)}) async-start(f32[32,8,128]{2,1,0:T(8,128)} %get-tuple-element.160), calls=%async_computation.7 | async-start | bytes 262144 | tf_op jit(solution)/shard_map/all_to_all | solution.py:544
  176.6 3.7 %all-to-all-done.7.gathered = f32[32,8,128]{2,1,0:T(8,128)S(1)} async-done(((f32[32,8,128]{2,1,0:T(8,128)}), f32[32,8,128]{2,1,0:T(8,128)S(1)}, u32[]{:S(2)}, u32[]{:S(2)}) %all-to-all-start.7) | async-done | bytes 131104 | tf_op jit(solution)/shard_map/all_to_all | solution.py:544
  181.0 22.0 %collective-permute-done.13.refs_5_ = bf16[2,64,512]{2,1,0:T(8,128)(2,1)S(1)} collective-permute-done((bf16[2,64,512]{2,1,0:T(8,128)(2,1)S(1)}, bf16[2,64,512]{2,1,0:T(8,128)(2,1)S(1)}, u32[]{:S(2)}, u32[]{:S(2)}) %collective-permute-start.13) | collective-permute-done | bytes 131104 | tf_op jit(solution)/shard_map/ppermute | solution.py:552
  (57 shorter events, 62.3 us)
Async XLA Ops:
  10.8 25.1 %copy-start.4 = (bf16[512,2,2,256]{3,2,1,0:T(2,128)(2,1)S(1)}, bf16[512,2,2,256]{3,2,1,0:T(2,128)(2,1)}, u32[]{:S(2)}) copy-start(bf16[512,2,2,256]{3,2,1,0:T(2,128)(2,1)} %param.29) | copy-start | bytes 3145732
  10.9 15.7 %all-to-all-start = ((f32[32,4,128]{2,1,0:T(4,128)}), f32[32,4,128]{2,1,0:T(4,128)S(1)}, u32[]{:S(2)}, u32[]{:S(2)}) async-start(f32[32,4,128]{2,1,0:T(4,128)} %get-tuple-element.95), calls=%async_computation | async-start | bytes 131072 | tf_op jit(solution)/shard_map/all_to_all | solution.py:517
  23.5 1.2 collective-permute-start
  29.2 13.4 %all-to-all-start.1 = ((f32[32,8,128]{2,1,0:T(8,128)}), f32[32,8,128]{2,1,0:T(8,128)S(1)}, u32[]{:S(2)}, u32[]{:S(2)}) async-start(f32[32,8,128]{2,1,0:T(8,128)} %get-tuple-element.100), calls=%async_computation.1 | async-start | bytes 262144 | tf_op jit(solution)/shard_map/all_to_all | solution.py:544
  35.2 79.2 %all-gather.3.cloned.1.call-start = ((), (), s32[]{:S(2)}) async-start(), calls=%async_computation.8 | async-start | bytes 1572864 | tf_op jit(solution)/shard_map/all_gather | solution.py:513
  43.3 7.2 %collective-permute-start.1 = (bf16[256,256]{1,0:T(8,128)(2,1)S(1)}, bf16[256,256]{1,0:T(8,128)(2,1)S(1)}, u32[]{:S(2)}, u32[]{:S(2)}) collective-permute-start(bf16[256,256]{1,0:T(8,128)(2,1)S(1)} %get-tuple-element.116.refs_1_), channel_id=1, source_target_pairs={{0,32},{32,64},{64,96},{128,160},{160,192},{192,224},{1,33},{33,65... | collective-permute-start | bytes 393224 | tf_op jit(solution)/shard_map/ppermute | solution.py:568
  46.7 2.2 %collective-permute-start.2 = (bf16[64,512]{1,0:T(8,128)(2,1)S(1)}, bf16[64,512]{1,0:T(8,128)(2,1)S(1)}, u32[]{:S(2)}, u32[]{:S(2)}) collective-permute-start(bf16[64,512]{1,0:T(8,128)(2,1)S(1)} %get-tuple-element.117.refs_2_), channel_id=1, source_target_pairs={{96,128},{97,129},{98,130},{99,131},{100,132},{101,133},{102,134},... | collective-permute-start | bytes 196616 | tf_op jit(solution)/shard_map/ppermute | solution.py:567
  47.4 12.8 %collective-permute-start.3 = (bf16[64,512]{1,0:T(8,128)(2,1)S(1)}, bf16[64,512]{1,0:T(8,128)(2,1)S(1)}, u32[]{:S(2)}, u32[]{:S(2)}) collective-permute-start(bf16[64,512]{1,0:T(8,128)(2,1)S(1)} %get-tuple-element.108), channel_id=1, source_target_pairs={{0,32},{32,64},{64,96},{96,128},{128,160},{160,192},{192,224},{224... | collective-permute-start | bytes 196616 | tf_op jit(solution)/shard_map/ppermute | solution.py:569
  60.2 17.8 %all-to-all-start.2 = ((f32[32,4,128]{2,1,0:T(4,128)}), f32[32,4,128]{2,1,0:T(4,128)S(1)}, u32[]{:S(2)}, u32[]{:S(2)}) async-start(f32[32,4,128]{2,1,0:T(4,128)} %get-tuple-element.109), calls=%async_computation.2 | async-start | bytes 131072 | tf_op jit(solution)/shard_map/all_to_all | solution.py:517
  67.5 1.2 collective-permute-start.4
  80.7 12.4 %all-to-all-start.3 = ((f32[32,8,128]{2,1,0:T(8,128)}), f32[32,8,128]{2,1,0:T(8,128)S(1)}, u32[]{:S(2)}, u32[]{:S(2)}) async-start(f32[32,8,128]{2,1,0:T(8,128)} %get-tuple-element.115), calls=%async_computation.3 | async-start | bytes 262144 | tf_op jit(solution)/shard_map/all_to_all | solution.py:544
  93.8 7.8 %collective-permute-start.5 = (bf16[256,256]{1,0:T(8,128)(2,1)S(1)}, bf16[256,256]{1,0:T(8,128)(2,1)S(1)}, u32[]{:S(2)}, u32[]{:S(2)}) collective-permute-start(bf16[256,256]{1,0:T(8,128)(2,1)S(1)} %get-tuple-element.137.refs_1_), channel_id=1, source_target_pairs={{0,32},{32,64},{64,96},{128,160},{160,192},{192,224},{1,33},{33,65... | collective-permute-start | bytes 393224 | tf_op jit(solution)/shard_map/ppermute | solution.py:568
  97.8 2.1 %collective-permute-start.6 = (bf16[64,512]{1,0:T(8,128)(2,1)S(1)}, bf16[64,512]{1,0:T(8,128)(2,1)S(1)}, u32[]{:S(2)}, u32[]{:S(2)}) collective-permute-start(bf16[64,512]{1,0:T(8,128)(2,1)S(1)} %get-tuple-element.138.refs_2_), channel_id=1, source_target_pairs={{96,128},{97,129},{98,130},{99,131},{100,132},{101,133},{102,134},... | collective-permute-start | bytes 196616 | tf_op jit(solution)/shard_map/ppermute | solution.py:567
  98.4 11.6 %collective-permute-start.7 = (bf16[64,512]{1,0:T(8,128)(2,1)S(1)}, bf16[64,512]{1,0:T(8,128)(2,1)S(1)}, u32[]{:S(2)}, u32[]{:S(2)}) collective-permute-start(bf16[64,512]{1,0:T(8,128)(2,1)S(1)} %get-tuple-element.128), channel_id=1, source_target_pairs={{0,32},{32,64},{64,96},{96,128},{128,160},{160,192},{192,224},{224... | collective-permute-start | bytes 196616 | tf_op jit(solution)/shard_map/ppermute | solution.py:569
  110.1 11.1 %all-to-all-start.4 = ((f32[32,4,128]{2,1,0:T(4,128)}), f32[32,4,128]{2,1,0:T(4,128)S(1)}, u32[]{:S(2)}, u32[]{:S(2)}) async-start(f32[32,4,128]{2,1,0:T(4,128)} %get-tuple-element.129), calls=%async_computation.4 | async-start | bytes 131072 | tf_op jit(solution)/shard_map/all_to_all | solution.py:517
  118.1 1.2 collective-permute-start.8
  123.8 13.4 %all-to-all-start.5 = ((f32[32,8,128]{2,1,0:T(8,128)}), f32[32,8,128]{2,1,0:T(8,128)S(1)}, u32[]{:S(2)}, u32[]{:S(2)}) async-start(f32[32,8,128]{2,1,0:T(8,128)} %get-tuple-element.136), calls=%async_computation.5 | async-start | bytes 262144 | tf_op jit(solution)/shard_map/all_to_all | solution.py:544
  137.9 8.3 %collective-permute-start.9 = (bf16[256,256]{1,0:T(8,128)(2,1)S(1)}, bf16[256,256]{1,0:T(8,128)(2,1)S(1)}, u32[]{:S(2)}, u32[]{:S(2)}) collective-permute-start(bf16[256,256]{1,0:T(8,128)(2,1)S(1)} %get-tuple-element.161.refs_1_), channel_id=1, source_target_pairs={{0,32},{32,64},{64,96},{128,160},{160,192},{192,224},{1,33},{33,65... | collective-permute-start | bytes 393224 | tf_op jit(solution)/shard_map/ppermute | solution.py:568
  141.0 5.2 %collective-permute-start.10 = (bf16[64,512]{1,0:T(8,128)(2,1)S(1)}, bf16[64,512]{1,0:T(8,128)(2,1)S(1)}, u32[]{:S(2)}, u32[]{:S(2)}) collective-permute-start(bf16[64,512]{1,0:T(8,128)(2,1)S(1)} %get-tuple-element.162.refs_2_), channel_id=1, source_target_pairs={{96,128},{97,129},{98,130},{99,131},{100,132},{101,133},{102,134},... | collective-permute-start | bytes 196616 | tf_op jit(solution)/shard_map/ppermute | solution.py:567
  141.7 11.5 %collective-permute-start.11 = (bf16[64,512]{1,0:T(8,128)(2,1)S(1)}, bf16[64,512]{1,0:T(8,128)(2,1)S(1)}, u32[]{:S(2)}, u32[]{:S(2)}) collective-permute-start(bf16[64,512]{1,0:T(8,128)(2,1)S(1)} %get-tuple-element.153), channel_id=1, source_target_pairs={{0,32},{32,64},{64,96},{96,128},{128,160},{160,192},{192,224},{224... | collective-permute-start | bytes 196616 | tf_op jit(solution)/shard_map/ppermute | solution.py:569
  153.2 11.0 %all-to-all-start.6 = ((f32[32,4,128]{2,1,0:T(4,128)}), f32[32,4,128]{2,1,0:T(4,128)S(1)}, u32[]{:S(2)}, u32[]{:S(2)}) async-start(f32[32,4,128]{2,1,0:T(4,128)} %get-tuple-element.154), calls=%async_computation.6 | async-start | bytes 131072 | tf_op jit(solution)/shard_map/all_to_all | solution.py:517
  161.2 1.2 collective-permute-start.12
  166.9 13.4 %all-to-all-start.7 = ((f32[32,8,128]{2,1,0:T(8,128)}), f32[32,8,128]{2,1,0:T(8,128)S(1)}, u32[]{:S(2)}, u32[]{:S(2)}) async-start(f32[32,8,128]{2,1,0:T(8,128)} %get-tuple-element.160), calls=%async_computation.7 | async-start | bytes 262144 | tf_op jit(solution)/shard_map/all_to_all | solution.py:544
  172.9 30.1 %collective-permute-start.13 = (bf16[2,64,512]{2,1,0:T(8,128)(2,1)S(1)}, bf16[2,64,512]{2,1,0:T(8,128)(2,1)S(1)}, u32[]{:S(2)}, u32[]{:S(2)}) collective-permute-start(bf16[2,64,512]{2,1,0:T(8,128)(2,1)S(1)} %copy-done.5), channel_id=1, source_target_pairs={{128,0},{160,32},{192,64},{224,96},{129,1},{161,33},{193,65},{225,... | collective-permute-start | bytes 393224 | tf_op jit(solution)/shard_map/ppermute | solution.py:552
  (5 other events, 103.9 us)
Sparse Core Ops, SparseCore 0:
  37.8 41.0 all-gather.2

commit v2 on v1

--- a/solution.py
+++ b/solution.py
@@ -116,15 +116,19 @@
 
 def fine_first(tick, *refs):
     if tick == 0:
-        place, inflow, pending, mixing, kernels, cpending = refs[:6]
-        refs = refs[6:]
+        place, inflow, pending, mixing, kernels = refs[:5]
+        refs = refs[5:]
     else:
         place, arrived, raised_in, entries, raising, pending, mixing, kernels = refs[:8]
         refs = refs[8:]
     h_ref, pay_ref = refs[:2]
-    x_ref, padded, skip_ref, mix_ref, held, sems = refs[(3 if tick == 0 else 2) :][:6]
+    if tick == 0:
+        packed, held, second = refs[2:5]
+        x_ref, padded, skip_ref, mix_ref, sems, staged, pack_sems = refs[5:]
+    else:
+        x_ref, padded, skip_ref, mix_ref, sems, spread_ref, up_ref, up_sems = refs[2:]
     segment = place[0]
-    kernel = Streamed(kernels.at[0], held, sems.at[pl.ds(0, 3)])
+    kernel = Streamed(kernels.at[0], held, sems.at[pl.ds(0, 3)]) if tick == 0 else kernels
     skip = pltpu.make_async_copy(pending.at[tick], skip_ref, sems.at[3])
     mix = pltpu.make_async_copy(mixing, mix_ref, sems.at[4])
 
@@ -132,7 +136,6 @@
         x = pltpu.make_async_copy(inflow, x_ref, sems.at[5])
         x.start()
     else:
-        spread_ref, up_ref, up_sems = refs[8:]
         up = Streamed(raising, up_ref, up_sems)
 
         @pl.when(segment == HALF)
@@ -148,30 +151,16 @@
         mix.start()
         skip.start()
 
-    kernel.start()
-    if tick == 0:
-        packed, staged, pack_sems = refs[2], refs[9], refs[10]
+    if tick == 0:
+        kernel.start()
+        onward = pltpu.make_async_copy(kernels.at[1], second, pack_sems.at[5])
+        onward.start()
         loads = [pltpu.make_async_copy(pending.at[slot], staged.at[slot], pack_sems.at[slot]) for slot in range(4)]
-        cloads = [
-            pltpu.make_async_copy(
-                cpending.at[slot, :, pl.ds(side * FCH, FCH)],
-                staged.at[0, pl.ds((2 * slot + side) * CCELLS, CCELLS)],
-                pack_sems.at[2 * slot + side],
-            )
-            for slot in range(2)
-            for side in range(2)
-        ]
         store = pltpu.make_async_copy(staged, packed, pack_sems.at[4])
-        cstore = pltpu.make_async_copy(staged.at[0], packed.at[0], pack_sems.at[4])
 
         @pl.when(segment < HALF)
         def _():
             for copy in loads:
-                copy.start()
-
-        @pl.when(segment >= HALF)
-        def _():
-            for copy in cloads:
                 copy.start()
 
     if tick == 0:
@@ -213,43 +202,24 @@
                 copy.wait()
             store.start()
 
-        @pl.when(segment >= HALF)
-        def _():
-            for copy in cloads:
-                copy.wait()
-            cstore.start()
-
     h = fine_convolution(x_ref[...].astype(F32), padded, kernel)
     h_ref[...] = h
     mean, spread = local_moments(h)
     pay = jnp.concatenate(rows_of(mean) + rows_of(spread), axis=0)
     pay_ref[...] = jnp.broadcast_to(pay[None], pay_ref.shape)
     if tick == 0:
+        onward.wait()
 
         @pl.when(segment < HALF)
         def _():
             store.wait()
-
-        @pl.when(segment >= HALF)
-        def _():
-            cstore.wait()
 
 
 def coarse_first(tick, *refs):
     place, arrived, pending, mixing, kernels = refs[:5]
     h_ref, mine_ref, other_ref, x_ref, padded, mix_ref, held, sems, skip_ref = refs[5:]
     kernel = Streamed(kernels, held, sems.at[pl.ds(3, 3)])
-    if tick < 2:
-        skips = [pltpu.make_async_copy(pending.at[tick], skip_ref, sems.at[1])]
-    else:
-        skips = [
-            pltpu.make_async_copy(
-                pending.at[1, 0, pl.ds((2 * (tick - 2) + side) * CCELLS, CCELLS)],
-                skip_ref.at[:, pl.ds(side * FCH, FCH)],
-                sems.at[(1, 6)[side]],
-            )
-            for side in range(2)
-        ]
+    skips = [pltpu.make_async_copy(pending.at[tick % 2], skip_ref, sems.at[1])]
     segment = place[0]
     mix = pltpu.make_async_copy(mixing, mix_ref, sems.at[0])
 
@@ -293,8 +263,7 @@
     other_ref[...] = jnp.where(is_first, second, first)
 
 
-def fine_second(gathered, h_ref, gains, shifts, kernels, mine, theirs, out_ref, pay_ref, padded, held, sems):
-    kernel = Streamed(kernels.at[1], held, sems).start()
+def fine_second(gathered, h_ref, gains, shifts, kernel, mine, theirs, out_ref, pay_ref, padded):
     mean, spread = merged([gathered[i] for i in range(N_DP)], float(CELLS))
     x = activated(h_ref[...], mean, spread, gains[0:1], shifts[0:1]).astype(BF16)
     h = fine_convolution(x.astype(F32), padded, kernel)
@@ -307,46 +276,36 @@
     pay_ref[...] = jnp.broadcast_to(pay[None], pay_ref.shape)
 
 
-def finish(tick, place, gathered, h_ref, hc_ref, gains, shifts, cgains, cshifts, *refs):
-    if tick == TICKS - 1:
-        fine_ref, coarse_ref = refs
-    else:
-        descent, fine_ref, coarse_ref, going, fine32, packed, down_ref, sem = refs
-        fetch = pltpu.make_async_copy(descent, down_ref, sem)
-
-        @pl.when(place[0] == HALF - 1)
-        def _():
-            fetch.start()
-
+def finish(tick, gathered, h_ref, hc_ref, gains, shifts, cgains, cshifts, fine_ref, coarse_ref):
     mean, spread = merged([gathered[i, 0:4] for i in range(N_DP)], float(CELLS))
-    fine = activated(h_ref[...], mean, spread, gains[1:2], shifts[1:2]).astype(BF16)
+    fine_ref[...] = activated(h_ref[...], mean, spread, gains[1:2], shifts[1:2]).astype(BF16)
     mean0, spread0 = merged([gathered[i, 4:8] for i in range(0, N_DP, 2)], 2.0 * CCELLS)
     mean1, spread1 = merged([gathered[i, 4:8] for i in range(1, N_DP, 2)], 2.0 * CCELLS)
     mean = jnp.concatenate([mean0, mean1], axis=1)
     spread = jnp.concatenate([spread0, spread1], axis=1)
-    coarse = activated(hc_ref[...], mean, spread, cgains[...], cshifts[...]).astype(BF16)
-    fine_ref[...] = fine
-    coarse_ref[...] = coarse
-    if tick < TICKS - 1:
-        segment = place[0]
-
-        @pl.when(segment != HALF - 1)
-        def _():
-            going[...] = coarse
-
-        @pl.when(segment == HALF - 1)
-        def _():
-            for p in range(FCH // 128):
-                fine32[...] = fine[:, p * 128 : (p + 1) * 128].astype(F32)
-                for a in range(2):
-                    for c in range(2):
-                        taken = [
-                            fine32[pl.ds((2 * i + a) * SIDE + c, CSIDE, stride=2), :] for i in range(CSIDE)
-                        ]
-                        column = (2 * a + c) * FCH + p * 128
-                        packed[:, column : column + 128] = jnp.concatenate(taken, axis=0).astype(BF16)
-            fetch.wait()
-            going[...] = dot(packed[...], down_ref[...]).astype(BF16)
+    coarse_ref[...] = activated(hc_ref[...], mean, spread, cgains[...], cshifts[...]).astype(BF16)
+
+
+def coarse_sent(place, fine, coarse, descent, going, fine32, packed, down_ref, sem):
+    segment = place[0]
+
+    @pl.when(segment != HALF - 1)
+    def _():
+        going[...] = coarse[...]
+
+    @pl.when(segment == HALF - 1)
+    def _():
+        fetch = pltpu.make_async_copy(descent, down_ref, sem)
+        fetch.start()
+        for p in range(FCH // 128):
+            fine32[...] = fine[:, p * 128 : (p + 1) * 128].astype(F32)
+            for a in range(2):
+                for c in range(2):
+                    taken = [fine32[pl.ds((2 * i + a) * SIDE + c, CSIDE, stride=2), :] for i in range(CSIDE)]
+                    column = (2 * a + c) * FCH + p * 128
+                    packed[:, column : column + 128] = jnp.concatenate(taken, axis=0).astype(BF16)
+        fetch.wait()
+        going[...] = dot(packed[...], down_ref[...]).astype(BF16)
 
 
 def keep(tick, *refs):
@@ -386,7 +345,7 @@
         fetch = pltpu.make_async_copy(cmixing, cmix_ref, sems.at[3])
         fetch.start()
         if tick == 2:
-            received = pltpu.make_async_copy(extra.at[0], staged, sems.at[4])
+            received = pltpu.make_async_copy(extra, staged, sems.at[4])
             received.start()
         fetch.wait()
         cterm[...] = dot(coarse[...], cmix_ref[...]).astype(BF16)
@@ -474,43 +433,45 @@
     fine_route = [(0, 1), (1, 2), (2, 3), (4, 5), (5, 6), (6, 7)]
     up_route = [(HALF - 1, HALF)]
     coarse_route = [(p, (p + 1) % (2 * HALF)) for p in range(2 * HALF)]
-    pairs = [[p, p + HALF] for p in range(HALF)]
+    to_decoder = [(p, p + HALF) for p in range(HALF)]
+    to_encoder = [(p + HALF, p) for p in range(HALF)]
     cores = [(i, i ^ 1) for i in range(N_DP)]
 
     ftile, ctile = (CELLS, FCH), (CCELLS, CCH)
     fine_bf, coarse_bf = pltpu.VMEM(ftile, BF16), pltpu.VMEM(ctile, BF16)
     padded = pltpu.VMEM((CELLS + 2 * SIDE, 3 * FCH), BF16)
-    held = pltpu.VMEM((3, 3 * FCH, FCH), BF16)
+    vmem, hbm = pltpu.VMEM, pltpu.HBM
+    kernel_kept = (vmem, (3, 3 * FCH, FCH))
     conv_flops = 2 * CELLS * 9 * FCH * FCH
-    vmem, hbm = pltpu.VMEM, pltpu.HBM
 
     arrived = raised = carrived = kept = None
     for tick in range(TICKS):
         sending = tick < TICKS - 1
         if tick == 0:
-            sources, specs = (inflow, pending, mixing, kernels, cpending), [SM, ANY, ANY, ANY, ANY, ANY]
-            more = (pltpu.VMEM((4, CELLS, FCH), BF16), pltpu.SemaphoreType.DMA((5,)))
+            sources, specs = (inflow, pending, mixing, kernels), [SM, ANY, ANY, ANY, ANY]
+            more = (pltpu.VMEM((4, CELLS, FCH), BF16), pltpu.SemaphoreType.DMA((6,)))
         else:
-            sources = (arrived, raised, entries, upsampling, pending, mixing, kernels)
-            specs = [SM, VM, VM, ANY, ANY, ANY, ANY, ANY]
+            sources = (arrived, raised, entries, upsampling, pending, mixing, kernel_one)
+            specs = [SM, VM, VM, ANY, ANY, ANY, ANY, VM]
             more = (
                 pltpu.VMEM((2, CELLS, 128), F32),
                 pltpu.VMEM((4, CCH, FCH), BF16),
                 pltpu.SemaphoreType.DMA((4,)),
             )
-        h1, pay, *packed = call(
+        h1, pay, *handed = call(
             functools.partial(fine_first, tick),
-            [(vmem, ftile, F32), (vmem, (N_DP, 4, 128), F32)] + [(hbm, (4, CELLS, FCH))] * (tick == 0),
+            [(vmem, ftile, F32), (vmem, (N_DP, 4, 128), F32)] + ([(hbm, (4, CELLS, FCH)), kernel_kept, kernel_kept] if tick == 0 else []),
             specs,
-            (fine_bf, padded, fine_bf, pltpu.VMEM((FCH, FCH), BF16), held, pltpu.SemaphoreType.DMA((6,)), *more),
+            (fine_bf, padded, fine_bf, pltpu.VMEM((FCH, FCH), BF16), pltpu.SemaphoreType.DMA((6,)), *more),
             conv_flops,
             1_000_000,
         )(place, *sources)
 
         if tick == 0:
             carrived = cinflow
+            packed, kernel_one, kernel_two = handed
             pay, later = tied(pay, place)
-            skips = lax.all_gather(packed[0], "segment", axis_index_groups=pairs)
+            skips = lax.ppermute(packed, "segment", to_decoder)
         else:
             pay, carrived = tied(pay, carrived)
             later = place
@@ -529,44 +490,55 @@
             ),
             2 * CCELLS * 9 * CCH * CCH,
             1_500_000,
-        )(later, carrived, cpending if tick < 2 else skips, cmixing, ckernel)
+        )(later, carrived, cpending if tick < 2 else cskips, cmixing, ckernel)
         theirs = lax.ppermute(other, "dp", cores)
+        if tick == 2:
+            gathered, skips = tied(gathered, skips)
         h2, pay2 = call(
             fine_second,
             [(vmem, ftile, F32), (vmem, (N_DP, 8, 128), F32)],
-            [VM, VM, VM, VM, ANY, VM, VM],
-            (padded, held, pltpu.SemaphoreType.DMA((3,))),
+            [VM] * 7,
+            (padded,),
             conv_flops,
             1_000_000,
-        )(gathered, h1, gains, shifts, kernels, mine, theirs)
+        )(gathered, h1, gains, shifts, kernel_two, mine, theirs)
         if tick > 0:
             pay2, own, cown = tied(pay2, own, cown)
         gathered2 = lax.all_to_all(pay2, "dp", 0, 0, tiled=True)
         if tick == 0:
-            gathered2, upsampling = tied(gathered2, upsampling)
+            cskips = lax.ppermute(tied(cpending, pay2)[0], "segment", to_encoder)
+            gathered2, upsampling, cskips = tied(gathered2, upsampling, cskips)
         else:
             added = ((pending,), (), (skips,))[tick - 1]
             kept = kept_after(tick - 1, (place, own, cown, mixing, cmixing), added, kept)
             gathered2, *kept = tied(gathered2, *kept)
             if tick == 2:
-                fresh = lax.ppermute(kept[3], "segment", [(p + HALF, p) for p in range(HALF)])
-        own, cown, *going = call(
+                fresh = lax.ppermute(kept[3], "segment", to_encoder)
+        own, cown = call(
             functools.partial(finish, tick),
-            [(vmem, ftile), (vmem, ctile)] + ([(vmem, ctile)] if sending else []),
-            [SM] + [VM] * 7 + [ANY] * sending,
-            (
-                pltpu.VMEM((CELLS, 128), F32),
-                pltpu.VMEM((CCELLS, 4 * FCH), BF16),
-                pltpu.VMEM((4 * FCH, CCH), BF16),
-                pltpu.SemaphoreType.DMA,
-            ) if sending else (),
-            100_000_000,
+            [(vmem, ftile), (vmem, ctile)],
+            [VM] * 7,
+            (),
             1_000_000,
-        )(place, gathered2, h2, hc, gains, shifts, cgains, cshifts, *((descent,) if sending else ()))
+            1_000_000,
+        )(gathered2, h2, hc, gains, shifts, cgains, cshifts)
         if sending:
             raised = lax.ppermute(cown, "segment", up_route)
             arrived = lax.ppermute(own, "segment", fine_route)
-            carrived = lax.ppermute(going[0], "segment", coarse_route)
+            (going,) = call(
+                coarse_sent,
+                [(vmem, ctile)],
+                [SM, VM, VM, ANY],
+                (
+                    pltpu.VMEM((CELLS, 128), F32),
+                    pltpu.VMEM((CCELLS, 4 * FCH), BF16),
+                    pltpu.VMEM((4 * FCH, CCH), BF16),
+                    pltpu.SemaphoreType.DMA,
+                ),
+                100_000_000,
+                1_000_000,
+            )(place, own, cown, descent)
+            carrived = lax.ppermute(going, "segment", coarse_route)
     fstash, cstash, fback, cback = kept_after(
         TICKS - 1, (place, own, cown, mixing, cmixing), (fresh,), kept
     )

time: 213 us -> 196 us (0.920)
  starting transfers between devices: 66.2 us -> 85.8 us
  waiting for transfers between devices: 78.2 us -> 61.2 us
  between operations: 14.4 us -> 1.17 us
  Pallas kernels: 52.2 us -> 44.8 us
    all_to_all x4, starting transfers between devices: 21.2 us -> 38.7 us  [on_device(): gathered = lax.all_to_all(pay, 'dp', 0, 0, tiled=True)]
    all_to_all x4, waiting for transfers between devices: 18.5 us -> 8.64 us  [on_device(): gathered2 = lax.all_to_all(pay2, 'dp', 0, 0, tiled=True)]
    pallas_call x20 -> x23, Pallas kernels: 52.2 us -> 44.8 us  [call(): kernel(*[placed(spec, arg) for spec, arg in zip(in_specs, args, strict=Tr...]
    all_to_all x4, waiting for transfers between devices: 14.6 us -> 8.13 us  [on_device(): gathered = lax.all_to_all(pay, 'dp', 0, 0, tiled=True)]
    ppermute x4 -> x6, starting transfers between devices: 8.82 us -> 13.8 us  [the longest x1 7.35 us: on_device(): skips = lax.ppermute(packed, 'segment', to_decoder)]
    ppermute x3, starting transfers between devices: 10.5 us -> 6.46 us  [on_device(): arrived = lax.ppermute(own, 'segment', fine_route)]
    ppermute x4 -> x6, waiting for transfers between devices: 37 us -> 39 us  [the longest x3 18.2 us: on_device(): carrived = lax.ppermute(going, 'segment', coarse_route)]
  transfers between devices with their start and end apart: 23 -> 24, of which waited for: 18 -> 15; matrix products, arithmetic and copies ran while one was open for 1% -> 1% of each run, Pallas kernels for 18% -> 17%
where the time goes in v2:
time: 196 us; the launch traced here: 195 us
  starting transfers between devices  85.8 us (44%)
  waiting for transfers between devices  61.2 us (31%)
  Pallas kernels  44.8 us (23%)
  local copies, waits for them, and re-layouts  2.43 us (1%)
    pallas_call x23, Pallas kernels, call(): kernel(*[placed(spec, arg) for spec, arg in zip(in_specs, args, strict=Tr...  44.8 us
    all_to_all x4, starting transfers between devices, on_device(): gathered = lax.all_to_all(pay, 'dp', 0, 0, tiled=True)  38.7 us
    all_to_all x4, starting transfers between devices, on_device(): gathered2 = lax.all_to_all(pay2, 'dp', 0, 0, tiled=True)  23.8 us
    ppermute x3, waiting for transfers between devices, on_device(): carrived = lax.ppermute(going, 'segment', coarse_route)  18.2 us
    ppermute x1, waiting for transfers between devices, on_device(): cskips = lax.ppermute(tied(cpending, pay2)[0], 'segment', to_encoder)  10.6 us
    ppermute x1, waiting for transfers between devices, on_device(): fresh = lax.ppermute(kept[3], 'segment', to_encoder)  10.1 us
    all_to_all x4, waiting for transfers between devices, on_device(): gathered2 = lax.all_to_all(pay2, 'dp', 0, 0, tiled=True)  8.64 us
    all_to_all x4, waiting for transfers between devices, on_device(): gathered = lax.all_to_all(pay, 'dp', 0, 0, tiled=True)  8.13 us
  transfers between devices with their start and end apart: 24, of which 15 were waited for; matrix products, arithmetic and copies ran while one was open for 1% of the time, Pallas kernels for 17%

profile of v2, /device:TPU:32, one launch (start us, length us, event | category | flops | bytes accessed | tf_op | source)
XLA Modules:
  0.0 195.4 jit_solution(57381072137396093)
XLA Ops:
  0.7 4.0 %shard_map.174 = (f32[256,256]{1,0:T(8,128)S(1)}, f32[32,4,128]{2,1,0:T(4,128)}, bf16[4,256,256]{2,1,0:T(8,128)(2,1)}, bf16[3,768,256]{2,1,0:T(8,128)(2,1)S(1)}, bf16[3,768,256]{2,1,0:T(8,128)(2,1)S(1)}) custom-call(s32[2]{0:T(128)S(1)} %pad_add_fusion.refs_0_.place, bf16[256,256]{1,0:T(8,128)(2,1)} %bitcast.86, bf16[6,256,256]{2,1,0:T(8,128)(2,1)} %bitcast.56, ...), custom_call_target="tpu_custom_call" | custom-call | flops 301989888 | bytes 1000000 | tf_op jit(solution)/shard_map/pallas_call | solution.py:40
  4.8 8.8 %all-to-all-start = ((f32[32,4,128]{2,1,0:T(4,128)}), f32[32,4,128]{2,1,0:T(4,128)S(1)}, u32[]{:S(2)}, u32[]{:S(2)}) async-start(f32[32,4,128]{2,1,0:T(4,128)} %get-tuple-element.98), calls=%async_computation | async-start | bytes 131072 | tf_op jit(solution)/shard_map/all_to_all | solution.py:478
  13.6 3.7 %shard_map.175 = (f32[64,512]{1,0:T(8,128)S(1)}, f32[4,128]{1,0:T(4,128)S(1)}, f32[4,128]{1,0:T(4,128)S(1)}) custom-call(s32[2]{0:T(128)S(1)} %pad_add_fusion.refs_0_.place, bf16[64,512]{1,0:T(8,128)(2,1)} %bitcast.88, bf16[2,64,512]{2,1,0:T(8,128)(2,1)} %bitcast.83, bf16[512,512]{1,0:T(8,128)(2,1)} %bitcast.48, bf16[3,1536,512]{2,1,0:T(8,128)(2,1)} %bitcast.44), custom_call_target="tpu_custom_call" | custom-call | flops 301989888 | bytes 1500000 | tf_op jit(solution)/shard_map/pallas_call | solution.py:40
  21.6 6.0 %all-to-all-start.1 = ((f32[32,8,128]{2,1,0:T(8,128)}), f32[32,8,128]{2,1,0:T(8,128)S(1)}, u32[]{:S(2)}, u32[]{:S(2)}) async-start(f32[32,8,128]{2,1,0:T(8,128)} %get-tuple-element.104), calls=%async_computation.1 | async-start | bytes 262144 | tf_op jit(solution)/shard_map/all_to_all | solution.py:507
  31.3 10.6 %collective-permute-done.1.refs_2_ = bf16[2,64,512]{2,1,0:T(8,128)(2,1)S(1)} collective-permute-done((bf16[2,64,512]{2,1,0:T(8,128)(2,1)S(1)}, bf16[2,64,512]{2,1,0:T(8,128)(2,1)S(1)}, u32[]{:S(2)}, u32[]{:S(2)}) %collective-permute-start.1) | collective-permute-done | bytes 131104 | tf_op jit(solution)/shard_map/ppermute | solution.py:509
  42.1 3.4 %collective-permute-start.2 = (bf16[256,256]{1,0:T(8,128)(2,1)S(1)}, bf16[256,256]{1,0:T(8,128)(2,1)S(1)}, u32[]{:S(2)}, u32[]{:S(2)}) collective-permute-start(bf16[256,256]{1,0:T(8,128)(2,1)S(1)} %get-tuple-element.121.fine.refs_1_), channel_id=1, source_target_pairs={{0,32},{32,64},{64,96},{128,160},{160,192},{192,224},{1,33},{33,65... | collective-permute-start | bytes 393224 | tf_op jit(solution)/shard_map/ppermute | solution.py:527
  51.1 6.1 %collective-permute-done.4.refs_1_ = bf16[64,512]{1,0:T(8,128)(2,1)S(1)} collective-permute-done((bf16[64,512]{1,0:T(8,128)(2,1)S(1)}, bf16[64,512]{1,0:T(8,128)(2,1)S(1)}, u32[]{:S(2)}, u32[]{:S(2)}) %collective-permute-start.4) | collective-permute-done | bytes 65568 | tf_op jit(solution)/shard_map/ppermute | solution.py:541
  57.2 6.6 %all-to-all-start.2 = ((f32[32,4,128]{2,1,0:T(4,128)}), f32[32,4,128]{2,1,0:T(4,128)S(1)}, u32[]{:S(2)}, u32[]{:S(2)}) async-start(f32[32,4,128]{2,1,0:T(4,128)} %get-tuple-element.114), calls=%async_computation.2 | async-start | bytes 131072 | tf_op jit(solution)/shard_map/all_to_all | solution.py:478
  63.8 3.7 %shard_map.180 = (f32[64,512]{1,0:T(8,128)S(1)}, f32[4,128]{1,0:T(4,128)S(1)}, f32[4,128]{1,0:T(4,128)S(1)}) custom-call(s32[2]{0:T(128)S(1)} %pad_add_fusion.refs_0_.place, bf16[64,512]{1,0:T(8,128)(2,1)S(1)} %collective-permute-done.4.refs_1_, bf16[2,64,512]{2,1,0:T(8,128)(2,1)} %bitcast.84, bf16[512,512]{1,0:T(8,128)(2,1)} %bitcast.49, ...), custom_call_target="tpu_custom_call" | custom-call | flops 301989888 | bytes 1500000 | tf_op jit(solution)/shard_map/pallas_call | solution.py:40
  71.7 5.9 %all-to-all-start.3 = ((f32[32,8,128]{2,1,0:T(8,128)}), f32[32,8,128]{2,1,0:T(8,128)S(1)}, u32[]{:S(2)}, u32[]{:S(2)}) async-start(f32[32,8,128]{2,1,0:T(8,128)} %get-tuple-element.120), calls=%async_computation.3 | async-start | bytes 262144 | tf_op jit(solution)/shard_map/all_to_all | solution.py:507
  77.7 7.3 %collective-permute-start.9 = (bf16[4,256,256]{2,1,0:T(8,128)(2,1)}, bf16[4,256,256]{2,1,0:T(8,128)(2,1)}, u32[]{:S(2)}, u32[]{:S(2)}) collective-permute-start(bf16[4,256,256]{2,1,0:T(8,128)(2,1)} %get-tuple-element.134), channel_id=1, source_target_pairs={{0,128},{32,160},{64,192},{96,224},{1,129},{33,161},{65,193},{97,2... | collective-permute-start | bytes 1572872 | tf_op jit(solution)/shard_map/ppermute | solution.py:474
  85.0 3.2 %shard_map.182 = (bf16[4,256,256]{2,1,0:T(8,128)(2,1)}, bf16[4,64,512]{2,1,0:T(8,128)(2,1)}, bf16[6,256,256]{2,1,0:T(8,128)(2,1)}, bf16[2,64,512]{2,1,0:T(8,128)(2,1)}) custom-call(s32[2]{0:T(128)S(1)} %pad_add_fusion.refs_0_.place, bf16[256,256]{1,0:T(8,128)(2,1)S(1)} %get-tuple-element.121.fine.refs_1_, ...), custom_call_target="tpu_custom_call" | custom-call | flops 40000000 | bytes 1000000 | tf_op jit(solution)/shard_map/pallas_call | solution.py:40
  96.4 5.5 %collective-permute-done.8.refs_1_ = bf16[64,512]{1,0:T(8,128)(2,1)S(1)} collective-permute-done((bf16[64,512]{1,0:T(8,128)(2,1)S(1)}, bf16[64,512]{1,0:T(8,128)(2,1)S(1)}, u32[]{:S(2)}, u32[]{:S(2)}) %collective-permute-start.8) | collective-permute-done | bytes 65568 | tf_op jit(solution)/shard_map/ppermute | solution.py:541
  101.9 19.2 %all-to-all-start.4 = ((f32[32,4,128]{2,1,0:T(4,128)}), f32[32,4,128]{2,1,0:T(4,128)S(1)}, u32[]{:S(2)}, u32[]{:S(2)}) async-start(f32[32,4,128]{2,1,0:T(4,128)} %get-tuple-element.133), calls=%async_computation.4 | async-start | bytes 131072 | tf_op jit(solution)/shard_map/all_to_all | solution.py:478
  121.1 3.7 %shard_map.186 = (f32[64,512]{1,0:T(8,128)S(1)}, f32[4,128]{1,0:T(4,128)S(1)}, f32[4,128]{1,0:T(4,128)S(1)}) custom-call(s32[2]{0:T(128)S(1)} %pad_add_fusion.refs_0_.place, bf16[64,512]{1,0:T(8,128)(2,1)S(1)} %collective-permute-done.8.refs_1_, bf16[2,64,512]{2,1,0:T(8,128)(2,1)} %copy-done.5, bf16[512,512]{1,0:T(8,128)(2,1)} %bitcast.51, ...), custom_call_target="tpu_custom_call" | custom-call | flops 301989888 | bytes 1500000 | tf_op jit(solution)/shard_map/pallas_call | solution.py:40
  125.0 2.8 %all-to-all-done.4.gathered = f32[32,4,128]{2,1,0:T(4,128)S(1)} async-done(((f32[32,4,128]{2,1,0:T(4,128)}), f32[32,4,128]{2,1,0:T(4,128)S(1)}, u32[]{:S(2)}, u32[]{:S(2)}) %all-to-all-start.4) | async-done | bytes 65568 | tf_op jit(solution)/shard_map/all_to_all | solution.py:478
  129.1 5.9 %all-to-all-start.5 = ((f32[32,8,128]{2,1,0:T(8,128)}), f32[32,8,128]{2,1,0:T(8,128)S(1)}, u32[]{:S(2)}, u32[]{:S(2)}) async-start(f32[32,8,128]{2,1,0:T(8,128)} %get-tuple-element.142), calls=%async_computation.5 | async-start | bytes 262144 | tf_op jit(solution)/shard_map/all_to_all | solution.py:507
  137.5 5.0 %all-to-all-done.5.gathered = f32[32,8,128]{2,1,0:T(8,128)S(1)} async-done(((f32[32,8,128]{2,1,0:T(8,128)}), f32[32,8,128]{2,1,0:T(8,128)S(1)}, u32[]{:S(2)}, u32[]{:S(2)}) %all-to-all-start.5) | async-done | bytes 131104 | tf_op jit(solution)/shard_map/all_to_all | solution.py:507
  150.4 6.7 %collective-permute-done.13.refs_1_ = bf16[64,512]{1,0:T(8,128)(2,1)S(1)} collective-permute-done((bf16[64,512]{1,0:T(8,128)(2,1)S(1)}, bf16[64,512]{1,0:T(8,128)(2,1)S(1)}, u32[]{:S(2)}, u32[]{:S(2)}) %collective-permute-start.13) | collective-permute-done | bytes 65568 | tf_op jit(solution)/shard_map/ppermute | solution.py:541
  157.1 4.1 %all-to-all-start.6 = ((f32[32,4,128]{2,1,0:T(4,128)}), f32[32,4,128]{2,1,0:T(4,128)S(1)}, u32[]{:S(2)}, u32[]{:S(2)}) async-start(f32[32,4,128]{2,1,0:T(4,128)} %get-tuple-element.159), calls=%async_computation.6 | async-start | bytes 131072 | tf_op jit(solution)/shard_map/all_to_all | solution.py:478
  161.2 3.7 %shard_map.192 = (f32[64,512]{1,0:T(8,128)S(1)}, f32[4,128]{1,0:T(4,128)S(1)}, f32[4,128]{1,0:T(4,128)S(1)}) custom-call(s32[2]{0:T(128)S(1)} %pad_add_fusion.refs_0_.place, bf16[64,512]{1,0:T(8,128)(2,1)S(1)} %collective-permute-done.13.refs_1_, bf16[2,64,512]{2,1,0:T(8,128)(2,1)} %copy-done.5, bf16[512,512]{1,0:T(8,128)(2,1)} %bitcast.53, ...), custom_call_target="tpu_custom_call" | custom-call | flops 301989888 | bytes 1500000 | tf_op jit(solution)/shard_map/pallas_call | solution.py:40
  169.2 5.9 %all-to-all-start.7 = ((f32[32,8,128]{2,1,0:T(8,128)}), f32[32,8,128]{2,1,0:T(8,128)S(1)}, u32[]{:S(2)}, u32[]{:S(2)}) async-start(f32[32,8,128]{2,1,0:T(8,128)} %get-tuple-element.165), calls=%async_computation.7 | async-start | bytes 262144 | tf_op jit(solution)/shard_map/all_to_all | solution.py:507
  178.9 3.7 %all-to-all-done.7.gathered = f32[32,8,128]{2,1,0:T(8,128)S(1)} async-done(((f32[32,8,128]{2,1,0:T(8,128)}), f32[32,8,128]{2,1,0:T(8,128)S(1)}, u32[]{:S(2)}, u32[]{:S(2)}) %all-to-all-start.7) | async-done | bytes 131104 | tf_op jit(solution)/shard_map/all_to_all | solution.py:507
  182.7 10.1 %collective-permute-done.15.refs_5_ = bf16[2,64,512]{2,1,0:T(8,128)(2,1)S(1)} collective-permute-done((bf16[2,64,512]{2,1,0:T(8,128)(2,1)S(1)}, bf16[2,64,512]{2,1,0:T(8,128)(2,1)S(1)}, u32[]{:S(2)}, u32[]{:S(2)}) %collective-permute-start.15) | collective-permute-done | bytes 131104 | tf_op jit(solution)/shard_map/ppermute | solution.py:516
  (63 shorter events, 48.7 us)
Async XLA Ops:
  4.8 15.5 %all-to-all-start = ((f32[32,4,128]{2,1,0:T(4,128)}), f32[32,4,128]{2,1,0:T(4,128)S(1)}, u32[]{:S(2)}, u32[]{:S(2)}) async-start(f32[32,4,128]{2,1,0:T(4,128)} %get-tuple-element.98), calls=%async_computation | async-start | bytes 131072 | tf_op jit(solution)/shard_map/all_to_all | solution.py:478
  17.3 1.2 collective-permute-start
  21.6 20.4 %all-to-all-start.1 = ((f32[32,8,128]{2,1,0:T(8,128)}), f32[32,8,128]{2,1,0:T(8,128)S(1)}, u32[]{:S(2)}, u32[]{:S(2)}) async-start(f32[32,8,128]{2,1,0:T(8,128)} %get-tuple-element.104), calls=%async_computation.1 | async-start | bytes 262144 | tf_op jit(solution)/shard_map/all_to_all | solution.py:507
  27.6 14.3 %collective-permute-start.1 = (bf16[2,64,512]{2,1,0:T(8,128)(2,1)S(1)}, bf16[2,64,512]{2,1,0:T(8,128)(2,1)S(1)}, u32[]{:S(2)}, u32[]{:S(2)}) collective-permute-start(bf16[2,64,512]{2,1,0:T(8,128)(2,1)S(1)} %bitcast.85), channel_id=1, source_target_pairs={{128,0},{160,32},{192,64},{224,96},{129,1},{161,33},{193,65},{225,... | collective-permute-start | bytes 393224 | tf_op jit(solution)/shard_map/ppermute | solution.py:509
  42.1 6.2 %collective-permute-start.2 = (bf16[256,256]{1,0:T(8,128)(2,1)S(1)}, bf16[256,256]{1,0:T(8,128)(2,1)S(1)}, u32[]{:S(2)}, u32[]{:S(2)}) collective-permute-start(bf16[256,256]{1,0:T(8,128)(2,1)S(1)} %get-tuple-element.121.fine.refs_1_), channel_id=1, source_target_pairs={{0,32},{32,64},{64,96},{128,160},{160,192},{192,224},{1,33},{33,65... | collective-permute-start | bytes 393224 | tf_op jit(solution)/shard_map/ppermute | solution.py:527
  45.5 2.8 %collective-permute-start.3 = (bf16[64,512]{1,0:T(8,128)(2,1)S(1)}, bf16[64,512]{1,0:T(8,128)(2,1)S(1)}, u32[]{:S(2)}, u32[]{:S(2)}) collective-permute-start(bf16[64,512]{1,0:T(8,128)(2,1)S(1)} %get-tuple-element.122.coarse.refs_2_), channel_id=1, source_target_pairs={{96,128},{97,129},{98,130},{99,131},{100,132},{101,133},{102,134},... | collective-permute-start | bytes 196616 | tf_op jit(solution)/shard_map/ppermute | solution.py:526
  46.8 10.4 %collective-permute-start.4 = (bf16[64,512]{1,0:T(8,128)(2,1)S(1)}, bf16[64,512]{1,0:T(8,128)(2,1)S(1)}, u32[]{:S(2)}, u32[]{:S(2)}) collective-permute-start(bf16[64,512]{1,0:T(8,128)(2,1)S(1)} %shard_map.179), channel_id=1, source_target_pairs={{0,32},{32,64},{64,96},{96,128},{128,160},{160,192},{192,224},{224... | collective-permute-start | bytes 196616 | tf_op jit(solution)/shard_map/ppermute | solution.py:541
  57.2 13.3 %all-to-all-start.2 = ((f32[32,4,128]{2,1,0:T(4,128)}), f32[32,4,128]{2,1,0:T(4,128)S(1)}, u32[]{:S(2)}, u32[]{:S(2)}) async-start(f32[32,4,128]{2,1,0:T(4,128)} %get-tuple-element.114), calls=%async_computation.2 | async-start | bytes 131072 | tf_op jit(solution)/shard_map/all_to_all | solution.py:478
  67.4 1.2 collective-permute-start.5
  71.7 16.5 %all-to-all-start.3 = ((f32[32,8,128]{2,1,0:T(8,128)}), f32[32,8,128]{2,1,0:T(8,128)S(1)}, u32[]{:S(2)}, u32[]{:S(2)}) async-start(f32[32,8,128]{2,1,0:T(8,128)} %get-tuple-element.120), calls=%async_computation.3 | async-start | bytes 262144 | tf_op jit(solution)/shard_map/all_to_all | solution.py:507
  77.7 47.3 %collective-permute-start.9 = (bf16[4,256,256]{2,1,0:T(8,128)(2,1)}, bf16[4,256,256]{2,1,0:T(8,128)(2,1)}, u32[]{:S(2)}, u32[]{:S(2)}) collective-permute-start(bf16[4,256,256]{2,1,0:T(8,128)(2,1)} %get-tuple-element.134), channel_id=1, source_target_pairs={{0,128},{32,160},{64,192},{96,224},{1,129},{33,161},{65,193},{97,2... | collective-permute-start | bytes 1572872 | tf_op jit(solution)/shard_map/ppermute | solution.py:474
  88.4 5.3 %collective-permute-start.6 = (bf16[256,256]{1,0:T(8,128)(2,1)S(1)}, bf16[256,256]{1,0:T(8,128)(2,1)S(1)}, u32[]{:S(2)}, u32[]{:S(2)}) collective-permute-start(bf16[256,256]{1,0:T(8,128)(2,1)S(1)} %get-tuple-element.143.fine.refs_1_), channel_id=1, source_target_pairs={{0,32},{32,64},{64,96},{128,160},{160,192},{192,224},{1,33},{33,65... | collective-permute-start | bytes 393224 | tf_op jit(solution)/shard_map/ppermute | solution.py:527
  90.2 3.5 %collective-permute-start.7 = (bf16[64,512]{1,0:T(8,128)(2,1)S(1)}, bf16[64,512]{1,0:T(8,128)(2,1)S(1)}, u32[]{:S(2)}, u32[]{:S(2)}) collective-permute-start(bf16[64,512]{1,0:T(8,128)(2,1)S(1)} %get-tuple-element.144.coarse.refs_2_), channel_id=1, source_target_pairs={{96,128},{97,129},{98,130},{99,131},{100,132},{101,133},{102,134},... | collective-permute-start | bytes 196616 | tf_op jit(solution)/shard_map/ppermute | solution.py:526
  91.4 10.5 %collective-permute-start.8 = (bf16[64,512]{1,0:T(8,128)(2,1)S(1)}, bf16[64,512]{1,0:T(8,128)(2,1)S(1)}, u32[]{:S(2)}, u32[]{:S(2)}) collective-permute-start(bf16[64,512]{1,0:T(8,128)(2,1)S(1)} %shard_map.185), channel_id=1, source_target_pairs={{0,32},{32,64},{64,96},{96,128},{128,160},{160,192},{192,224},{224... | collective-permute-start | bytes 196616 | tf_op jit(solution)/shard_map/ppermute | solution.py:541
  101.9 26.0 %all-to-all-start.4 = ((f32[32,4,128]{2,1,0:T(4,128)}), f32[32,4,128]{2,1,0:T(4,128)S(1)}, u32[]{:S(2)}, u32[]{:S(2)}) async-start(f32[32,4,128]{2,1,0:T(4,128)} %get-tuple-element.133), calls=%async_computation.4 | async-start | bytes 131072 | tf_op jit(solution)/shard_map/all_to_all | solution.py:478
  124.8 3.0 %collective-permute-start.10 = (f32[4,128]{1,0:T(4,128)S(1)}, f32[4,128]{1,0:T(4,128)S(1)}, u32[]{:S(2)}, u32[]{:S(2)}) collective-permute-start(f32[4,128]{1,0:T(4,128)S(1)} %get-tuple-element.140), channel_id=1, source_target_pairs={{0,1},{1,0},{2,3},{3,2},{4,5},{5,4},{6,7},{7,6},{8,9},{9,8},{10,11... | collective-permute-start | bytes 6152 | tf_op jit(solution)/shard_map/ppermute | solution.py:494
  129.1 13.3 %all-to-all-start.5 = ((f32[32,8,128]{2,1,0:T(8,128)}), f32[32,8,128]{2,1,0:T(8,128)S(1)}, u32[]{:S(2)}, u32[]{:S(2)}) async-start(f32[32,8,128]{2,1,0:T(8,128)} %get-tuple-element.142), calls=%async_computation.5 | async-start | bytes 262144 | tf_op jit(solution)/shard_map/all_to_all | solution.py:507
  142.6 5.1 %collective-permute-start.11 = (bf16[256,256]{1,0:T(8,128)(2,1)S(1)}, bf16[256,256]{1,0:T(8,128)(2,1)S(1)}, u32[]{:S(2)}, u32[]{:S(2)}) collective-permute-start(bf16[256,256]{1,0:T(8,128)(2,1)S(1)} %get-tuple-element.166.fine.refs_1_), channel_id=1, source_target_pairs={{0,32},{32,64},{64,96},{128,160},{160,192},{192,224},{1,33},{33,65... | collective-permute-start | bytes 393224 | tf_op jit(solution)/shard_map/ppermute | solution.py:527
  143.9 1.3 collective-permute-start.12
  145.2 11.9 %collective-permute-start.13 = (bf16[64,512]{1,0:T(8,128)(2,1)S(1)}, bf16[64,512]{1,0:T(8,128)(2,1)S(1)}, u32[]{:S(2)}, u32[]{:S(2)}) collective-permute-start(bf16[64,512]{1,0:T(8,128)(2,1)S(1)} %shard_map.191), channel_id=1, source_target_pairs={{0,32},{32,64},{64,96},{96,128},{128,160},{160,192},{192,224},{224... | collective-permute-start | bytes 196616 | tf_op jit(solution)/shard_map/ppermute | solution.py:541
  157.1 10.8 %all-to-all-start.6 = ((f32[32,4,128]{2,1,0:T(4,128)}), f32[32,4,128]{2,1,0:T(4,128)S(1)}, u32[]{:S(2)}, u32[]{:S(2)}) async-start(f32[32,4,128]{2,1,0:T(4,128)} %get-tuple-element.159), calls=%async_computation.6 | async-start | bytes 131072 | tf_op jit(solution)/shard_map/all_to_all | solution.py:478
  164.9 1.2 collective-permute-start.14
  169.2 13.4 %all-to-all-start.7 = ((f32[32,8,128]{2,1,0:T(8,128)}), f32[32,8,128]{2,1,0:T(8,128)S(1)}, u32[]{:S(2)}, u32[]{:S(2)}) async-start(f32[32,8,128]{2,1,0:T(8,128)} %get-tuple-element.165), calls=%async_computation.7 | async-start | bytes 262144 | tf_op jit(solution)/shard_map/all_to_all | solution.py:507
  175.2 17.6 %collective-permute-start.15 = (bf16[2,64,512]{2,1,0:T(8,128)(2,1)S(1)}, bf16[2,64,512]{2,1,0:T(8,128)(2,1)S(1)}, u32[]{:S(2)}, u32[]{:S(2)}) collective-permute-start(bf16[2,64,512]{2,1,0:T(8,128)(2,1)S(1)} %copy-done.6), channel_id=1, source_target_pairs={{128,0},{160,32},{192,64},{224,96},{129,1},{161,33},{193,65},{225,... | collective-permute-start | bytes 393224 | tf_op jit(solution)/shard_map/ppermute | solution.py:516
  (7 other events, 94.9 us)

commit v3 on v2

--- a/solution.py
+++ b/solution.py
@@ -492,8 +492,6 @@
             1_500_000,
         )(later, carrived, cpending if tick < 2 else cskips, cmixing, ckernel)
         theirs = lax.ppermute(other, "dp", cores)
-        if tick == 2:
-            gathered, skips = tied(gathered, skips)
         h2, pay2 = call(
             fine_second,
             [(vmem, ftile, F32), (vmem, (N_DP, 8, 128), F32)],
@@ -506,12 +504,14 @@
             pay2, own, cown = tied(pay2, own, cown)
         gathered2 = lax.all_to_all(pay2, "dp", 0, 0, tiled=True)
         if tick == 0:
-            cskips = lax.ppermute(tied(cpending, pay2)[0], "segment", to_encoder)
-            gathered2, upsampling, cskips = tied(gathered2, upsampling, cskips)
+            cskips = lax.ppermute(tied(cpending, pay)[0], "segment", to_encoder)
+            gathered2, skips = tied(gathered2, skips)
         else:
             added = ((pending,), (), (skips,))[tick - 1]
             kept = kept_after(tick - 1, (place, own, cown, mixing, cmixing), added, kept)
             gathered2, *kept = tied(gathered2, *kept)
+            if tick == 1:
+                gathered2, cskips = tied(gathered2, cskips)
             if tick == 2:
                 fresh = lax.ppermute(kept[3], "segment", to_encoder)
         own, cown = call(

time: 196 us -> 200 us (1.020)
  starting transfers between devices: 85.8 us -> 62.4 us
  blocking collectives: 0 us -> 16.3 us
  waiting for transfers between devices: 61.2 us -> 73.9 us
    all_to_all x0 -> x1, blocking collectives: none -> 16.3 us  [on_device(): gathered2 = lax.all_to_all(pay2, 'dp', 0, 0, tiled=True)]
    all_to_all x4, starting transfers between devices: 38.7 us -> 22.6 us  [on_device(): gathered = lax.all_to_all(pay, 'dp', 0, 0, tiled=True)]
    all_to_all x4, waiting for transfers between devices: 8.13 us -> 16.3 us  [on_device(): gathered = lax.all_to_all(pay, 'dp', 0, 0, tiled=True)]
    all_to_all x4 -> x3, starting transfers between devices: 23.8 us -> 17.8 us  [on_device(): gathered2 = lax.all_to_all(pay2, 'dp', 0, 0, tiled=True)]
    ppermute x1, waiting for transfers between devices: 10.6 us -> 6.76 us  [on_device(): cskips = lax.ppermute(tied(cpending, pay)[0], 'segment', to_encoder)]
    all_to_all x4 -> x3, waiting for transfers between devices: 8.64 us -> 11.5 us  [on_device(): gathered2 = lax.all_to_all(pay2, 'dp', 0, 0, tiled=True)]
    ppermute x1, waiting for transfers between devices: 10.1 us -> 12.3 us  [on_device(): fresh = lax.ppermute(kept[3], 'segment', to_encoder)]
    ppermute x3, starting transfers between devices: 3.89 us -> 1.73 us  [on_device(): carrived = lax.ppermute(going, 'segment', coarse_route)]
  transfers between devices with their start and end apart: 24 -> 23, of which waited for: 15 -> 18; matrix products, arithmetic and copies ran while one was open for 1% -> 1% of each run, Pallas kernels for 17% -> 17%
where the time goes in v3:
time: 200 us; the launch traced here: 199 us
  waiting for transfers between devices  73.9 us (37%)
  starting transfers between devices  62.4 us (31%)
  Pallas kernels  44 us (22%)
  blocking collectives  16.3 us (8%)
    pallas_call x23, Pallas kernels, call(): kernel(*[placed(spec, arg) for spec, arg in zip(in_specs, args, strict=Tr...  44 us
    all_to_all x4, starting transfers between devices, on_device(): gathered = lax.all_to_all(pay, 'dp', 0, 0, tiled=True)  22.6 us
    ppermute x3, waiting for transfers between devices, on_device(): carrived = lax.ppermute(going, 'segment', coarse_route)  18.7 us
    all_to_all x3, starting transfers between devices, on_device(): gathered2 = lax.all_to_all(pay2, 'dp', 0, 0, tiled=True)  17.8 us
    all_to_all x1, blocking collectives, on_device(): gathered2 = lax.all_to_all(pay2, 'dp', 0, 0, tiled=True)  16.3 us
    all_to_all x4, waiting for transfers between devices, on_device(): gathered = lax.all_to_all(pay, 'dp', 0, 0, tiled=True)  16.3 us
    ppermute x1, waiting for transfers between devices, on_device(): fresh = lax.ppermute(kept[3], 'segment', to_encoder)  12.3 us
    all_to_all x3, waiting for transfers between devices, on_device(): gathered2 = lax.all_to_all(pay2, 'dp', 0, 0, tiled=True)  11.5 us
  transfers between devices with their start and end apart: 23, of which 18 were waited for; matrix products, arithmetic and copies ran while one was open for 1% of the time, Pallas kernels for 17%

profile of v3, /device:TPU:32, one launch (start us, length us, event | category | flops | bytes accessed | tf_op | source)
XLA Modules:
  0.0 199.1 jit_solution(14819340291380366098)
XLA Ops:
  0.7 4.0 %shard_map.174 = (f32[256,256]{1,0:T(8,128)S(1)}, f32[32,4,128]{2,1,0:T(4,128)}, bf16[4,256,256]{2,1,0:T(8,128)(2,1)}, bf16[3,768,256]{2,1,0:T(8,128)(2,1)S(1)}, bf16[3,768,256]{2,1,0:T(8,128)(2,1)S(1)}) custom-call(s32[2]{0:T(128)S(1)} %pad_add_fusion.refs_0_.place, bf16[256,256]{1,0:T(8,128)(2,1)} %bitcast.86, bf16[6,256,256]{2,1,0:T(8,128)(2,1)} %bitcast.56, ...), custom_call_target="tpu_custom_call" | custom-call | flops 301989888 | bytes 1000000 | tf_op jit(solution)/shard_map/pallas_call | solution.py:40
  4.8 8.8 %collective-permute-start.1 = (bf16[4,256,256]{2,1,0:T(8,128)(2,1)}, bf16[4,256,256]{2,1,0:T(8,128)(2,1)}, u32[]{:S(2)}, u32[]{:S(2)}) collective-permute-start(bf16[4,256,256]{2,1,0:T(8,128)(2,1)} %get-tuple-element.104), channel_id=1, source_target_pairs={{0,128},{32,160},{64,192},{96,224},{1,129},{33,161},{65,193},{97,2... | collective-permute-start | bytes 1572872 | tf_op jit(solution)/shard_map/ppermute | solution.py:474
  13.5 7.0 %all-to-all-start = ((f32[32,4,128]{2,1,0:T(4,128)}), f32[32,4,128]{2,1,0:T(4,128)S(1)}, u32[]{:S(2)}, u32[]{:S(2)}) async-start(f32[32,4,128]{2,1,0:T(4,128)} %get-tuple-element.97), calls=%async_computation | async-start | bytes 131072 | tf_op jit(solution)/shard_map/all_to_all | solution.py:478
  20.6 3.7 %shard_map.175 = (f32[64,512]{1,0:T(8,128)S(1)}, f32[4,128]{1,0:T(4,128)S(1)}, f32[4,128]{1,0:T(4,128)S(1)}) custom-call(s32[2]{0:T(128)S(1)} %pad_add_fusion.refs_0_.place, bf16[64,512]{1,0:T(8,128)(2,1)} %bitcast.88, bf16[2,64,512]{2,1,0:T(8,128)(2,1)} %bitcast.83, bf16[512,512]{1,0:T(8,128)(2,1)} %bitcast.48, bf16[3,1536,512]{2,1,0:T(8,128)(2,1)} %bitcast.44), custom_call_target="tpu_custom_call" | custom-call | flops 301989888 | bytes 1500000 | tf_op jit(solution)/shard_map/pallas_call | solution.py:40
  25.5 10.9 %all-to-all-done.gathered = f32[32,4,128]{2,1,0:T(4,128)S(1)} async-done(((f32[32,4,128]{2,1,0:T(4,128)}), f32[32,4,128]{2,1,0:T(4,128)S(1)}, u32[]{:S(2)}, u32[]{:S(2)}) %all-to-all-start) | async-done | bytes 65568 | tf_op jit(solution)/shard_map/all_to_all | solution.py:478
  37.0 16.3 %all_to_all.40.gathered = f32[32,8,128]{2,1,0:T(8,128)S(1)} all-to-all(f32[32,8,128]{2,1,0:T(8,128)S(1)} %get-tuple-element.103), channel_id=1, replica_groups=mesh['segment'=8,'dp'=32] {'dp'}, dimensions={0} | all-to-all | bytes 262144 | tf_op jit(solution)/shard_map/all_to_all | solution.py:505
  53.5 3.4 %collective-permute-start.2 = (bf16[256,256]{1,0:T(8,128)(2,1)S(1)}, bf16[256,256]{1,0:T(8,128)(2,1)S(1)}, u32[]{:S(2)}, u32[]{:S(2)}) collective-permute-start(bf16[256,256]{1,0:T(8,128)(2,1)S(1)} %get-tuple-element.119.fine.refs_1_), channel_id=1, source_target_pairs={{0,32},{32,64},{64,96},{128,160},{160,192},{192,224},{1,33},{33,65... | collective-permute-start | bytes 393224 | tf_op jit(solution)/shard_map/ppermute | solution.py:527
  63.6 6.3 %collective-permute-done.4.refs_1_ = bf16[64,512]{1,0:T(8,128)(2,1)S(1)} collective-permute-done((bf16[64,512]{1,0:T(8,128)(2,1)S(1)}, bf16[64,512]{1,0:T(8,128)(2,1)S(1)}, u32[]{:S(2)}, u32[]{:S(2)}) %collective-permute-start.4) | collective-permute-done | bytes 65568 | tf_op jit(solution)/shard_map/ppermute | solution.py:541
  69.9 4.8 %all-to-all-start.2 = ((f32[32,4,128]{2,1,0:T(4,128)}), f32[32,4,128]{2,1,0:T(4,128)S(1)}, u32[]{:S(2)}, u32[]{:S(2)}) async-start(f32[32,4,128]{2,1,0:T(4,128)} %get-tuple-element.112), calls=%async_computation.2 | async-start | bytes 131072 | tf_op jit(solution)/shard_map/all_to_all | solution.py:478
  74.7 3.7 %shard_map.180 = (f32[64,512]{1,0:T(8,128)S(1)}, f32[4,128]{1,0:T(4,128)S(1)}, f32[4,128]{1,0:T(4,128)S(1)}) custom-call(s32[2]{0:T(128)S(1)} %pad_add_fusion.refs_0_.place, bf16[64,512]{1,0:T(8,128)(2,1)S(1)} %collective-permute-done.4.refs_1_, bf16[2,64,512]{2,1,0:T(8,128)(2,1)} %bitcast.84, bf16[512,512]{1,0:T(8,128)(2,1)} %bitcast.49, ...), custom_call_target="tpu_custom_call" | custom-call | flops 301989888 | bytes 1500000 | tf_op jit(solution)/shard_map/pallas_call | solution.py:40
  82.7 5.9 %all-to-all-start.3 = ((f32[32,8,128]{2,1,0:T(8,128)}), f32[32,8,128]{2,1,0:T(8,128)S(1)}, u32[]{:S(2)}, u32[]{:S(2)}) async-start(f32[32,8,128]{2,1,0:T(8,128)} %get-tuple-element.118), calls=%async_computation.3 | async-start | bytes 262144 | tf_op jit(solution)/shard_map/all_to_all | solution.py:505
  90.0 3.2 %shard_map.182 = (bf16[4,256,256]{2,1,0:T(8,128)(2,1)}, bf16[4,64,512]{2,1,0:T(8,128)(2,1)}, bf16[6,256,256]{2,1,0:T(8,128)(2,1)}, bf16[2,64,512]{2,1,0:T(8,128)(2,1)}) custom-call(s32[2]{0:T(128)S(1)} %pad_add_fusion.refs_0_.place, bf16[256,256]{1,0:T(8,128)(2,1)S(1)} %get-tuple-element.119.fine.refs_1_, ...), custom_call_target="tpu_custom_call" | custom-call | flops 40000000 | bytes 1000000 | tf_op jit(solution)/shard_map/pallas_call | solution.py:40
  96.1 6.8 %collective-permute-done.6.refs_2_ = bf16[2,64,512]{2,1,0:T(8,128)(2,1)S(1)} collective-permute-done((bf16[2,64,512]{2,1,0:T(8,128)(2,1)S(1)}, bf16[2,64,512]{2,1,0:T(8,128)(2,1)S(1)}, u32[]{:S(2)}, u32[]{:S(2)}) %collective-permute-start.6) | collective-permute-done | bytes 131104 | tf_op jit(solution)/shard_map/ppermute | solution.py:507
  110.2 5.8 %collective-permute-done.9.refs_1_ = bf16[64,512]{1,0:T(8,128)(2,1)S(1)} collective-permute-done((bf16[64,512]{1,0:T(8,128)(2,1)S(1)}, bf16[64,512]{1,0:T(8,128)(2,1)S(1)}, u32[]{:S(2)}, u32[]{:S(2)}) %collective-permute-start.9) | collective-permute-done | bytes 65568 | tf_op jit(solution)/shard_map/ppermute | solution.py:541
  116.0 6.6 %all-to-all-start.4 = ((f32[32,4,128]{2,1,0:T(4,128)}), f32[32,4,128]{2,1,0:T(4,128)S(1)}, u32[]{:S(2)}, u32[]{:S(2)}) async-start(f32[32,4,128]{2,1,0:T(4,128)} %get-tuple-element.133), calls=%async_computation.4 | async-start | bytes 131072 | tf_op jit(solution)/shard_map/all_to_all | solution.py:478
  122.7 3.7 %shard_map.186 = (f32[64,512]{1,0:T(8,128)S(1)}, f32[4,128]{1,0:T(4,128)S(1)}, f32[4,128]{1,0:T(4,128)S(1)}) custom-call(s32[2]{0:T(128)S(1)} %pad_add_fusion.refs_0_.place, bf16[64,512]{1,0:T(8,128)(2,1)S(1)} %collective-permute-done.9.refs_1_, bf16[2,64,512]{2,1,0:T(8,128)(2,1)} %copy-done.6, bf16[512,512]{1,0:T(8,128)(2,1)} %bitcast.51, ...), custom_call_target="tpu_custom_call" | custom-call | flops 301989888 | bytes 1500000 | tf_op jit(solution)/shard_map/pallas_call | solution.py:40
  130.7 5.9 %all-to-all-start.5 = ((f32[32,8,128]{2,1,0:T(8,128)}), f32[32,8,128]{2,1,0:T(8,128)S(1)}, u32[]{:S(2)}, u32[]{:S(2)}) async-start(f32[32,8,128]{2,1,0:T(8,128)} %get-tuple-element.140), calls=%async_computation.5 | async-start | bytes 262144 | tf_op jit(solution)/shard_map/all_to_all | solution.py:505
  139.0 5.0 %all-to-all-done.5.gathered = f32[32,8,128]{2,1,0:T(8,128)S(1)} async-done(((f32[32,8,128]{2,1,0:T(8,128)}), f32[32,8,128]{2,1,0:T(8,128)S(1)}, u32[]{:S(2)}, u32[]{:S(2)}) %all-to-all-start.5) | async-done | bytes 131104 | tf_op jit(solution)/shard_map/all_to_all | solution.py:505
  151.9 6.6 %collective-permute-done.13.refs_1_ = bf16[64,512]{1,0:T(8,128)(2,1)S(1)} collective-permute-done((bf16[64,512]{1,0:T(8,128)(2,1)S(1)}, bf16[64,512]{1,0:T(8,128)(2,1)S(1)}, u32[]{:S(2)}, u32[]{:S(2)}) %collective-permute-start.13) | collective-permute-done | bytes 65568 | tf_op jit(solution)/shard_map/ppermute | solution.py:541
  158.5 4.1 %all-to-all-start.6 = ((f32[32,4,128]{2,1,0:T(4,128)}), f32[32,4,128]{2,1,0:T(4,128)S(1)}, u32[]{:S(2)}, u32[]{:S(2)}) async-start(f32[32,4,128]{2,1,0:T(4,128)} %get-tuple-element.157), calls=%async_computation.6 | async-start | bytes 131072 | tf_op jit(solution)/shard_map/all_to_all | solution.py:478
  162.7 3.7 %shard_map.192 = (f32[64,512]{1,0:T(8,128)S(1)}, f32[4,128]{1,0:T(4,128)S(1)}, f32[4,128]{1,0:T(4,128)S(1)}) custom-call(s32[2]{0:T(128)S(1)} %pad_add_fusion.refs_0_.place, bf16[64,512]{1,0:T(8,128)(2,1)S(1)} %collective-permute-done.13.refs_1_, bf16[2,64,512]{2,1,0:T(8,128)(2,1)} %copy-done.6, bf16[512,512]{1,0:T(8,128)(2,1)} %bitcast.53, ...), custom_call_target="tpu_custom_call" | custom-call | flops 301989888 | bytes 1500000 | tf_op jit(solution)/shard_map/pallas_call | solution.py:40
  170.7 5.9 %all-to-all-start.7 = ((f32[32,8,128]{2,1,0:T(8,128)}), f32[32,8,128]{2,1,0:T(8,128)S(1)}, u32[]{:S(2)}, u32[]{:S(2)}) async-start(f32[32,8,128]{2,1,0:T(8,128)} %get-tuple-element.163), calls=%async_computation.7 | async-start | bytes 262144 | tf_op jit(solution)/shard_map/all_to_all | solution.py:505
  180.3 3.7 %all-to-all-done.7.gathered = f32[32,8,128]{2,1,0:T(8,128)S(1)} async-done(((f32[32,8,128]{2,1,0:T(8,128)}), f32[32,8,128]{2,1,0:T(8,128)S(1)}, u32[]{:S(2)}, u32[]{:S(2)}) %all-to-all-start.7) | async-done | bytes 131104 | tf_op jit(solution)/shard_map/all_to_all | solution.py:505
  184.2 12.3 %collective-permute-done.15.refs_5_ = bf16[2,64,512]{2,1,0:T(8,128)(2,1)S(1)} collective-permute-done((bf16[2,64,512]{2,1,0:T(8,128)(2,1)S(1)}, bf16[2,64,512]{2,1,0:T(8,128)(2,1)S(1)}, u32[]{:S(2)}, u32[]{:S(2)}) %collective-permute-start.15) | collective-permute-done | bytes 131104 | tf_op jit(solution)/shard_map/ppermute | solution.py:516
  (64 shorter events, 49.8 us)
Async XLA Ops:
  4.8 48.6 %collective-permute-start.1 = (bf16[4,256,256]{2,1,0:T(8,128)(2,1)}, bf16[4,256,256]{2,1,0:T(8,128)(2,1)}, u32[]{:S(2)}, u32[]{:S(2)}) collective-permute-start(bf16[4,256,256]{2,1,0:T(8,128)(2,1)} %get-tuple-element.104), channel_id=1, source_target_pairs={{0,128},{32,160},{64,192},{96,224},{1,129},{33,161},{65,193},{97,2... | collective-permute-start | bytes 1572872 | tf_op jit(solution)/shard_map/ppermute | solution.py:474
  13.5 22.9 %all-to-all-start = ((f32[32,4,128]{2,1,0:T(4,128)}), f32[32,4,128]{2,1,0:T(4,128)S(1)}, u32[]{:S(2)}, u32[]{:S(2)}) async-start(f32[32,4,128]{2,1,0:T(4,128)} %get-tuple-element.97), calls=%async_computation | async-start | bytes 131072 | tf_op jit(solution)/shard_map/all_to_all | solution.py:478
  20.6 32.8 %copy-start.2 = (f32[1,512]{1,0:T(1,128)S(1)}, f32[1,512]{1,0:T(1,128)}, u32[]{:S(2)}) copy-start(f32[1,512]{1,0:T(1,128)} %cgains.7) | copy-start | bytes 6148
  24.3 1.2 collective-permute-start
  53.5 7.4 %collective-permute-start.2 = (bf16[256,256]{1,0:T(8,128)(2,1)S(1)}, bf16[256,256]{1,0:T(8,128)(2,1)S(1)}, u32[]{:S(2)}, u32[]{:S(2)}) collective-permute-start(bf16[256,256]{1,0:T(8,128)(2,1)S(1)} %get-tuple-element.119.fine.refs_1_), channel_id=1, source_target_pairs={{0,32},{32,64},{64,96},{128,160},{160,192},{192,224},{1,33},{33,65... | collective-permute-start | bytes 393224 | tf_op jit(solution)/shard_map/ppermute | solution.py:527
  56.9 4.0 %collective-permute-start.3 = (bf16[64,512]{1,0:T(8,128)(2,1)S(1)}, bf16[64,512]{1,0:T(8,128)(2,1)S(1)}, u32[]{:S(2)}, u32[]{:S(2)}) collective-permute-start(bf16[64,512]{1,0:T(8,128)(2,1)S(1)} %get-tuple-element.120.coarse.refs_2_), channel_id=1, source_target_pairs={{96,128},{97,129},{98,130},{99,131},{100,132},{101,133},{102,134},... | collective-permute-start | bytes 196616 | tf_op jit(solution)/shard_map/ppermute | solution.py:526
  58.2 11.7 %collective-permute-start.4 = (bf16[64,512]{1,0:T(8,128)(2,1)S(1)}, bf16[64,512]{1,0:T(8,128)(2,1)S(1)}, u32[]{:S(2)}, u32[]{:S(2)}) collective-permute-start(bf16[64,512]{1,0:T(8,128)(2,1)S(1)} %shard_map.179), channel_id=1, source_target_pairs={{0,32},{32,64},{64,96},{96,128},{128,160},{160,192},{192,224},{224... | collective-permute-start | bytes 196616 | tf_op jit(solution)/shard_map/ppermute | solution.py:541
  69.9 11.5 %all-to-all-start.2 = ((f32[32,4,128]{2,1,0:T(4,128)}), f32[32,4,128]{2,1,0:T(4,128)S(1)}, u32[]{:S(2)}, u32[]{:S(2)}) async-start(f32[32,4,128]{2,1,0:T(4,128)} %get-tuple-element.112), calls=%async_computation.2 | async-start | bytes 131072 | tf_op jit(solution)/shard_map/all_to_all | solution.py:478
  78.4 1.2 collective-permute-start.5
  82.7 13.4 %all-to-all-start.3 = ((f32[32,8,128]{2,1,0:T(8,128)}), f32[32,8,128]{2,1,0:T(8,128)S(1)}, u32[]{:S(2)}, u32[]{:S(2)}) async-start(f32[32,8,128]{2,1,0:T(8,128)} %get-tuple-element.118), calls=%async_computation.3 | async-start | bytes 262144 | tf_op jit(solution)/shard_map/all_to_all | solution.py:505
  88.7 14.2 %collective-permute-start.6 = (bf16[2,64,512]{2,1,0:T(8,128)(2,1)S(1)}, bf16[2,64,512]{2,1,0:T(8,128)(2,1)S(1)}, u32[]{:S(2)}, u32[]{:S(2)}) collective-permute-start(bf16[2,64,512]{2,1,0:T(8,128)(2,1)S(1)} %bitcast.85), channel_id=1, source_target_pairs={{128,0},{160,32},{192,64},{224,96},{129,1},{161,33},{193,65},{225,... | collective-permute-start | bytes 393224 | tf_op jit(solution)/shard_map/ppermute | solution.py:507
  103.0 4.5 %collective-permute-start.7 = (bf16[256,256]{1,0:T(8,128)(2,1)S(1)}, bf16[256,256]{1,0:T(8,128)(2,1)S(1)}, u32[]{:S(2)}, u32[]{:S(2)}) collective-permute-start(bf16[256,256]{1,0:T(8,128)(2,1)S(1)} %get-tuple-element.141.fine.refs_1_), channel_id=1, source_target_pairs={{0,32},{32,64},{64,96},{128,160},{160,192},{192,224},{1,33},{33,65... | collective-permute-start | bytes 393224 | tf_op jit(solution)/shard_map/ppermute | solution.py:527
  104.3 1.3 collective-permute-start.8
  105.5 10.5 %collective-permute-start.9 = (bf16[64,512]{1,0:T(8,128)(2,1)S(1)}, bf16[64,512]{1,0:T(8,128)(2,1)S(1)}, u32[]{:S(2)}, u32[]{:S(2)}) collective-permute-start(bf16[64,512]{1,0:T(8,128)(2,1)S(1)} %shard_map.185), channel_id=1, source_target_pairs={{0,32},{32,64},{64,96},{96,128},{128,160},{160,192},{192,224},{224... | collective-permute-start | bytes 196616 | tf_op jit(solution)/shard_map/ppermute | solution.py:541
  116.0 13.4 %all-to-all-start.4 = ((f32[32,4,128]{2,1,0:T(4,128)}), f32[32,4,128]{2,1,0:T(4,128)S(1)}, u32[]{:S(2)}, u32[]{:S(2)}) async-start(f32[32,4,128]{2,1,0:T(4,128)} %get-tuple-element.133), calls=%async_computation.4 | async-start | bytes 131072 | tf_op jit(solution)/shard_map/all_to_all | solution.py:478
  126.3 1.2 collective-permute-start.10
  130.7 13.3 %all-to-all-start.5 = ((f32[32,8,128]{2,1,0:T(8,128)}), f32[32,8,128]{2,1,0:T(8,128)S(1)}, u32[]{:S(2)}, u32[]{:S(2)}) async-start(f32[32,8,128]{2,1,0:T(8,128)} %get-tuple-element.140), calls=%async_computation.5 | async-start | bytes 262144 | tf_op jit(solution)/shard_map/all_to_all | solution.py:505
  144.1 5.1 %collective-permute-start.11 = (bf16[256,256]{1,0:T(8,128)(2,1)S(1)}, bf16[256,256]{1,0:T(8,128)(2,1)S(1)}, u32[]{:S(2)}, u32[]{:S(2)}) collective-permute-start(bf16[256,256]{1,0:T(8,128)(2,1)S(1)} %get-tuple-element.164.fine.refs_1_), channel_id=1, source_target_pairs={{0,32},{32,64},{64,96},{128,160},{160,192},{192,224},{1,33},{33,65... | collective-permute-start | bytes 393224 | tf_op jit(solution)/shard_map/ppermute | solution.py:527
  145.5 1.3 collective-permute-start.12
  146.7 11.8 %collective-permute-start.13 = (bf16[64,512]{1,0:T(8,128)(2,1)S(1)}, bf16[64,512]{1,0:T(8,128)(2,1)S(1)}, u32[]{:S(2)}, u32[]{:S(2)}) collective-permute-start(bf16[64,512]{1,0:T(8,128)(2,1)S(1)} %shard_map.191), channel_id=1, source_target_pairs={{0,32},{32,64},{64,96},{96,128},{128,160},{160,192},{192,224},{224... | collective-permute-start | bytes 196616 | tf_op jit(solution)/shard_map/ppermute | solution.py:541
  158.5 10.9 %all-to-all-start.6 = ((f32[32,4,128]{2,1,0:T(4,128)}), f32[32,4,128]{2,1,0:T(4,128)S(1)}, u32[]{:S(2)}, u32[]{:S(2)}) async-start(f32[32,4,128]{2,1,0:T(4,128)} %get-tuple-element.157), calls=%async_computation.6 | async-start | bytes 131072 | tf_op jit(solution)/shard_map/all_to_all | solution.py:478
  166.3 1.2 collective-permute-start.14
  170.7 13.4 %all-to-all-start.7 = ((f32[32,8,128]{2,1,0:T(8,128)}), f32[32,8,128]{2,1,0:T(8,128)S(1)}, u32[]{:S(2)}, u32[]{:S(2)}) async-start(f32[32,8,128]{2,1,0:T(8,128)} %get-tuple-element.163), calls=%async_computation.7 | async-start | bytes 262144 | tf_op jit(solution)/shard_map/all_to_all | solution.py:505
  176.6 19.9 %collective-permute-start.15 = (bf16[2,64,512]{2,1,0:T(8,128)(2,1)S(1)}, bf16[2,64,512]{2,1,0:T(8,128)(2,1)S(1)}, u32[]{:S(2)}, u32[]{:S(2)}) collective-permute-start(bf16[2,64,512]{2,1,0:T(8,128)(2,1)S(1)} %copy-done.7), channel_id=1, source_target_pairs={{128,0},{160,32},{192,64},{224,96},{129,1},{161,33},{193,65},{225,... | collective-permute-start | bytes 393224 | tf_op jit(solution)/shard_map/ppermute | solution.py:516
  (7 other events, 118.5 us)

commit v4 on v2

--- a/solution.py
+++ b/solution.py
@@ -123,8 +123,8 @@
         refs = refs[8:]
     h_ref, pay_ref = refs[:2]
     if tick == 0:
-        packed, held, second = refs[2:5]
-        x_ref, padded, skip_ref, mix_ref, sems, staged, pack_sems = refs[5:]
+        parts, held, second = refs[2:6], refs[6], refs[7]
+        x_ref, padded, skip_ref, mix_ref, sems, staged, pack_sems = refs[8:]
     else:
         x_ref, padded, skip_ref, mix_ref, sems, spread_ref, up_ref, up_sems = refs[2:]
     segment = place[0]
@@ -156,7 +156,7 @@
         onward = pltpu.make_async_copy(kernels.at[1], second, pack_sems.at[5])
         onward.start()
         loads = [pltpu.make_async_copy(pending.at[slot], staged.at[slot], pack_sems.at[slot]) for slot in range(4)]
-        store = pltpu.make_async_copy(staged, packed, pack_sems.at[4])
+        stores = [pltpu.make_async_copy(staged.at[slot], parts[slot], pack_sems.at[slot]) for slot in range(4)]
 
         @pl.when(segment < HALF)
         def _():
@@ -198,9 +198,9 @@
 
         @pl.when(segment < HALF)
         def _():
-            for copy in loads:
-                copy.wait()
-            store.start()
+            for load, store in zip(loads, stores):
+                load.wait()
+                store.start()
 
     h = fine_convolution(x_ref[...].astype(F32), padded, kernel)
     h_ref[...] = h
@@ -212,7 +212,8 @@
 
         @pl.when(segment < HALF)
         def _():
-            store.wait()
+            for store in stores:
+                store.wait()
 
 
 def coarse_first(tick, *refs):
@@ -309,9 +310,9 @@
 
 
 def keep(tick, *refs):
-    place, fine, coarse, mixing, cmixing = refs[:5]
-    refs = refs[5:]
-    if tick != 1:
+    place, fine, coarse, got, mixing, cmixing = refs[:6]
+    refs = refs[6:]
+    if tick % 3 == 0:
         extra, refs = refs[0], refs[1:]
     fstash, cstash, fback, ctarget, term, cterm, mix_ref, cmix_ref, staged, sems = refs[(0, 4, 3, 4)[tick] :]
     segment = place[0]
@@ -344,18 +345,13 @@
     def _():
         fetch = pltpu.make_async_copy(cmixing, cmix_ref, sems.at[3])
         fetch.start()
-        if tick == 2:
-            received = pltpu.make_async_copy(extra, staged, sems.at[4])
-            received.start()
+        received = pltpu.make_async_copy(got, fback.at[2 + tick], sems.at[4])
+        received.start()
         fetch.wait()
         cterm[...] = dot(coarse[...], cmix_ref[...]).astype(BF16)
         copy = pltpu.make_async_copy(cterm, ctarget.at[tick % 2], sems.at[5])
         copy.start()
-        if tick == 2:
-            received.wait()
-            stored = pltpu.make_async_copy(staged, fback.at[2:6], sems.at[4])
-            stored.start()
-            stored.wait()
+        received.wait()
         copy.wait()
 
     if tick == 0:
@@ -379,13 +375,13 @@
     return call(
         functools.partial(keep, tick),
         stashes,
-        [SM, VM, VM, ANY, ANY] + [VM if tick == 3 else ANY] * len(added) + [ANY] * len(earlier),
+        [SM, VM, VM, VM, ANY, ANY] + [VM if tick == 3 else ANY] * len(added) + [ANY] * len(earlier),
         (
             pltpu.VMEM((CELLS, FCH), BF16),
             pltpu.VMEM((CCELLS, CCH), BF16),
             pltpu.VMEM((FCH, FCH), BF16),
             pltpu.VMEM((CCH, CCH), BF16),
-            pltpu.VMEM((4, CELLS, FCH), BF16),
+            pltpu.VMEM((2, CELLS, FCH), BF16),
             pltpu.SemaphoreType.DMA((6,)),
         ),
         40_000_000,
@@ -460,7 +456,7 @@
             )
         h1, pay, *handed = call(
             functools.partial(fine_first, tick),
-            [(vmem, ftile, F32), (vmem, (N_DP, 4, 128), F32)] + ([(hbm, (4, CELLS, FCH)), kernel_kept, kernel_kept] if tick == 0 else []),
+            [(vmem, ftile, F32), (vmem, (N_DP, 4, 128), F32)] + ([(hbm, ftile)] * 4 + [kernel_kept, kernel_kept] if tick == 0 else []),
             specs,
             (fine_bf, padded, fine_bf, pltpu.VMEM((FCH, FCH), BF16), pltpu.SemaphoreType.DMA((6,)), *more),
             conv_flops,
@@ -469,9 +465,8 @@
 
         if tick == 0:
             carrived = cinflow
-            packed, kernel_one, kernel_two = handed
+            *parts, kernel_one, kernel_two = handed
             pay, later = tied(pay, place)
-            skips = lax.ppermute(packed, "segment", to_decoder)
         else:
             pay, carrived = tied(pay, carrived)
             later = place
@@ -492,8 +487,6 @@
             1_500_000,
         )(later, carrived, cpending if tick < 2 else cskips, cmixing, ckernel)
         theirs = lax.ppermute(other, "dp", cores)
-        if tick == 2:
-            gathered, skips = tied(gathered, skips)
         h2, pay2 = call(
             fine_second,
             [(vmem, ftile, F32), (vmem, (N_DP, 8, 128), F32)],
@@ -504,16 +497,19 @@
         )(gathered, h1, gains, shifts, kernel_two, mine, theirs)
         if tick > 0:
             pay2, own, cown = tied(pay2, own, cown)
+        pay2, skip = tied(pay2, parts[tick])
         gathered2 = lax.all_to_all(pay2, "dp", 0, 0, tiled=True)
+        came = lax.ppermute(skip, "segment", to_decoder)
         if tick == 0:
             cskips = lax.ppermute(tied(cpending, pay2)[0], "segment", to_encoder)
-            gathered2, upsampling, cskips = tied(gathered2, upsampling, cskips)
+            gathered2, cskips = tied(gathered2, cskips)
         else:
-            added = ((pending,), (), (skips,))[tick - 1]
-            kept = kept_after(tick - 1, (place, own, cown, mixing, cmixing), added, kept)
+            added = (pending,) if tick == 1 else ()
+            kept = kept_after(tick - 1, (place, own, cown, got, mixing, cmixing), added, kept)
             gathered2, *kept = tied(gathered2, *kept)
             if tick == 2:
                 fresh = lax.ppermute(kept[3], "segment", to_encoder)
+        gathered2, got = tied(gathered2, came)
         own, cown = call(
             functools.partial(finish, tick),
             [(vmem, ftile), (vmem, ctile)],
@@ -540,7 +536,7 @@
             )(place, own, cown, descent)
             carrived = lax.ppermute(going, "segment", coarse_route)
     fstash, cstash, fback, cback = kept_after(
-        TICKS - 1, (place, own, cown, mixing, cmixing), (fresh,), kept
+        TICKS - 1, (place, own, cown, got, mixing, cmixing), (fresh,), kept
     )
     return (
         fstash.reshape(1, TICKS, 1, SIDE, SIDE, FCH),

time: 196 us -> 218 us (1.11); the launches traced: 195 us -> 215 us
  starting transfers between devices: 85.8 us -> 115 us
  waiting for transfers between devices: 61.2 us -> 49.7 us
    ppermute x1 -> x4, starting transfers between devices: 7.35 us -> 49.5 us  [on_device(): came = lax.ppermute(skip, 'segment', to_decoder)]
    all_to_all x4, starting transfers between devices: 38.7 us -> 28.3 us  [on_device(): gathered = lax.all_to_all(pay, 'dp', 0, 0, tiled=True)]
    all_to_all x4, waiting for transfers between devices: 8.64 us -> 0.01 us  [on_device(): gathered2 = lax.all_to_all(pay2, 'dp', 0, 0, tiled=True)]
    ppermute x1 -> x4, waiting for transfers between devices: 0.01 us -> 7.57 us  [on_device(): came = lax.ppermute(skip, 'segment', to_decoder)]
    ppermute x1, waiting for transfers between devices: 10.6 us -> 4.8 us  [on_device(): cskips = lax.ppermute(tied(cpending, pay2)[0], 'segment', to_encoder)]
    ppermute x1, waiting for transfers between devices: 10.1 us -> 5.89 us  [on_device(): fresh = lax.ppermute(kept[3], 'segment', to_encoder)]
    unnamed x14 -> x26, local copies, waits for them, and re-layouts: 0.04 us -> 2.49 us
  transfers between devices with their start and end apart: 24 -> 27, of which waited for: 15 -> 18; matrix products, arithmetic and copies ran while one was open for 1% -> 1% of each run, Pallas kernels for 17% -> 15%
where the time goes in v4:
time: 218 us; the launch traced here: 215 us
  starting transfers between devices  115 us (53%)
  waiting for transfers between devices  49.7 us (23%)
  Pallas kernels  44.7 us (21%)
  local copies, waits for them, and re-layouts  3.65 us (2%)
    ppermute x4, starting transfers between devices, on_device(): came = lax.ppermute(skip, 'segment', to_decoder)  49.5 us
    pallas_call x23, Pallas kernels, call(): kernel(*[placed(spec, arg) for spec, arg in zip(in_specs, args, strict=Tr...  44.7 us
    all_to_all x4, starting transfers between devices, on_device(): gathered = lax.all_to_all(pay, 'dp', 0, 0, tiled=True)  28.3 us
    all_to_all x4, starting transfers between devices, on_device(): gathered2 = lax.all_to_all(pay2, 'dp', 0, 0, tiled=True)  24.4 us
    ppermute x3, waiting for transfers between devices, on_device(): carrived = lax.ppermute(going, 'segment', coarse_route)  18.5 us
    ppermute x4, waiting for transfers between devices, on_device(): came = lax.ppermute(skip, 'segment', to_decoder)  7.57 us
    all_to_all x4, waiting for transfers between devices, on_device(): gathered = lax.all_to_all(pay, 'dp', 0, 0, tiled=True)  6.56 us
    ppermute x3, starting transfers between devices, on_device(): arrived = lax.ppermute(own, 'segment', fine_route)  6.13 us
  transfers between devices with their start and end apart: 27, of which 18 were waited for; matrix products, arithmetic and copies ran while one was open for 1% of the time, Pallas kernels for 15%

profile of v4, /device:TPU:32, one launch (start us, length us, event | category | flops | bytes accessed | tf_op | source)
XLA Modules:
  0.0 214.9 jit_solution(11394208168176282455)
XLA Ops:
  0.7 4.1 %shard_map.174 = (f32[256,256]{1,0:T(8,128)S(1)}, f32[32,4,128]{2,1,0:T(4,128)}, bf16[256,256]{1,0:T(8,128)(2,1)}, bf16[256,256]{1,0:T(8,128)(2,1)}, bf16[256,25...) custom-call(s32[2]{0:T(128)S(1)} %pad_add_fusion.refs_0_.place, ...), custom_call_target="tpu_custom_call" | custom-call | flops 301989888 | bytes 1000000 | tf_op jit(solution)/shard_map/pallas_call | solution.py:40
  4.8 8.8 %all-to-all-start = ((f32[32,4,128]{2,1,0:T(4,128)}), f32[32,4,128]{2,1,0:T(4,128)S(1)}, u32[]{:S(2)}, u32[]{:S(2)}) async-start(f32[32,4,128]{2,1,0:T(4,128)} %get-tuple-element.114), calls=%async_computation | async-start | bytes 131072 | tf_op jit(solution)/shard_map/all_to_all | solution.py:473
  13.6 3.7 %shard_map.175 = (f32[64,512]{1,0:T(8,128)S(1)}, f32[4,128]{1,0:T(4,128)S(1)}, f32[4,128]{1,0:T(4,128)S(1)}) custom-call(s32[2]{0:T(128)S(1)} %pad_add_fusion.refs_0_.place, bf16[64,512]{1,0:T(8,128)(2,1)} %bitcast.85, bf16[2,64,512]{2,1,0:T(8,128)(2,1)} %bitcast.9.refs_2_, bf16[512,512]{1,0:T(8,128)(2,1)} %bitcast.48, bf16[3,1536,512]{2,1,0:T(8,128)(2,1)} %bitcast.44), custom_call_target="tpu_custom_call" | custom-call | flops 301989888 | bytes 1500000 | tf_op jit(solution)/shard_map/pallas_call | solution.py:40
  21.6 6.0 %all-to-all-start.1 = ((f32[32,8,128]{2,1,0:T(8,128)}), f32[32,8,128]{2,1,0:T(8,128)S(1)}, u32[]{:S(2)}, u32[]{:S(2)}) async-start(f32[32,8,128]{2,1,0:T(8,128)} %get-tuple-element.122), calls=%async_computation.1 | async-start | bytes 262144 | tf_op jit(solution)/shard_map/all_to_all | solution.py:501
  28.9 8.5 %collective-permute-start.2 = (bf16[256,256]{1,0:T(8,128)(2,1)}, bf16[256,256]{1,0:T(8,128)(2,1)S(1)}, u32[]{:S(2)}, u32[]{:S(2)}) collective-permute-start(bf16[256,256]{1,0:T(8,128)(2,1)} %get-tuple-element.125), channel_id=1, source_target_pairs={{0,128},{32,160},{64,192},{96,224},{1,129},{33,161},{65,193},{97,2... | collective-permute-start | bytes 393224 | tf_op jit(solution)/shard_map/ppermute | solution.py:502
  37.4 4.8 %collective-permute-done.1.refs_2_ = bf16[2,64,512]{2,1,0:T(8,128)(2,1)S(1)} collective-permute-done((bf16[2,64,512]{2,1,0:T(8,128)(2,1)}, bf16[2,64,512]{2,1,0:T(8,128)(2,1)S(1)}, u32[]{:S(2)}, u32[]{:S(2)}) %collective-permute-start.1) | collective-permute-done | bytes 131104 | tf_op jit(solution)/shard_map/ppermute | solution.py:504
  42.4 3.5 %collective-permute-start.3 = (bf16[256,256]{1,0:T(8,128)(2,1)S(1)}, bf16[256,256]{1,0:T(8,128)(2,1)S(1)}, u32[]{:S(2)}, u32[]{:S(2)}) collective-permute-start(bf16[256,256]{1,0:T(8,128)(2,1)S(1)} %get-tuple-element.142.fine.refs_1_), channel_id=1, source_target_pairs={{0,32},{32,64},{64,96},{128,160},{160,192},{192,224},{1,33},{33,65... | collective-permute-start | bytes 393224 | tf_op jit(solution)/shard_map/ppermute | solution.py:523
  52.6 4.9 %collective-permute-done.5.refs_1_ = bf16[64,512]{1,0:T(8,128)(2,1)S(1)} collective-permute-done((bf16[64,512]{1,0:T(8,128)(2,1)S(1)}, bf16[64,512]{1,0:T(8,128)(2,1)S(1)}, u32[]{:S(2)}, u32[]{:S(2)}) %collective-permute-start.5) | collective-permute-done | bytes 65568 | tf_op jit(solution)/shard_map/ppermute | solution.py:537
  57.6 6.8 %all-to-all-start.2 = ((f32[32,4,128]{2,1,0:T(4,128)}), f32[32,4,128]{2,1,0:T(4,128)S(1)}, u32[]{:S(2)}, u32[]{:S(2)}) async-start(f32[32,4,128]{2,1,0:T(4,128)} %get-tuple-element.133), calls=%async_computation.2 | async-start | bytes 131072 | tf_op jit(solution)/shard_map/all_to_all | solution.py:473
  64.4 3.7 %shard_map.180 = (f32[64,512]{1,0:T(8,128)S(1)}, f32[4,128]{1,0:T(4,128)S(1)}, f32[4,128]{1,0:T(4,128)S(1)}) custom-call(s32[2]{0:T(128)S(1)} %pad_add_fusion.refs_0_.place, bf16[64,512]{1,0:T(8,128)(2,1)S(1)} %collective-permute-done.5.refs_1_, bf16[2,64,512]{2,1,0:T(8,128)(2,1)} %bitcast.9.refs_2_, bf16[512,512]{1,0:T(8,128)(2,1)} %bitcast.49, ...), custom_call_target="tpu_custom_call" | custom-call | flops 301989888 | bytes 1500000 | tf_op jit(solution)/shard_map/pallas_call | solution.py:40
  72.3 6.5 %all-to-all-start.3 = ((f32[32,8,128]{2,1,0:T(8,128)}), f32[32,8,128]{2,1,0:T(8,128)S(1)}, u32[]{:S(2)}, u32[]{:S(2)}) async-start(f32[32,8,128]{2,1,0:T(8,128)} %get-tuple-element.141), calls=%async_computation.3 | async-start | bytes 262144 | tf_op jit(solution)/shard_map/all_to_all | solution.py:501
  78.8 12.9 %collective-permute-start.7 = (bf16[256,256]{1,0:T(8,128)(2,1)S(1)}, bf16[256,256]{1,0:T(8,128)(2,1)S(1)}, u32[]{:S(2)}, u32[]{:S(2)}) collective-permute-start(bf16[256,256]{1,0:T(8,128)(2,1)S(1)} %copy-done.12), channel_id=1, source_target_pairs={{0,128},{32,160},{64,192},{96,224},{1,129},{33,161},{65,193},{97,2... | collective-permute-start | bytes 393224 | tf_op jit(solution)/shard_map/ppermute | solution.py:502
  105.2 7.2 %collective-permute-done.10.refs_1_ = bf16[64,512]{1,0:T(8,128)(2,1)S(1)} collective-permute-done((bf16[64,512]{1,0:T(8,128)(2,1)S(1)}, bf16[64,512]{1,0:T(8,128)(2,1)S(1)}, u32[]{:S(2)}, u32[]{:S(2)}) %collective-permute-start.10) | collective-permute-done | bytes 65568 | tf_op jit(solution)/shard_map/ppermute | solution.py:537
  112.4 6.0 %all-to-all-start.4 = ((f32[32,4,128]{2,1,0:T(4,128)}), f32[32,4,128]{2,1,0:T(4,128)S(1)}, u32[]{:S(2)}, u32[]{:S(2)}) async-start(f32[32,4,128]{2,1,0:T(4,128)} %get-tuple-element.157), calls=%async_computation.4 | async-start | bytes 131072 | tf_op jit(solution)/shard_map/all_to_all | solution.py:473
  118.4 3.7 %shard_map.186 = (f32[64,512]{1,0:T(8,128)S(1)}, f32[4,128]{1,0:T(4,128)S(1)}, f32[4,128]{1,0:T(4,128)S(1)}) custom-call(s32[2]{0:T(128)S(1)} %pad_add_fusion.refs_0_.place, bf16[64,512]{1,0:T(8,128)(2,1)S(1)} %collective-permute-done.10.refs_1_, bf16[2,64,512]{2,1,0:T(8,128)(2,1)} %copy-done.9, bf16[512,512]{1,0:T(8,128)(2,1)} %bitcast.51, ...), custom_call_target="tpu_custom_call" | custom-call | flops 301989888 | bytes 1500000 | tf_op jit(solution)/shard_map/pallas_call | solution.py:40
  126.4 5.9 %all-to-all-start.5 = ((f32[32,8,128]{2,1,0:T(8,128)}), f32[32,8,128]{2,1,0:T(8,128)S(1)}, u32[]{:S(2)}, u32[]{:S(2)}) async-start(f32[32,8,128]{2,1,0:T(8,128)} %get-tuple-element.166), calls=%async_computation.5 | async-start | bytes 262144 | tf_op jit(solution)/shard_map/all_to_all | solution.py:501
  132.3 14.1 %collective-permute-start.12 = (bf16[256,256]{1,0:T(8,128)(2,1)}, bf16[256,256]{1,0:T(8,128)(2,1)S(1)}, u32[]{:S(2)}, u32[]{:S(2)}) collective-permute-start(bf16[256,256]{1,0:T(8,128)(2,1)} %get-tuple-element.179), channel_id=1, source_target_pairs={{0,128},{32,160},{64,192},{96,224},{1,129},{33,161},{65,193},{97,2... | collective-permute-start | bytes 393224 | tf_op jit(solution)/shard_map/ppermute | solution.py:502
  148.9 3.7 %collective-permute-done.12.refs_3_ = bf16[256,256]{1,0:T(8,128)(2,1)S(1)} collective-permute-done((bf16[256,256]{1,0:T(8,128)(2,1)}, bf16[256,256]{1,0:T(8,128)(2,1)S(1)}, u32[]{:S(2)}, u32[]{:S(2)}) %collective-permute-start.12) | collective-permute-done | bytes 131104 | tf_op jit(solution)/shard_map/ppermute | solution.py:502
  159.3 6.4 %collective-permute-done.15.refs_1_ = bf16[64,512]{1,0:T(8,128)(2,1)S(1)} collective-permute-done((bf16[64,512]{1,0:T(8,128)(2,1)S(1)}, bf16[64,512]{1,0:T(8,128)(2,1)S(1)}, u32[]{:S(2)}, u32[]{:S(2)}) %collective-permute-start.15) | collective-permute-done | bytes 65568 | tf_op jit(solution)/shard_map/ppermute | solution.py:537
  165.7 6.8 %all-to-all-start.6 = ((f32[32,4,128]{2,1,0:T(4,128)}), f32[32,4,128]{2,1,0:T(4,128)S(1)}, u32[]{:S(2)}, u32[]{:S(2)}) async-start(f32[32,4,128]{2,1,0:T(4,128)} %get-tuple-element.186), calls=%async_computation.6 | async-start | bytes 131072 | tf_op jit(solution)/shard_map/all_to_all | solution.py:473
  172.4 3.7 %shard_map.192 = (f32[64,512]{1,0:T(8,128)S(1)}, f32[4,128]{1,0:T(4,128)S(1)}, f32[4,128]{1,0:T(4,128)S(1)}) custom-call(s32[2]{0:T(128)S(1)} %pad_add_fusion.refs_0_.place, bf16[64,512]{1,0:T(8,128)(2,1)S(1)} %collective-permute-done.15.refs_1_, bf16[2,64,512]{2,1,0:T(8,128)(2,1)} %copy-done.9, bf16[512,512]{1,0:T(8,128)(2,1)} %bitcast.53, ...), custom_call_target="tpu_custom_call" | custom-call | flops 301989888 | bytes 1500000 | tf_op jit(solution)/shard_map/pallas_call | solution.py:40
  180.4 5.9 %all-to-all-start.7 = ((f32[32,8,128]{2,1,0:T(8,128)}), f32[32,8,128]{2,1,0:T(8,128)S(1)}, u32[]{:S(2)}, u32[]{:S(2)}) async-start(f32[32,8,128]{2,1,0:T(8,128)} %get-tuple-element.194), calls=%async_computation.7 | async-start | bytes 262144 | tf_op jit(solution)/shard_map/all_to_all | solution.py:501
  186.4 14.0 %collective-permute-start.17 = (bf16[256,256]{1,0:T(8,128)(2,1)S(1)}, bf16[256,256]{1,0:T(8,128)(2,1)S(1)}, u32[]{:S(2)}, u32[]{:S(2)}) collective-permute-start(bf16[256,256]{1,0:T(8,128)(2,1)S(1)} %copy-done.11), channel_id=1, source_target_pairs={{0,128},{32,160},{64,192},{96,224},{1,129},{33,161},{65,193},{97,2... | collective-permute-start | bytes 393224 | tf_op jit(solution)/shard_map/ppermute | solution.py:502
  206.4 5.9 %collective-permute-done.18.refs_6_ = bf16[2,64,512]{2,1,0:T(8,128)(2,1)S(1)} collective-permute-done((bf16[2,64,512]{2,1,0:T(8,128)(2,1)S(1)}, bf16[2,64,512]{2,1,0:T(8,128)(2,1)S(1)}, u32[]{:S(2)}, u32[]{:S(2)}) %collective-permute-start.18) | collective-permute-done | bytes 131104 | tf_op jit(solution)/shard_map/ppermute | solution.py:511
  (81 shorter events, 56.3 us)
Async XLA Ops:
  4.8 15.5 %all-to-all-start = ((f32[32,4,128]{2,1,0:T(4,128)}), f32[32,4,128]{2,1,0:T(4,128)S(1)}, u32[]{:S(2)}, u32[]{:S(2)}) async-start(f32[32,4,128]{2,1,0:T(4,128)} %get-tuple-element.114), calls=%async_computation | async-start | bytes 131072 | tf_op jit(solution)/shard_map/all_to_all | solution.py:473
  17.3 1.2 collective-permute-start
  21.6 20.6 %all-to-all-start.1 = ((f32[32,8,128]{2,1,0:T(8,128)}), f32[32,8,128]{2,1,0:T(8,128)S(1)}, u32[]{:S(2)}, u32[]{:S(2)}) async-start(f32[32,8,128]{2,1,0:T(8,128)} %get-tuple-element.122), calls=%async_computation.1 | async-start | bytes 262144 | tf_op jit(solution)/shard_map/all_to_all | solution.py:501
  27.6 14.6 %collective-permute-start.1 = (bf16[2,64,512]{2,1,0:T(8,128)(2,1)}, bf16[2,64,512]{2,1,0:T(8,128)(2,1)S(1)}, u32[]{:S(2)}, u32[]{:S(2)}) collective-permute-start(bf16[2,64,512]{2,1,0:T(8,128)(2,1)} %bitcast.9.refs_2_), channel_id=1, source_target_pairs={{128,0},{160,32},{192,64},{224,96},{129,1},{161,33},{193,65},{225,... | collective-permute-start | bytes 393224 | tf_op jit(solution)/shard_map/ppermute | solution.py:504
  28.9 13.3 %collective-permute-start.2 = (bf16[256,256]{1,0:T(8,128)(2,1)}, bf16[256,256]{1,0:T(8,128)(2,1)S(1)}, u32[]{:S(2)}, u32[]{:S(2)}) collective-permute-start(bf16[256,256]{1,0:T(8,128)(2,1)} %get-tuple-element.125), channel_id=1, source_target_pairs={{0,128},{32,160},{64,192},{96,224},{1,129},{33,161},{65,193},{97,2... | collective-permute-start | bytes 393224 | tf_op jit(solution)/shard_map/ppermute | solution.py:502
  42.4 7.5 %collective-permute-start.3 = (bf16[256,256]{1,0:T(8,128)(2,1)S(1)}, bf16[256,256]{1,0:T(8,128)(2,1)S(1)}, u32[]{:S(2)}, u32[]{:S(2)}) collective-permute-start(bf16[256,256]{1,0:T(8,128)(2,1)S(1)} %get-tuple-element.142.fine.refs_1_), channel_id=1, source_target_pairs={{0,32},{32,64},{64,96},{128,160},{160,192},{192,224},{1,33},{33,65... | collective-permute-start | bytes 393224 | tf_op jit(solution)/shard_map/ppermute | solution.py:523
  45.9 4.0 %collective-permute-start.4 = (bf16[64,512]{1,0:T(8,128)(2,1)S(1)}, bf16[64,512]{1,0:T(8,128)(2,1)S(1)}, u32[]{:S(2)}, u32[]{:S(2)}) collective-permute-start(bf16[64,512]{1,0:T(8,128)(2,1)S(1)} %get-tuple-element.143.coarse.refs_2_), channel_id=1, source_target_pairs={{96,128},{97,129},{98,130},{99,131},{100,132},{101,133},{102,134},... | collective-permute-start | bytes 196616 | tf_op jit(solution)/shard_map/ppermute | solution.py:522
  47.2 10.4 %collective-permute-start.5 = (bf16[64,512]{1,0:T(8,128)(2,1)S(1)}, bf16[64,512]{1,0:T(8,128)(2,1)S(1)}, u32[]{:S(2)}, u32[]{:S(2)}) collective-permute-start(bf16[64,512]{1,0:T(8,128)(2,1)S(1)} %shard_map.179), channel_id=1, source_target_pairs={{0,32},{32,64},{64,96},{96,128},{128,160},{160,192},{192,224},{224... | collective-permute-start | bytes 196616 | tf_op jit(solution)/shard_map/ppermute | solution.py:537
  57.6 13.5 %all-to-all-start.2 = ((f32[32,4,128]{2,1,0:T(4,128)}), f32[32,4,128]{2,1,0:T(4,128)S(1)}, u32[]{:S(2)}, u32[]{:S(2)}) async-start(f32[32,4,128]{2,1,0:T(4,128)} %get-tuple-element.133), calls=%async_computation.2 | async-start | bytes 131072 | tf_op jit(solution)/shard_map/all_to_all | solution.py:473
  72.3 23.6 %all-to-all-start.3 = ((f32[32,8,128]{2,1,0:T(8,128)}), f32[32,8,128]{2,1,0:T(8,128)S(1)}, u32[]{:S(2)}, u32[]{:S(2)}) async-start(f32[32,8,128]{2,1,0:T(8,128)} %get-tuple-element.141), calls=%async_computation.3 | async-start | bytes 262144 | tf_op jit(solution)/shard_map/all_to_all | solution.py:501
  78.8 18.8 %collective-permute-start.7 = (bf16[256,256]{1,0:T(8,128)(2,1)S(1)}, bf16[256,256]{1,0:T(8,128)(2,1)S(1)}, u32[]{:S(2)}, u32[]{:S(2)}) collective-permute-start(bf16[256,256]{1,0:T(8,128)(2,1)S(1)} %copy-done.12), channel_id=1, source_target_pairs={{0,128},{32,160},{64,192},{96,224},{1,129},{33,161},{65,193},{97,2... | collective-permute-start | bytes 393224 | tf_op jit(solution)/shard_map/ppermute | solution.py:502
  98.7 3.8 %collective-permute-start.8 = (bf16[256,256]{1,0:T(8,128)(2,1)S(1)}, bf16[256,256]{1,0:T(8,128)(2,1)S(1)}, u32[]{:S(2)}, u32[]{:S(2)}) collective-permute-start(bf16[256,256]{1,0:T(8,128)(2,1)S(1)} %get-tuple-element.167.fine.refs_1_), channel_id=1, source_target_pairs={{0,32},{32,64},{64,96},{128,160},{160,192},{192,224},{1,33},{33,65... | collective-permute-start | bytes 393224 | tf_op jit(solution)/shard_map/ppermute | solution.py:523
  100.0 1.3 collective-permute-start.9
  101.3 11.2 %collective-permute-start.10 = (bf16[64,512]{1,0:T(8,128)(2,1)S(1)}, bf16[64,512]{1,0:T(8,128)(2,1)S(1)}, u32[]{:S(2)}, u32[]{:S(2)}) collective-permute-start(bf16[64,512]{1,0:T(8,128)(2,1)S(1)} %shard_map.185), channel_id=1, source_target_pairs={{0,32},{32,64},{64,96},{96,128},{128,160},{160,192},{192,224},{224... | collective-permute-start | bytes 196616 | tf_op jit(solution)/shard_map/ppermute | solution.py:537
  112.4 12.7 %all-to-all-start.4 = ((f32[32,4,128]{2,1,0:T(4,128)}), f32[32,4,128]{2,1,0:T(4,128)S(1)}, u32[]{:S(2)}, u32[]{:S(2)}) async-start(f32[32,4,128]{2,1,0:T(4,128)} %get-tuple-element.157), calls=%async_computation.4 | async-start | bytes 131072 | tf_op jit(solution)/shard_map/all_to_all | solution.py:473
  126.4 22.5 %all-to-all-start.5 = ((f32[32,8,128]{2,1,0:T(8,128)}), f32[32,8,128]{2,1,0:T(8,128)S(1)}, u32[]{:S(2)}, u32[]{:S(2)}) async-start(f32[32,8,128]{2,1,0:T(8,128)} %get-tuple-element.166), calls=%async_computation.5 | async-start | bytes 262144 | tf_op jit(solution)/shard_map/all_to_all | solution.py:501
  132.3 20.3 %collective-permute-start.12 = (bf16[256,256]{1,0:T(8,128)(2,1)}, bf16[256,256]{1,0:T(8,128)(2,1)S(1)}, u32[]{:S(2)}, u32[]{:S(2)}) collective-permute-start(bf16[256,256]{1,0:T(8,128)(2,1)} %get-tuple-element.179), channel_id=1, source_target_pairs={{0,128},{32,160},{64,192},{96,224},{1,129},{33,161},{65,193},{97,2... | collective-permute-start | bytes 393224 | tf_op jit(solution)/shard_map/ppermute | solution.py:502
  152.7 3.8 %collective-permute-start.13 = (bf16[256,256]{1,0:T(8,128)(2,1)S(1)}, bf16[256,256]{1,0:T(8,128)(2,1)S(1)}, u32[]{:S(2)}, u32[]{:S(2)}) collective-permute-start(bf16[256,256]{1,0:T(8,128)(2,1)S(1)} %get-tuple-element.195.fine.refs_1_), channel_id=1, source_target_pairs={{0,32},{32,64},{64,96},{128,160},{160,192},{192,224},{1,33},{33,65... | collective-permute-start | bytes 393224 | tf_op jit(solution)/shard_map/ppermute | solution.py:523
  154.0 1.3 collective-permute-start.14
  155.3 10.4 %collective-permute-start.15 = (bf16[64,512]{1,0:T(8,128)(2,1)S(1)}, bf16[64,512]{1,0:T(8,128)(2,1)S(1)}, u32[]{:S(2)}, u32[]{:S(2)}) collective-permute-start(bf16[64,512]{1,0:T(8,128)(2,1)S(1)} %shard_map.191), channel_id=1, source_target_pairs={{0,32},{32,64},{64,96},{96,128},{128,160},{160,192},{192,224},{224... | collective-permute-start | bytes 196616 | tf_op jit(solution)/shard_map/ppermute | solution.py:537
  165.7 13.5 %all-to-all-start.6 = ((f32[32,4,128]{2,1,0:T(4,128)}), f32[32,4,128]{2,1,0:T(4,128)S(1)}, u32[]{:S(2)}, u32[]{:S(2)}) async-start(f32[32,4,128]{2,1,0:T(4,128)} %get-tuple-element.186), calls=%async_computation.6 | async-start | bytes 131072 | tf_op jit(solution)/shard_map/all_to_all | solution.py:473
  180.4 23.7 %all-to-all-start.7 = ((f32[32,8,128]{2,1,0:T(8,128)}), f32[32,8,128]{2,1,0:T(8,128)S(1)}, u32[]{:S(2)}, u32[]{:S(2)}) async-start(f32[32,8,128]{2,1,0:T(8,128)} %get-tuple-element.194), calls=%async_computation.7 | async-start | bytes 262144 | tf_op jit(solution)/shard_map/all_to_all | solution.py:501
  186.4 19.9 %collective-permute-start.17 = (bf16[256,256]{1,0:T(8,128)(2,1)S(1)}, bf16[256,256]{1,0:T(8,128)(2,1)S(1)}, u32[]{:S(2)}, u32[]{:S(2)}) collective-permute-start(bf16[256,256]{1,0:T(8,128)(2,1)S(1)} %copy-done.11), channel_id=1, source_target_pairs={{0,128},{32,160},{64,192},{96,224},{1,129},{33,161},{65,193},{97,2... | collective-permute-start | bytes 393224 | tf_op jit(solution)/shard_map/ppermute | solution.py:502
  200.4 11.9 %collective-permute-start.18 = (bf16[2,64,512]{2,1,0:T(8,128)(2,1)S(1)}, bf16[2,64,512]{2,1,0:T(8,128)(2,1)S(1)}, u32[]{:S(2)}, u32[]{:S(2)}) collective-permute-start(bf16[2,64,512]{2,1,0:T(8,128)(2,1)S(1)} %copy-done.10), channel_id=1, source_target_pairs={{128,0},{160,32},{192,64},{224,96},{129,1},{161,33},{193,65},{225,... | collective-permute-start | bytes 393224 | tf_op jit(solution)/shard_map/ppermute | solution.py:511
  (16 other events, 151.8 us)

commit v5 on v2

--- a/solution.py
+++ b/solution.py
@@ -123,16 +123,18 @@
         refs = refs[8:]
     h_ref, pay_ref = refs[:2]
     if tick == 0:
-        packed, held, second = refs[2:5]
-        x_ref, padded, skip_ref, mix_ref, sems, staged, pack_sems = refs[5:]
+        packed, held, second, mix_ref = refs[2:6]
+        x_ref, padded, skip_ref, sems, staged, pack_sems = refs[6:]
     else:
-        x_ref, padded, skip_ref, mix_ref, sems, spread_ref, up_ref, up_sems = refs[2:]
+        x_ref, padded, skip_ref, sems, spread_ref, up_ref, up_sems = refs[2:]
+        mix_ref = mixing
     segment = place[0]
     kernel = Streamed(kernels.at[0], held, sems.at[pl.ds(0, 3)]) if tick == 0 else kernels
     skip = pltpu.make_async_copy(pending.at[tick], skip_ref, sems.at[3])
-    mix = pltpu.make_async_copy(mixing, mix_ref, sems.at[4])
-
-    if tick == 0:
+
+    if tick == 0:
+        mix = pltpu.make_async_copy(mixing, mix_ref, sems.at[4])
+        mix.start()
         x = pltpu.make_async_copy(inflow, x_ref, sems.at[5])
         x.start()
     else:
@@ -148,7 +150,6 @@
 
     @pl.when(segment >= HALF)
     def _():
-        mix.start()
         skip.start()
 
     if tick == 0:
@@ -188,10 +189,12 @@
             for p in range(FCH // 128):
                 x_ref[:, p * 128 : (p + 1) * 128] = spread_ref[p].astype(BF16)
 
+    if tick == 0:
+        mix.wait()
+
     @pl.when(segment >= HALF)
     def _():
         skip.wait()
-        mix.wait()
         x_ref[...] = (dot(x_ref[...], mix_ref[...]) + skip_ref[...].astype(F32)).astype(BF16)
 
     if tick == 0:
@@ -311,7 +314,7 @@
 def keep(tick, *refs):
     place, fine, coarse, mixing, cmixing = refs[:5]
     refs = refs[5:]
-    if tick != 1:
+    if tick in (0, 2):
         extra, refs = refs[0], refs[1:]
     fstash, cstash, fback, ctarget, term, cterm, mix_ref, cmix_ref, staged, sems = refs[(0, 4, 3, 4)[tick] :]
     segment = place[0]
@@ -329,15 +332,10 @@
     def _():
         fetch = pltpu.make_async_copy(mixing, mix_ref, sems.at[3])
         fetch.start()
-        if tick == 3:
-            ccopy = pltpu.make_async_copy(extra, ctarget, sems.at[5])
-            ccopy.start()
         fetch.wait()
         term[...] = dot(fine[...], mix_ref[...]).astype(BF16)
         copy = pltpu.make_async_copy(term, fback.at[2 + tick], sems.at[4])
         copy.start()
-        if tick == 3:
-            ccopy.wait()
         copy.wait()
 
     @pl.when(segment >= HALF)
@@ -367,6 +365,14 @@
         copy.wait()
 
 
+def settle(place, received, _, target, sem):
+    @pl.when(place[0] < HALF)
+    def _():
+        copy = pltpu.make_async_copy(received, target, sem)
+        copy.start()
+        copy.wait()
+
+
 def kept_after(tick, common, added, kept):
     stashes = [
         (pltpu.HBM, (TICKS, CELLS, FCH)),
@@ -379,7 +385,7 @@
     return call(
         functools.partial(keep, tick),
         stashes,
-        [SM, VM, VM, ANY, ANY] + [VM if tick == 3 else ANY] * len(added) + [ANY] * len(earlier),
+        [SM, VM, VM, ANY, ANY] + [ANY] * (len(added) + len(earlier)),
         (
             pltpu.VMEM((CELLS, FCH), BF16),
             pltpu.VMEM((CCELLS, CCH), BF16),
@@ -451,8 +457,8 @@
             sources, specs = (inflow, pending, mixing, kernels), [SM, ANY, ANY, ANY, ANY]
             more = (pltpu.VMEM((4, CELLS, FCH), BF16), pltpu.SemaphoreType.DMA((6,)))
         else:
-            sources = (arrived, raised, entries, upsampling, pending, mixing, kernel_one)
-            specs = [SM, VM, VM, ANY, ANY, ANY, ANY, VM]
+            sources = (arrived, raised, entries, upsampling, pending, near_mixing, kernel_one)
+            specs = [SM, VM, VM, ANY, ANY, ANY, VM, VM]
             more = (
                 pltpu.VMEM((2, CELLS, 128), F32),
                 pltpu.VMEM((4, CCH, FCH), BF16),
@@ -460,16 +466,16 @@
             )
         h1, pay, *handed = call(
             functools.partial(fine_first, tick),
-            [(vmem, ftile, F32), (vmem, (N_DP, 4, 128), F32)] + ([(hbm, (4, CELLS, FCH)), kernel_kept, kernel_kept] if tick == 0 else []),
+            [(vmem, ftile, F32), (vmem, (N_DP, 4, 128), F32)] + ([(hbm, (4, CELLS, FCH)), kernel_kept, kernel_kept, (vmem, (FCH, FCH))] if tick == 0 else []),
             specs,
-            (fine_bf, padded, fine_bf, pltpu.VMEM((FCH, FCH), BF16), pltpu.SemaphoreType.DMA((6,)), *more),
+            (fine_bf, padded, fine_bf, pltpu.SemaphoreType.DMA((6,)), *more),
             conv_flops,
             1_000_000,
         )(place, *sources)
 
         if tick == 0:
             carrived = cinflow
-            packed, kernel_one, kernel_two = handed
+            packed, kernel_one, kernel_two, near_mixing = handed
             pay, later = tied(pay, place)
             skips = lax.ppermute(packed, "segment", to_decoder)
         else:
@@ -507,7 +513,7 @@
         gathered2 = lax.all_to_all(pay2, "dp", 0, 0, tiled=True)
         if tick == 0:
             cskips = lax.ppermute(tied(cpending, pay2)[0], "segment", to_encoder)
-            gathered2, upsampling, cskips = tied(gathered2, upsampling, cskips)
+            gathered2, cskips = tied(gathered2, cskips)
         else:
             added = ((pending,), (), (skips,))[tick - 1]
             kept = kept_after(tick - 1, (place, own, cown, mixing, cmixing), added, kept)
@@ -540,8 +546,17 @@
             )(place, own, cown, descent)
             carrived = lax.ppermute(going, "segment", coarse_route)
     fstash, cstash, fback, cback = kept_after(
-        TICKS - 1, (place, own, cown, mixing, cmixing), (fresh,), kept
+        TICKS - 1, (place, own, cown, mixing, cmixing), (), kept
     )
+    (cback,) = call(
+        settle,
+        [(hbm, (2, CCELLS, CCH))],
+        [SM, VM, ANY],
+        (pltpu.SemaphoreType.DMA,),
+        0,
+        300_000,
+        {2: 0},
+    )(place, fresh, cback)
     return (
         fstash.reshape(1, TICKS, 1, SIDE, SIDE, FCH),
         cstash.reshape(1, TICKS, 1, CSIDE, CSIDE, CCH),

time: 196 us -> 197 us (level)
  waiting for transfers between devices: 61.2 us -> 58.9 us
  starting transfers between devices: 85.8 us -> 88 us
    ppermute x1, waiting for transfers between devices: 10.1 us -> 7.66 us  [on_device(): fresh = lax.ppermute(kept[3], 'segment', to_encoder)]
    ppermute x1, waiting for transfers between devices: 10.6 us -> 13 us  [on_device(): cskips = lax.ppermute(tied(cpending, pay2)[0], 'segment', to_encoder)]
    ppermute x3, waiting for transfers between devices: 18.2 us -> 15.9 us  [on_device(): carrived = lax.ppermute(going, 'segment', coarse_route)]
    pallas_call x23 -> x24, Pallas kernels: 44.8 us -> 46 us  [call(): kernel(*[placed(spec, arg) for spec, arg in zip(in_specs, args, strict=Tr...]
  transfers between devices with their start and end apart: 24 -> 24, of which waited for: 15 -> 15; matrix products, arithmetic and copies ran while one was open for 1% -> 1% of each run, Pallas kernels for 17% -> 18%
where the time goes in v5:
time: 197 us; the launch traced here: 196 us
  starting transfers between devices  88 us (45%)
  waiting for transfers between devices  58.9 us (30%)
  Pallas kernels  46 us (23%)
    pallas_call x24, Pallas kernels, call(): kernel(*[placed(spec, arg) for spec, arg in zip(in_specs, args, strict=Tr...  46 us
    all_to_all x4, starting transfers between devices, on_device(): gathered = lax.all_to_all(pay, 'dp', 0, 0, tiled=True)  39.8 us
    all_to_all x4, starting transfers between devices, on_device(): gathered2 = lax.all_to_all(pay2, 'dp', 0, 0, tiled=True)  23.8 us
    ppermute x3, waiting for transfers between devices, on_device(): carrived = lax.ppermute(going, 'segment', coarse_route)  15.9 us
    ppermute x1, waiting for transfers between devices, on_device(): cskips = lax.ppermute(tied(cpending, pay2)[0], 'segment', to_encoder)  13 us
    all_to_all x4, waiting for transfers between devices, on_device(): gathered2 = lax.all_to_all(pay2, 'dp', 0, 0, tiled=True)  8.65 us
    all_to_all x4, waiting for transfers between devices, on_device(): gathered = lax.all_to_all(pay, 'dp', 0, 0, tiled=True)  8.12 us
    ppermute x1, waiting for transfers between devices, on_device(): fresh = lax.ppermute(kept[3], 'segment', to_encoder)  7.66 us
  transfers between devices with their start and end apart: 24, of which 15 were waited for; matrix products, arithmetic and copies ran while one was open for 1% of the time, Pallas kernels for 18%

profile of v5, /device:TPU:32, one launch (start us, length us, event | category | flops | bytes accessed | tf_op | source)
XLA Modules:
  0.0 196.0 jit_solution(14193982635063991444)
XLA Ops:
  0.7 4.1 %shard_map.174 = (f32[256,256]{1,0:T(8,128)S(1)}, f32[32,4,128]{2,1,0:T(4,128)}, bf16[4,256,256]{2,1,0:T(8,128)(2,1)}, bf16[3,768,256]{2,1,0:T(8,128)(2,1)S(1)},...) custom-call(s32[2]{0:T(128)S(1)} %pad_add_fusion.refs_0_.place, bf16[256,256]{1,0:T(8,128)(2,1)} %bitcast.84, ...), custom_call_target="tpu_custom_call" | custom-call | flops 301989888 | bytes 1000000 | tf_op jit(solution)/shard_map/pallas_call | solution.py:40
  4.8 8.8 %all-to-all-start = ((f32[32,4,128]{2,1,0:T(4,128)}), f32[32,4,128]{2,1,0:T(4,128)S(1)}, u32[]{:S(2)}, u32[]{:S(2)}) async-start(f32[32,4,128]{2,1,0:T(4,128)} %get-tuple-element.98), calls=%async_computation | async-start | bytes 131072 | tf_op jit(solution)/shard_map/all_to_all | solution.py:484
  13.7 3.7 %shard_map.175 = (f32[64,512]{1,0:T(8,128)S(1)}, f32[4,128]{1,0:T(4,128)S(1)}, f32[4,128]{1,0:T(4,128)S(1)}) custom-call(s32[2]{0:T(128)S(1)} %pad_add_fusion.refs_0_.place, bf16[64,512]{1,0:T(8,128)(2,1)} %bitcast.85, bf16[2,64,512]{2,1,0:T(8,128)(2,1)} %bitcast.80, bf16[512,512]{1,0:T(8,128)(2,1)} %bitcast.48, bf16[3,1536,512]{2,1,0:T(8,128)(2,1)} %bitcast.44), custom_call_target="tpu_custom_call" | custom-call | flops 301989888 | bytes 1500000 | tf_op jit(solution)/shard_map/pallas_call | solution.py:40
  21.7 6.0 %all-to-all-start.1 = ((f32[32,8,128]{2,1,0:T(8,128)}), f32[32,8,128]{2,1,0:T(8,128)S(1)}, u32[]{:S(2)}, u32[]{:S(2)}) async-start(f32[32,8,128]{2,1,0:T(8,128)} %get-tuple-element.104), calls=%async_computation.1 | async-start | bytes 262144 | tf_op jit(solution)/shard_map/all_to_all | solution.py:513
  29.0 13.0 %collective-permute-done.1.refs_2_ = bf16[2,64,512]{2,1,0:T(8,128)(2,1)S(1)} collective-permute-done((bf16[2,64,512]{2,1,0:T(8,128)(2,1)S(1)}, bf16[2,64,512]{2,1,0:T(8,128)(2,1)S(1)}, u32[]{:S(2)}, u32[]{:S(2)}) %collective-permute-start.1) | collective-permute-done | bytes 131104 | tf_op jit(solution)/shard_map/ppermute | solution.py:515
  42.8 3.4 %collective-permute-start.2 = (bf16[256,256]{1,0:T(8,128)(2,1)S(1)}, bf16[256,256]{1,0:T(8,128)(2,1)S(1)}, u32[]{:S(2)}, u32[]{:S(2)}) collective-permute-start(bf16[256,256]{1,0:T(8,128)(2,1)S(1)} %get-tuple-element.121.fine.refs_1_), channel_id=1, source_target_pairs={{0,32},{32,64},{64,96},{128,160},{160,192},{192,224},{1,33},{33,65... | collective-permute-start | bytes 393224 | tf_op jit(solution)/shard_map/ppermute | solution.py:533
  52.9 4.9 %collective-permute-done.4.refs_1_ = bf16[64,512]{1,0:T(8,128)(2,1)S(1)} collective-permute-done((bf16[64,512]{1,0:T(8,128)(2,1)S(1)}, bf16[64,512]{1,0:T(8,128)(2,1)S(1)}, u32[]{:S(2)}, u32[]{:S(2)}) %collective-permute-start.4) | collective-permute-done | bytes 65568 | tf_op jit(solution)/shard_map/ppermute | solution.py:547
  57.8 6.6 %all-to-all-start.2 = ((f32[32,4,128]{2,1,0:T(4,128)}), f32[32,4,128]{2,1,0:T(4,128)S(1)}, u32[]{:S(2)}, u32[]{:S(2)}) async-start(f32[32,4,128]{2,1,0:T(4,128)} %get-tuple-element.114), calls=%async_computation.2 | async-start | bytes 131072 | tf_op jit(solution)/shard_map/all_to_all | solution.py:484
  64.4 3.7 %shard_map.180 = (f32[64,512]{1,0:T(8,128)S(1)}, f32[4,128]{1,0:T(4,128)S(1)}, f32[4,128]{1,0:T(4,128)S(1)}) custom-call(s32[2]{0:T(128)S(1)} %pad_add_fusion.refs_0_.place, bf16[64,512]{1,0:T(8,128)(2,1)S(1)} %collective-permute-done.4.refs_1_, bf16[2,64,512]{2,1,0:T(8,128)(2,1)} %bitcast.81, bf16[512,512]{1,0:T(8,128)(2,1)} %bitcast.49, ...), custom_call_target="tpu_custom_call" | custom-call | flops 301989888 | bytes 1500000 | tf_op jit(solution)/shard_map/pallas_call | solution.py:40
  72.4 5.9 %all-to-all-start.3 = ((f32[32,8,128]{2,1,0:T(8,128)}), f32[32,8,128]{2,1,0:T(8,128)S(1)}, u32[]{:S(2)}, u32[]{:S(2)}) async-start(f32[32,8,128]{2,1,0:T(8,128)} %get-tuple-element.120), calls=%async_computation.3 | async-start | bytes 262144 | tf_op jit(solution)/shard_map/all_to_all | solution.py:513
  78.4 7.4 %collective-permute-start.9 = (bf16[4,256,256]{2,1,0:T(8,128)(2,1)}, bf16[4,256,256]{2,1,0:T(8,128)(2,1)}, u32[]{:S(2)}, u32[]{:S(2)}) collective-permute-start(bf16[4,256,256]{2,1,0:T(8,128)(2,1)} %get-tuple-element.134), channel_id=1, source_target_pairs={{0,128},{32,160},{64,192},{96,224},{1,129},{33,161},{65,193},{97,2... | collective-permute-start | bytes 1572872 | tf_op jit(solution)/shard_map/ppermute | solution.py:480
  85.8 3.2 %shard_map.182 = (bf16[4,256,256]{2,1,0:T(8,128)(2,1)}, bf16[4,64,512]{2,1,0:T(8,128)(2,1)}, bf16[6,256,256]{2,1,0:T(8,128)(2,1)}, bf16[2,64,512]{2,1,0:T(8,128)(2,1)}) custom-call(s32[2]{0:T(128)S(1)} %pad_add_fusion.refs_0_.place, bf16[256,256]{1,0:T(8,128)(2,1)S(1)} %get-tuple-element.121.fine.refs_1_, ...), custom_call_target="tpu_custom_call" | custom-call | flops 40000000 | bytes 1000000 | tf_op jit(solution)/shard_map/pallas_call | solution.py:40
  92.1 3.4 %collective-permute-start.8 = (bf16[64,512]{1,0:T(8,128)(2,1)S(1)}, bf16[64,512]{1,0:T(8,128)(2,1)S(1)}, u32[]{:S(2)}, u32[]{:S(2)}) collective-permute-start(bf16[64,512]{1,0:T(8,128)(2,1)S(1)} %shard_map.185), channel_id=1, source_target_pairs={{0,32},{32,64},{64,96},{96,128},{128,160},{160,192},{192,224},{224... | collective-permute-start | bytes 196616 | tf_op jit(solution)/shard_map/ppermute | solution.py:547
  98.2 4.4 %collective-permute-done.8.refs_1_ = bf16[64,512]{1,0:T(8,128)(2,1)S(1)} collective-permute-done((bf16[64,512]{1,0:T(8,128)(2,1)S(1)}, bf16[64,512]{1,0:T(8,128)(2,1)S(1)}, u32[]{:S(2)}, u32[]{:S(2)}) %collective-permute-start.8) | collective-permute-done | bytes 65568 | tf_op jit(solution)/shard_map/ppermute | solution.py:547
  102.6 20.3 %all-to-all-start.4 = ((f32[32,4,128]{2,1,0:T(4,128)}), f32[32,4,128]{2,1,0:T(4,128)S(1)}, u32[]{:S(2)}, u32[]{:S(2)}) async-start(f32[32,4,128]{2,1,0:T(4,128)} %get-tuple-element.133), calls=%async_computation.4 | async-start | bytes 131072 | tf_op jit(solution)/shard_map/all_to_all | solution.py:484
  122.9 3.7 %shard_map.186 = (f32[64,512]{1,0:T(8,128)S(1)}, f32[4,128]{1,0:T(4,128)S(1)}, f32[4,128]{1,0:T(4,128)S(1)}) custom-call(s32[2]{0:T(128)S(1)} %pad_add_fusion.refs_0_.place, bf16[64,512]{1,0:T(8,128)(2,1)S(1)} %collective-permute-done.8.refs_1_, bf16[2,64,512]{2,1,0:T(8,128)(2,1)} %copy-done.6, bf16[512,512]{1,0:T(8,128)(2,1)} %bitcast.51, ...), custom_call_target="tpu_custom_call" | custom-call | flops 301989888 | bytes 1500000 | tf_op jit(solution)/shard_map/pallas_call | solution.py:40
  130.9 5.9 %all-to-all-start.5 = ((f32[32,8,128]{2,1,0:T(8,128)}), f32[32,8,128]{2,1,0:T(8,128)S(1)}, u32[]{:S(2)}, u32[]{:S(2)}) async-start(f32[32,8,128]{2,1,0:T(8,128)} %get-tuple-element.142), calls=%async_computation.5 | async-start | bytes 262144 | tf_op jit(solution)/shard_map/all_to_all | solution.py:513
  139.3 5.0 %all-to-all-done.5.gathered = f32[32,8,128]{2,1,0:T(8,128)S(1)} async-done(((f32[32,8,128]{2,1,0:T(8,128)}), f32[32,8,128]{2,1,0:T(8,128)S(1)}, u32[]{:S(2)}, u32[]{:S(2)}) %all-to-all-start.5) | async-done | bytes 131104 | tf_op jit(solution)/shard_map/all_to_all | solution.py:513
  152.2 6.7 %collective-permute-done.13.refs_1_ = bf16[64,512]{1,0:T(8,128)(2,1)S(1)} collective-permute-done((bf16[64,512]{1,0:T(8,128)(2,1)S(1)}, bf16[64,512]{1,0:T(8,128)(2,1)S(1)}, u32[]{:S(2)}, u32[]{:S(2)}) %collective-permute-start.13) | collective-permute-done | bytes 65568 | tf_op jit(solution)/shard_map/ppermute | solution.py:547
  158.9 4.1 %all-to-all-start.6 = ((f32[32,4,128]{2,1,0:T(4,128)}), f32[32,4,128]{2,1,0:T(4,128)S(1)}, u32[]{:S(2)}, u32[]{:S(2)}) async-start(f32[32,4,128]{2,1,0:T(4,128)} %get-tuple-element.159), calls=%async_computation.6 | async-start | bytes 131072 | tf_op jit(solution)/shard_map/all_to_all | solution.py:484
  163.0 3.7 %shard_map.192 = (f32[64,512]{1,0:T(8,128)S(1)}, f32[4,128]{1,0:T(4,128)S(1)}, f32[4,128]{1,0:T(4,128)S(1)}) custom-call(s32[2]{0:T(128)S(1)} %pad_add_fusion.refs_0_.place, bf16[64,512]{1,0:T(8,128)(2,1)S(1)} %collective-permute-done.13.refs_1_, bf16[2,64,512]{2,1,0:T(8,128)(2,1)} %copy-done.6, bf16[512,512]{1,0:T(8,128)(2,1)} %bitcast.53, ...), custom_call_target="tpu_custom_call" | custom-call | flops 301989888 | bytes 1500000 | tf_op jit(solution)/shard_map/pallas_call | solution.py:40
  171.0 5.9 %all-to-all-start.7 = ((f32[32,8,128]{2,1,0:T(8,128)}), f32[32,8,128]{2,1,0:T(8,128)S(1)}, u32[]{:S(2)}, u32[]{:S(2)}) async-start(f32[32,8,128]{2,1,0:T(8,128)} %get-tuple-element.165), calls=%async_computation.7 | async-start | bytes 262144 | tf_op jit(solution)/shard_map/all_to_all | solution.py:513
  180.7 3.7 %all-to-all-done.7.gathered = f32[32,8,128]{2,1,0:T(8,128)S(1)} async-done(((f32[32,8,128]{2,1,0:T(8,128)}), f32[32,8,128]{2,1,0:T(8,128)S(1)}, u32[]{:S(2)}, u32[]{:S(2)}) %all-to-all-start.7) | async-done | bytes 131104 | tf_op jit(solution)/shard_map/all_to_all | solution.py:513
  186.9 7.7 %collective-permute-done.15.received = bf16[2,64,512]{2,1,0:T(8,128)(2,1)S(1)} collective-permute-done((bf16[2,64,512]{2,1,0:T(8,128)(2,1)S(1)}, bf16[2,64,512]{2,1,0:T(8,128)(2,1)S(1)}, u32[]{:S(2)}, u32[]{:S(2)}) %collective-permute-start.15) | collective-permute-done | bytes 131104 | tf_op jit(solution)/shard_map/ppermute | solution.py:522
  (66 shorter events, 49.8 us)
Async XLA Ops:
  4.8 15.5 %all-to-all-start = ((f32[32,4,128]{2,1,0:T(4,128)}), f32[32,4,128]{2,1,0:T(4,128)S(1)}, u32[]{:S(2)}, u32[]{:S(2)}) async-start(f32[32,4,128]{2,1,0:T(4,128)} %get-tuple-element.98), calls=%async_computation | async-start | bytes 131072 | tf_op jit(solution)/shard_map/all_to_all | solution.py:484
  17.4 1.2 collective-permute-start
  21.7 20.4 %all-to-all-start.1 = ((f32[32,8,128]{2,1,0:T(8,128)}), f32[32,8,128]{2,1,0:T(8,128)S(1)}, u32[]{:S(2)}, u32[]{:S(2)}) async-start(f32[32,8,128]{2,1,0:T(8,128)} %get-tuple-element.104), calls=%async_computation.1 | async-start | bytes 262144 | tf_op jit(solution)/shard_map/all_to_all | solution.py:513
  27.7 14.3 %collective-permute-start.1 = (bf16[2,64,512]{2,1,0:T(8,128)(2,1)S(1)}, bf16[2,64,512]{2,1,0:T(8,128)(2,1)S(1)}, u32[]{:S(2)}, u32[]{:S(2)}) collective-permute-start(bf16[2,64,512]{2,1,0:T(8,128)(2,1)S(1)} %bitcast.82), channel_id=1, source_target_pairs={{128,0},{160,32},{192,64},{224,96},{129,1},{161,33},{193,65},{225,... | collective-permute-start | bytes 393224 | tf_op jit(solution)/shard_map/ppermute | solution.py:515
  42.8 7.4 %collective-permute-start.2 = (bf16[256,256]{1,0:T(8,128)(2,1)S(1)}, bf16[256,256]{1,0:T(8,128)(2,1)S(1)}, u32[]{:S(2)}, u32[]{:S(2)}) collective-permute-start(bf16[256,256]{1,0:T(8,128)(2,1)S(1)} %get-tuple-element.121.fine.refs_1_), channel_id=1, source_target_pairs={{0,32},{32,64},{64,96},{128,160},{160,192},{192,224},{1,33},{33,65... | collective-permute-start | bytes 393224 | tf_op jit(solution)/shard_map/ppermute | solution.py:533
  46.2 4.0 %collective-permute-start.3 = (bf16[64,512]{1,0:T(8,128)(2,1)S(1)}, bf16[64,512]{1,0:T(8,128)(2,1)S(1)}, u32[]{:S(2)}, u32[]{:S(2)}) collective-permute-start(bf16[64,512]{1,0:T(8,128)(2,1)S(1)} %get-tuple-element.122.coarse.refs_2_), channel_id=1, source_target_pairs={{96,128},{97,129},{98,130},{99,131},{100,132},{101,133},{102,134},... | collective-permute-start | bytes 196616 | tf_op jit(solution)/shard_map/ppermute | solution.py:532
  47.5 10.4 %collective-permute-start.4 = (bf16[64,512]{1,0:T(8,128)(2,1)S(1)}, bf16[64,512]{1,0:T(8,128)(2,1)S(1)}, u32[]{:S(2)}, u32[]{:S(2)}) collective-permute-start(bf16[64,512]{1,0:T(8,128)(2,1)S(1)} %shard_map.179), channel_id=1, source_target_pairs={{0,32},{32,64},{64,96},{96,128},{128,160},{160,192},{192,224},{224... | collective-permute-start | bytes 196616 | tf_op jit(solution)/shard_map/ppermute | solution.py:547
  57.8 13.3 %all-to-all-start.2 = ((f32[32,4,128]{2,1,0:T(4,128)}), f32[32,4,128]{2,1,0:T(4,128)S(1)}, u32[]{:S(2)}, u32[]{:S(2)}) async-start(f32[32,4,128]{2,1,0:T(4,128)} %get-tuple-element.114), calls=%async_computation.2 | async-start | bytes 131072 | tf_op jit(solution)/shard_map/all_to_all | solution.py:484
  68.1 1.2 collective-permute-start.5
  72.4 16.5 %all-to-all-start.3 = ((f32[32,8,128]{2,1,0:T(8,128)}), f32[32,8,128]{2,1,0:T(8,128)S(1)}, u32[]{:S(2)}, u32[]{:S(2)}) async-start(f32[32,8,128]{2,1,0:T(8,128)} %get-tuple-element.120), calls=%async_computation.3 | async-start | bytes 262144 | tf_op jit(solution)/shard_map/all_to_all | solution.py:513
  78.4 48.4 %collective-permute-start.9 = (bf16[4,256,256]{2,1,0:T(8,128)(2,1)}, bf16[4,256,256]{2,1,0:T(8,128)(2,1)}, u32[]{:S(2)}, u32[]{:S(2)}) collective-permute-start(bf16[4,256,256]{2,1,0:T(8,128)(2,1)} %get-tuple-element.134), channel_id=1, source_target_pairs={{0,128},{32,160},{64,192},{96,224},{1,129},{33,161},{65,193},{97,2... | collective-permute-start | bytes 1572872 | tf_op jit(solution)/shard_map/ppermute | solution.py:480
  89.1 6.4 %collective-permute-start.6 = (bf16[256,256]{1,0:T(8,128)(2,1)S(1)}, bf16[256,256]{1,0:T(8,128)(2,1)S(1)}, u32[]{:S(2)}, u32[]{:S(2)}) collective-permute-start(bf16[256,256]{1,0:T(8,128)(2,1)S(1)} %get-tuple-element.143.fine.refs_1_), channel_id=1, source_target_pairs={{0,32},{32,64},{64,96},{128,160},{160,192},{192,224},{1,33},{33,65... | collective-permute-start | bytes 393224 | tf_op jit(solution)/shard_map/ppermute | solution.py:533
  90.9 4.6 %collective-permute-start.7 = (bf16[64,512]{1,0:T(8,128)(2,1)S(1)}, bf16[64,512]{1,0:T(8,128)(2,1)S(1)}, u32[]{:S(2)}, u32[]{:S(2)}) collective-permute-start(bf16[64,512]{1,0:T(8,128)(2,1)S(1)} %get-tuple-element.144.coarse.refs_2_), channel_id=1, source_target_pairs={{96,128},{97,129},{98,130},{99,131},{100,132},{101,133},{102,134},... | collective-permute-start | bytes 196616 | tf_op jit(solution)/shard_map/ppermute | solution.py:532
  92.1 10.5 %collective-permute-start.8 = (bf16[64,512]{1,0:T(8,128)(2,1)S(1)}, bf16[64,512]{1,0:T(8,128)(2,1)S(1)}, u32[]{:S(2)}, u32[]{:S(2)}) collective-permute-start(bf16[64,512]{1,0:T(8,128)(2,1)S(1)} %shard_map.185), channel_id=1, source_target_pairs={{0,32},{32,64},{64,96},{96,128},{128,160},{160,192},{192,224},{224... | collective-permute-start | bytes 196616 | tf_op jit(solution)/shard_map/ppermute | solution.py:547
  102.6 27.0 %all-to-all-start.4 = ((f32[32,4,128]{2,1,0:T(4,128)}), f32[32,4,128]{2,1,0:T(4,128)S(1)}, u32[]{:S(2)}, u32[]{:S(2)}) async-start(f32[32,4,128]{2,1,0:T(4,128)} %get-tuple-element.133), calls=%async_computation.4 | async-start | bytes 131072 | tf_op jit(solution)/shard_map/all_to_all | solution.py:484
  126.6 3.0 %collective-permute-start.10 = (f32[4,128]{1,0:T(4,128)S(1)}, f32[4,128]{1,0:T(4,128)S(1)}, u32[]{:S(2)}, u32[]{:S(2)}) collective-permute-start(f32[4,128]{1,0:T(4,128)S(1)} %get-tuple-element.140), channel_id=1, source_target_pairs={{0,1},{1,0},{2,3},{3,2},{4,5},{5,4},{6,7},{7,6},{8,9},{9,8},{10,11... | collective-permute-start | bytes 6152 | tf_op jit(solution)/shard_map/ppermute | solution.py:500
  130.9 13.3 %all-to-all-start.5 = ((f32[32,8,128]{2,1,0:T(8,128)}), f32[32,8,128]{2,1,0:T(8,128)S(1)}, u32[]{:S(2)}, u32[]{:S(2)}) async-start(f32[32,8,128]{2,1,0:T(8,128)} %get-tuple-element.142), calls=%async_computation.5 | async-start | bytes 262144 | tf_op jit(solution)/shard_map/all_to_all | solution.py:513
  144.4 5.1 %collective-permute-start.11 = (bf16[256,256]{1,0:T(8,128)(2,1)S(1)}, bf16[256,256]{1,0:T(8,128)(2,1)S(1)}, u32[]{:S(2)}, u32[]{:S(2)}) collective-permute-start(bf16[256,256]{1,0:T(8,128)(2,1)S(1)} %get-tuple-element.166.fine.refs_1_), channel_id=1, source_target_pairs={{0,32},{32,64},{64,96},{128,160},{160,192},{192,224},{1,33},{33,65... | collective-permute-start | bytes 393224 | tf_op jit(solution)/shard_map/ppermute | solution.py:533
  145.7 1.3 collective-permute-start.12
  146.9 12.0 %collective-permute-start.13 = (bf16[64,512]{1,0:T(8,128)(2,1)S(1)}, bf16[64,512]{1,0:T(8,128)(2,1)S(1)}, u32[]{:S(2)}, u32[]{:S(2)}) collective-permute-start(bf16[64,512]{1,0:T(8,128)(2,1)S(1)} %shard_map.191), channel_id=1, source_target_pairs={{0,32},{32,64},{64,96},{96,128},{128,160},{160,192},{192,224},{224... | collective-permute-start | bytes 196616 | tf_op jit(solution)/shard_map/ppermute | solution.py:547
  158.9 10.8 %all-to-all-start.6 = ((f32[32,4,128]{2,1,0:T(4,128)}), f32[32,4,128]{2,1,0:T(4,128)S(1)}, u32[]{:S(2)}, u32[]{:S(2)}) async-start(f32[32,4,128]{2,1,0:T(4,128)} %get-tuple-element.159), calls=%async_computation.6 | async-start | bytes 131072 | tf_op jit(solution)/shard_map/all_to_all | solution.py:484
  166.7 1.2 collective-permute-start.14
  171.0 13.4 %all-to-all-start.7 = ((f32[32,8,128]{2,1,0:T(8,128)}), f32[32,8,128]{2,1,0:T(8,128)S(1)}, u32[]{:S(2)}, u32[]{:S(2)}) async-start(f32[32,8,128]{2,1,0:T(8,128)} %get-tuple-element.165), calls=%async_computation.7 | async-start | bytes 262144 | tf_op jit(solution)/shard_map/all_to_all | solution.py:513
  176.9 17.6 %collective-permute-start.15 = (bf16[2,64,512]{2,1,0:T(8,128)(2,1)S(1)}, bf16[2,64,512]{2,1,0:T(8,128)(2,1)S(1)}, u32[]{:S(2)}, u32[]{:S(2)}) collective-permute-start(bf16[2,64,512]{2,1,0:T(8,128)(2,1)S(1)} %copy-done.7), channel_id=1, source_target_pairs={{128,0},{160,32},{192,64},{224,96},{129,1},{161,33},{193,65},{225,... | collective-permute-start | bytes 393224 | tf_op jit(solution)/shard_map/ppermute | solution.py:522
  (8 other events, 107.0 us)

commit v6 on v5

--- a/solution.py
+++ b/solution.py
@@ -116,8 +116,8 @@
 
 def fine_first(tick, *refs):
     if tick == 0:
-        place, inflow, pending, mixing, kernels = refs[:5]
-        refs = refs[5:]
+        place, inflow, pending, mixing, kernels, cpending = refs[:6]
+        refs = refs[6:]
     else:
         place, arrived, raised_in, entries, raising, pending, mixing, kernels = refs[:8]
         refs = refs[8:]
@@ -157,11 +157,26 @@
         onward = pltpu.make_async_copy(kernels.at[1], second, pack_sems.at[5])
         onward.start()
         loads = [pltpu.make_async_copy(pending.at[slot], staged.at[slot], pack_sems.at[slot]) for slot in range(4)]
+        cloads = [
+            pltpu.make_async_copy(
+                cpending.at[slot, :, pl.ds(side * FCH, FCH)],
+                staged.at[0, pl.ds((2 * slot + side) * CCELLS, CCELLS)],
+                pack_sems.at[2 * slot + side],
+            )
+            for slot in range(2)
+            for side in range(2)
+        ]
         store = pltpu.make_async_copy(staged, packed, pack_sems.at[4])
+        cstore = pltpu.make_async_copy(staged.at[0], packed.at[0], pack_sems.at[4])
 
         @pl.when(segment < HALF)
         def _():
             for copy in loads:
+                copy.start()
+
+        @pl.when(segment >= HALF)
+        def _():
+            for copy in cloads:
                 copy.start()
 
     if tick == 0:
@@ -205,6 +220,12 @@
                 copy.wait()
             store.start()
 
+        @pl.when(segment >= HALF)
+        def _():
+            for copy in cloads:
+                copy.wait()
+            cstore.start()
+
     h = fine_convolution(x_ref[...].astype(F32), padded, kernel)
     h_ref[...] = h
     mean, spread = local_moments(h)
@@ -217,12 +238,26 @@
         def _():
             store.wait()
 
+        @pl.when(segment >= HALF)
+        def _():
+            cstore.wait()
+
 
 def coarse_first(tick, *refs):
     place, arrived, pending, mixing, kernels = refs[:5]
     h_ref, mine_ref, other_ref, x_ref, padded, mix_ref, held, sems, skip_ref = refs[5:]
     kernel = Streamed(kernels, held, sems.at[pl.ds(3, 3)])
-    skips = [pltpu.make_async_copy(pending.at[tick % 2], skip_ref, sems.at[1])]
+    if tick < 2:
+        skips = [pltpu.make_async_copy(pending.at[tick], skip_ref, sems.at[1])]
+    else:
+        skips = [
+            pltpu.make_async_copy(
+                pending.at[0, pl.ds((2 * (tick - 2) + side) * CCELLS, CCELLS)],
+                skip_ref.at[:, pl.ds(side * FCH, FCH)],
+                sems.at[(1, 6)[side]],
+            )
+            for side in range(2)
+        ]
     segment = place[0]
     mix = pltpu.make_async_copy(mixing, mix_ref, sems.at[0])
 
@@ -454,7 +489,7 @@
     for tick in range(TICKS):
         sending = tick < TICKS - 1
         if tick == 0:
-            sources, specs = (inflow, pending, mixing, kernels), [SM, ANY, ANY, ANY, ANY]
+            sources, specs = (inflow, pending, mixing, kernels, cpending), [SM, ANY, ANY, ANY, ANY, ANY]
             more = (pltpu.VMEM((4, CELLS, FCH), BF16), pltpu.SemaphoreType.DMA((6,)))
         else:
             sources = (arrived, raised, entries, upsampling, pending, near_mixing, kernel_one)
@@ -477,7 +512,6 @@
             carrived = cinflow
             packed, kernel_one, kernel_two, near_mixing = handed
             pay, later = tied(pay, place)
-            skips = lax.ppermute(packed, "segment", to_decoder)
         else:
             pay, carrived = tied(pay, carrived)
             later = place
@@ -496,7 +530,7 @@
             ),
             2 * CCELLS * 9 * CCH * CCH,
             1_500_000,
-        )(later, carrived, cpending if tick < 2 else cskips, cmixing, ckernel)
+        )(later, carrived, cpending if tick < 2 else skips, cmixing, ckernel)
         theirs = lax.ppermute(other, "dp", cores)
         if tick == 2:
             gathered, skips = tied(gathered, skips)
@@ -510,11 +544,12 @@
         )(gathered, h1, gains, shifts, kernel_two, mine, theirs)
         if tick > 0:
             pay2, own, cown = tied(pay2, own, cown)
+        if tick == 1:
+            pay2, packed = tied(pay2, packed)
         gathered2 = lax.all_to_all(pay2, "dp", 0, 0, tiled=True)
-        if tick == 0:
-            cskips = lax.ppermute(tied(cpending, pay2)[0], "segment", to_encoder)
-            gathered2, cskips = tied(gathered2, cskips)
-        else:
+        if tick == 1:
+            skips = lax.ppermute(packed, "segment", to_decoder + to_encoder)
+        if tick > 0:
             added = ((pending,), (), (skips,))[tick - 1]
             kept = kept_after(tick - 1, (place, own, cown, mixing, cmixing), added, kept)
             gathered2, *kept = tied(gathered2, *kept)

time: 197 us -> 194 us (0.985)
  starting transfers between devices: 88 us -> 62.7 us
  blocking collectives: 0 us -> 13.2 us
  waiting for transfers between devices: 58.9 us -> 69.6 us
    all_to_all x4 -> x3, waiting for transfers between devices: 8.65 us -> 26.9 us  [on_device(): gathered2 = lax.all_to_all(pay2, 'dp', 0, 0, tiled=True)]
    all_to_all x4, starting transfers between devices: 39.8 us -> 22.4 us  [on_device(): gathered = lax.all_to_all(pay, 'dp', 0, 0, tiled=True)]
    all_to_all x0 -> x1, blocking collectives: none -> 13.2 us  [on_device(): gathered2 = lax.all_to_all(pay2, 'dp', 0, 0, tiled=True)]
    ppermute x2 -> x1, waiting for transfers between devices: 13 us -> 0.01 us  [on_device(): skips = lax.ppermute(packed, 'segment', to_decoder + to_encoder)]
    all_to_all x4 -> x3, starting transfers between devices: 23.8 us -> 17.6 us  [on_device(): gathered2 = lax.all_to_all(pay2, 'dp', 0, 0, tiled=True)]
    ppermute x3, waiting for transfers between devices: 15.9 us -> 19.3 us  [on_device(): carrived = lax.ppermute(going, 'segment', coarse_route)]
    ppermute x3, starting transfers between devices: 5.02 us -> 1.73 us  [on_device(): carrived = lax.ppermute(going, 'segment', coarse_route)]
    ppermute x3, waiting for transfers between devices: 2.44 us -> 4.76 us  [on_device(): arrived = lax.ppermute(own, 'segment', fine_route)]
  transfers between devices with their start and end apart: 24 -> 22, of which waited for: 15 -> 16; matrix products, arithmetic and copies ran while one was open for 1% -> 1% of each run, Pallas kernels for 18% -> 18%
where the time goes in v6:
time: 194 us; the launch traced here: 193 us
  waiting for transfers between devices  69.6 us (36%)
  starting transfers between devices  62.7 us (32%)
  Pallas kernels  45.1 us (23%)
  blocking collectives  13.2 us (7%)
    pallas_call x24, Pallas kernels, call(): kernel(*[placed(spec, arg) for spec, arg in zip(in_specs, args, strict=Tr...  45.1 us
    all_to_all x3, waiting for transfers between devices, on_device(): gathered2 = lax.all_to_all(pay2, 'dp', 0, 0, tiled=True)  26.9 us
    all_to_all x4, starting transfers between devices, on_device(): gathered = lax.all_to_all(pay, 'dp', 0, 0, tiled=True)  22.4 us
    ppermute x3, waiting for transfers between devices, on_device(): carrived = lax.ppermute(going, 'segment', coarse_route)  19.3 us
    all_to_all x3, starting transfers between devices, on_device(): gathered2 = lax.all_to_all(pay2, 'dp', 0, 0, tiled=True)  17.6 us
    all_to_all x1, blocking collectives, on_device(): gathered2 = lax.all_to_all(pay2, 'dp', 0, 0, tiled=True)  13.2 us
    ppermute x1, starting transfers between devices, on_device(): skips = lax.ppermute(packed, 'segment', to_decoder + to_encoder)  10.7 us
    all_to_all x4, waiting for transfers between devices, on_device(): gathered = lax.all_to_all(pay, 'dp', 0, 0, tiled=True)  8.1 us
  transfers between devices with their start and end apart: 22, of which 16 were waited for; matrix products, arithmetic and copies ran while one was open for 1% of the time, Pallas kernels for 18%

profile of v6, /device:TPU:32, one launch (start us, length us, event | category | flops | bytes accessed | tf_op | source)
XLA Modules:
  0.0 193.0 jit_solution(2560223430163702869)
XLA Ops:
  0.7 3.9 %shard_map.174 = (f32[256,256]{1,0:T(8,128)S(1)}, f32[32,4,128]{2,1,0:T(4,128)}, bf16[4,256,256]{2,1,0:T(8,128)(2,1)}, bf16[3,768,256]{2,1,0:T(8,128)(2,1)S(1)},...) custom-call(s32[2]{0:T(128)S(1)} %pad_add_fusion.refs_0_.place, bf16[256,256]{1,0:T(8,128)(2,1)} %bitcast.84, ...), custom_call_target="tpu_custom_call" | custom-call | flops 301989888 | bytes 1000000 | tf_op jit(solution)/shard_map/pallas_call | solution.py:40
  4.6 8.8 %all-to-all-start = ((f32[32,4,128]{2,1,0:T(4,128)}), f32[32,4,128]{2,1,0:T(4,128)S(1)}, u32[]{:S(2)}, u32[]{:S(2)}) async-start(f32[32,4,128]{2,1,0:T(4,128)} %get-tuple-element.97), calls=%async_computation | async-start | bytes 131072 | tf_op jit(solution)/shard_map/all_to_all | solution.py:518
  13.4 3.7 %shard_map.175 = (f32[64,512]{1,0:T(8,128)S(1)}, f32[4,128]{1,0:T(4,128)S(1)}, f32[4,128]{1,0:T(4,128)S(1)}) custom-call(s32[2]{0:T(128)S(1)} %pad_add_fusion.refs_0_.place, bf16[64,512]{1,0:T(8,128)(2,1)} %bitcast.85, bf16[2,64,512]{2,1,0:T(8,128)(2,1)} %bitcast.80, bf16[512,512]{1,0:T(8,128)(2,1)} %bitcast.48, bf16[3,1536,512]{2,1,0:T(8,128)(2,1)} %bitcast.44), custom_call_target="tpu_custom_call" | custom-call | flops 301989888 | bytes 1500000 | tf_op jit(solution)/shard_map/pallas_call | solution.py:40
  20.7 13.2 %all_to_all.40.gathered = f32[32,8,128]{2,1,0:T(8,128)S(1)} all-to-all(f32[32,8,128]{2,1,0:T(8,128)S(1)} %get-tuple-element.103), channel_id=1, replica_groups=mesh['segment'=8,'dp'=32] {'dp'}, dimensions={0} | all-to-all | bytes 262144 | tf_op jit(solution)/shard_map/all_to_all | solution.py:549
  34.1 3.4 %collective-permute-start.1 = (bf16[256,256]{1,0:T(8,128)(2,1)S(1)}, bf16[256,256]{1,0:T(8,128)(2,1)S(1)}, u32[]{:S(2)}, u32[]{:S(2)}) collective-permute-start(bf16[256,256]{1,0:T(8,128)(2,1)S(1)} %get-tuple-element.120.fine.refs_1_), channel_id=1, source_target_pairs={{0,32},{32,64},{64,96},{128,160},{160,192},{192,224},{1,33},{33,65... | collective-permute-start | bytes 393224 | tf_op jit(solution)/shard_map/ppermute | solution.py:568
  44.2 6.1 %collective-permute-done.3.refs_1_ = bf16[64,512]{1,0:T(8,128)(2,1)S(1)} collective-permute-done((bf16[64,512]{1,0:T(8,128)(2,1)S(1)}, bf16[64,512]{1,0:T(8,128)(2,1)S(1)}, u32[]{:S(2)}, u32[]{:S(2)}) %collective-permute-start.3) | collective-permute-done | bytes 65568 | tf_op jit(solution)/shard_map/ppermute | solution.py:582
  50.3 4.2 %all-to-all-start.2 = ((f32[32,4,128]{2,1,0:T(4,128)}), f32[32,4,128]{2,1,0:T(4,128)S(1)}, u32[]{:S(2)}, u32[]{:S(2)}) async-start(f32[32,4,128]{2,1,0:T(4,128)} %get-tuple-element.111), calls=%async_computation.2 | async-start | bytes 131072 | tf_op jit(solution)/shard_map/all_to_all | solution.py:518
  54.6 3.7 %shard_map.180 = (f32[64,512]{1,0:T(8,128)S(1)}, f32[4,128]{1,0:T(4,128)S(1)}, f32[4,128]{1,0:T(4,128)S(1)}) custom-call(s32[2]{0:T(128)S(1)} %pad_add_fusion.refs_0_.place, bf16[64,512]{1,0:T(8,128)(2,1)S(1)} %collective-permute-done.3.refs_1_, bf16[2,64,512]{2,1,0:T(8,128)(2,1)} %bitcast.81, bf16[512,512]{1,0:T(8,128)(2,1)} %bitcast.49, ...), custom_call_target="tpu_custom_call" | custom-call | flops 301989888 | bytes 1500000 | tf_op jit(solution)/shard_map/pallas_call | solution.py:40
  62.5 10.7 %collective-permute-start.8 = (bf16[4,256,256]{2,1,0:T(8,128)(2,1)}, bf16[4,256,256]{2,1,0:T(8,128)(2,1)}, u32[]{:S(2)}, u32[]{:S(2)}) collective-permute-start(bf16[4,256,256]{2,1,0:T(8,128)(2,1)} %get-tuple-element.133), channel_id=1, source_target_pairs={{0,128},{32,160},{64,192},{96,224},{128,0},{160,32},{192,64},{224,... | collective-permute-start | bytes 1572872 | tf_op jit(solution)/shard_map/ppermute | solution.py:551
  73.3 5.7 %all-to-all-start.3 = ((f32[32,8,128]{2,1,0:T(8,128)}), f32[32,8,128]{2,1,0:T(8,128)S(1)}, u32[]{:S(2)}, u32[]{:S(2)}) async-start(f32[32,8,128]{2,1,0:T(8,128)} %get-tuple-element.119), calls=%async_computation.3 | async-start | bytes 262144 | tf_op jit(solution)/shard_map/all_to_all | solution.py:549
  79.0 3.2 %shard_map.182 = (bf16[4,256,256]{2,1,0:T(8,128)(2,1)}, bf16[4,64,512]{2,1,0:T(8,128)(2,1)}, bf16[6,256,256]{2,1,0:T(8,128)(2,1)}, bf16[2,64,512]{2,1,0:T(8,128)(2,1)}) custom-call(s32[2]{0:T(128)S(1)} %pad_add_fusion.refs_0_.place, bf16[256,256]{1,0:T(8,128)(2,1)S(1)} %get-tuple-element.120.fine.refs_1_, ...), custom_call_target="tpu_custom_call" | custom-call | flops 40000000 | bytes 1000000 | tf_op jit(solution)/shard_map/pallas_call | solution.py:40
  82.2 18.2 %all-to-all-done.3.gathered = f32[32,8,128]{2,1,0:T(8,128)S(1)} async-done(((f32[32,8,128]{2,1,0:T(8,128)}), f32[32,8,128]{2,1,0:T(8,128)S(1)}, u32[]{:S(2)}, u32[]{:S(2)}) %all-to-all-start.3) | async-done | bytes 131104 | tf_op jit(solution)/shard_map/all_to_all | solution.py:549
  108.3 6.6 %collective-permute-done.7.refs_1_ = bf16[64,512]{1,0:T(8,128)(2,1)S(1)} collective-permute-done((bf16[64,512]{1,0:T(8,128)(2,1)S(1)}, bf16[64,512]{1,0:T(8,128)(2,1)S(1)}, u32[]{:S(2)}, u32[]{:S(2)}) %collective-permute-start.7) | collective-permute-done | bytes 65568 | tf_op jit(solution)/shard_map/ppermute | solution.py:582
  114.9 5.2 %all-to-all-start.4 = ((f32[32,4,128]{2,1,0:T(4,128)}), f32[32,4,128]{2,1,0:T(4,128)S(1)}, u32[]{:S(2)}, u32[]{:S(2)}) async-start(f32[32,4,128]{2,1,0:T(4,128)} %get-tuple-element.132), calls=%async_computation.4 | async-start | bytes 131072 | tf_op jit(solution)/shard_map/all_to_all | solution.py:518
  120.1 3.7 %shard_map.186 = (f32[64,512]{1,0:T(8,128)S(1)}, f32[4,128]{1,0:T(4,128)S(1)}, f32[4,128]{1,0:T(4,128)S(1)}) custom-call(s32[2]{0:T(128)S(1)} %pad_add_fusion.refs_0_.place, bf16[64,512]{1,0:T(8,128)(2,1)S(1)} %collective-permute-done.7.refs_1_, bf16[4,256,256]{2,1,0:T(8,128)(2,1)} %collective-permute-done.8.refs_2_.refs_5_, bf16[512,512]{1,0:T(8,128)(2,1)} %bitcast.51, ...), custom_call_target="tpu_custom_call" | custom-call | flops 301989888 | bytes 1500000 | tf_op jit(solution)/shard_map/pallas_call | solution.py:40
  124.0 2.8 %all-to-all-done.4.gathered = f32[32,4,128]{2,1,0:T(4,128)S(1)} async-done(((f32[32,4,128]{2,1,0:T(4,128)}), f32[32,4,128]{2,1,0:T(4,128)S(1)}, u32[]{:S(2)}, u32[]{:S(2)}) %all-to-all-start.4) | async-done | bytes 65568 | tf_op jit(solution)/shard_map/all_to_all | solution.py:518
  128.1 5.9 %all-to-all-start.5 = ((f32[32,8,128]{2,1,0:T(8,128)}), f32[32,8,128]{2,1,0:T(8,128)S(1)}, u32[]{:S(2)}, u32[]{:S(2)}) async-start(f32[32,8,128]{2,1,0:T(8,128)} %get-tuple-element.140), calls=%async_computation.5 | async-start | bytes 262144 | tf_op jit(solution)/shard_map/all_to_all | solution.py:549
  136.5 5.0 %all-to-all-done.5.gathered = f32[32,8,128]{2,1,0:T(8,128)S(1)} async-done(((f32[32,8,128]{2,1,0:T(8,128)}), f32[32,8,128]{2,1,0:T(8,128)S(1)}, u32[]{:S(2)}, u32[]{:S(2)}) %all-to-all-start.5) | async-done | bytes 131104 | tf_op jit(solution)/shard_map/all_to_all | solution.py:549
  149.4 6.7 %collective-permute-done.12.refs_1_ = bf16[64,512]{1,0:T(8,128)(2,1)S(1)} collective-permute-done((bf16[64,512]{1,0:T(8,128)(2,1)S(1)}, bf16[64,512]{1,0:T(8,128)(2,1)S(1)}, u32[]{:S(2)}, u32[]{:S(2)}) %collective-permute-start.12) | collective-permute-done | bytes 65568 | tf_op jit(solution)/shard_map/ppermute | solution.py:582
  156.1 4.1 %all-to-all-start.6 = ((f32[32,4,128]{2,1,0:T(4,128)}), f32[32,4,128]{2,1,0:T(4,128)S(1)}, u32[]{:S(2)}, u32[]{:S(2)}) async-start(f32[32,4,128]{2,1,0:T(4,128)} %get-tuple-element.157), calls=%async_computation.6 | async-start | bytes 131072 | tf_op jit(solution)/shard_map/all_to_all | solution.py:518
  160.2 3.7 %shard_map.192 = (f32[64,512]{1,0:T(8,128)S(1)}, f32[4,128]{1,0:T(4,128)S(1)}, f32[4,128]{1,0:T(4,128)S(1)}) custom-call(s32[2]{0:T(128)S(1)} %pad_add_fusion.refs_0_.place, bf16[64,512]{1,0:T(8,128)(2,1)S(1)} %collective-permute-done.12.refs_1_, bf16[4,256,256]{2,1,0:T(8,128)(2,1)} %collective-permute-done.8.refs_2_.refs_5_, bf16[512,512]{1,0:T(8,128)(2,1)} %bitcast.53, ...), custom_call_target="tpu_custom_call" | custom-call | flops 301989888 | bytes 1500000 | tf_op jit(solution)/shard_map/pallas_call | solution.py:40
  168.2 6.0 %all-to-all-start.7 = ((f32[32,8,128]{2,1,0:T(8,128)}), f32[32,8,128]{2,1,0:T(8,128)S(1)}, u32[]{:S(2)}, u32[]{:S(2)}) async-start(f32[32,8,128]{2,1,0:T(8,128)} %get-tuple-element.164), calls=%async_computation.7 | async-start | bytes 262144 | tf_op jit(solution)/shard_map/all_to_all | solution.py:549
  177.9 3.7 %all-to-all-done.7.gathered = f32[32,8,128]{2,1,0:T(8,128)S(1)} async-done(((f32[32,8,128]{2,1,0:T(8,128)}), f32[32,8,128]{2,1,0:T(8,128)S(1)}, u32[]{:S(2)}, u32[]{:S(2)}) %all-to-all-start.7) | async-done | bytes 131104 | tf_op jit(solution)/shard_map/all_to_all | solution.py:549
  184.2 7.5 %collective-permute-done.14.received = bf16[2,64,512]{2,1,0:T(8,128)(2,1)S(1)} collective-permute-done((bf16[2,64,512]{2,1,0:T(8,128)(2,1)S(1)}, bf16[2,64,512]{2,1,0:T(8,128)(2,1)S(1)}, u32[]{:S(2)}, u32[]{:S(2)}) %collective-permute-start.14) | collective-permute-done | bytes 131104 | tf_op jit(solution)/shard_map/ppermute | solution.py:557
  (59 shorter events, 46.3 us)
Async XLA Ops:
  4.6 15.5 %all-to-all-start = ((f32[32,4,128]{2,1,0:T(4,128)}), f32[32,4,128]{2,1,0:T(4,128)S(1)}, u32[]{:S(2)}, u32[]{:S(2)}) async-start(f32[32,4,128]{2,1,0:T(4,128)} %get-tuple-element.97), calls=%async_computation | async-start | bytes 131072 | tf_op jit(solution)/shard_map/all_to_all | solution.py:518
  13.4 20.5 %copy-start.2 = (f32[1,512]{1,0:T(1,128)S(1)}, f32[1,512]{1,0:T(1,128)}, u32[]{:S(2)}) copy-start(f32[1,512]{1,0:T(1,128)} %cgains.7) | copy-start | bytes 6148
  13.4 20.5 %copy-start.3 = (f32[1,512]{1,0:T(1,128)S(1)}, f32[1,512]{1,0:T(1,128)}, u32[]{:S(2)}) copy-start(f32[1,512]{1,0:T(1,128)} %cshifts.7) | copy-start | bytes 6148
  17.1 1.2 collective-permute-start
  34.1 7.4 %collective-permute-start.1 = (bf16[256,256]{1,0:T(8,128)(2,1)S(1)}, bf16[256,256]{1,0:T(8,128)(2,1)S(1)}, u32[]{:S(2)}, u32[]{:S(2)}) collective-permute-start(bf16[256,256]{1,0:T(8,128)(2,1)S(1)} %get-tuple-element.120.fine.refs_1_), channel_id=1, source_target_pairs={{0,32},{32,64},{64,96},{128,160},{160,192},{192,224},{1,33},{33,65... | collective-permute-start | bytes 393224 | tf_op jit(solution)/shard_map/ppermute | solution.py:568
  37.5 3.9 %collective-permute-start.2 = (bf16[64,512]{1,0:T(8,128)(2,1)S(1)}, bf16[64,512]{1,0:T(8,128)(2,1)S(1)}, u32[]{:S(2)}, u32[]{:S(2)}) collective-permute-start(bf16[64,512]{1,0:T(8,128)(2,1)S(1)} %get-tuple-element.121.coarse.refs_2_), channel_id=1, source_target_pairs={{96,128},{97,129},{98,130},{99,131},{100,132},{101,133},{102,134},... | collective-permute-start | bytes 196616 | tf_op jit(solution)/shard_map/ppermute | solution.py:567
  38.8 11.5 %collective-permute-start.3 = (bf16[64,512]{1,0:T(8,128)(2,1)S(1)}, bf16[64,512]{1,0:T(8,128)(2,1)S(1)}, u32[]{:S(2)}, u32[]{:S(2)}) collective-permute-start(bf16[64,512]{1,0:T(8,128)(2,1)S(1)} %shard_map.179), channel_id=1, source_target_pairs={{0,32},{32,64},{64,96},{96,128},{128,160},{160,192},{192,224},{224... | collective-permute-start | bytes 196616 | tf_op jit(solution)/shard_map/ppermute | solution.py:582
  50.3 10.9 %all-to-all-start.2 = ((f32[32,4,128]{2,1,0:T(4,128)}), f32[32,4,128]{2,1,0:T(4,128)S(1)}, u32[]{:S(2)}, u32[]{:S(2)}) async-start(f32[32,4,128]{2,1,0:T(4,128)} %get-tuple-element.111), calls=%async_computation.2 | async-start | bytes 131072 | tf_op jit(solution)/shard_map/all_to_all | solution.py:518
  58.2 1.2 collective-permute-start.4
  62.5 57.5 %collective-permute-start.8 = (bf16[4,256,256]{2,1,0:T(8,128)(2,1)}, bf16[4,256,256]{2,1,0:T(8,128)(2,1)}, u32[]{:S(2)}, u32[]{:S(2)}) collective-permute-start(bf16[4,256,256]{2,1,0:T(8,128)(2,1)} %get-tuple-element.133), channel_id=1, source_target_pairs={{0,128},{32,160},{64,192},{96,224},{128,0},{160,32},{192,64},{224,... | collective-permute-start | bytes 1572872 | tf_op jit(solution)/shard_map/ppermute | solution.py:551
  73.3 27.2 %all-to-all-start.3 = ((f32[32,8,128]{2,1,0:T(8,128)}), f32[32,8,128]{2,1,0:T(8,128)S(1)}, u32[]{:S(2)}, u32[]{:S(2)}) async-start(f32[32,8,128]{2,1,0:T(8,128)} %get-tuple-element.119), calls=%async_computation.3 | async-start | bytes 262144 | tf_op jit(solution)/shard_map/all_to_all | solution.py:549
  100.6 5.0 %collective-permute-start.5 = (bf16[256,256]{1,0:T(8,128)(2,1)S(1)}, bf16[256,256]{1,0:T(8,128)(2,1)S(1)}, u32[]{:S(2)}, u32[]{:S(2)}) collective-permute-start(bf16[256,256]{1,0:T(8,128)(2,1)S(1)} %get-tuple-element.141.fine.refs_1_), channel_id=1, source_target_pairs={{0,32},{32,64},{64,96},{128,160},{160,192},{192,224},{1,33},{33,65... | collective-permute-start | bytes 393224 | tf_op jit(solution)/shard_map/ppermute | solution.py:568
  101.9 1.3 collective-permute-start.6
  103.2 11.7 %collective-permute-start.7 = (bf16[64,512]{1,0:T(8,128)(2,1)S(1)}, bf16[64,512]{1,0:T(8,128)(2,1)S(1)}, u32[]{:S(2)}, u32[]{:S(2)}) collective-permute-start(bf16[64,512]{1,0:T(8,128)(2,1)S(1)} %shard_map.185), channel_id=1, source_target_pairs={{0,32},{32,64},{64,96},{96,128},{128,160},{160,192},{192,224},{224... | collective-permute-start | bytes 196616 | tf_op jit(solution)/shard_map/ppermute | solution.py:582
  114.9 11.9 %all-to-all-start.4 = ((f32[32,4,128]{2,1,0:T(4,128)}), f32[32,4,128]{2,1,0:T(4,128)S(1)}, u32[]{:S(2)}, u32[]{:S(2)}) async-start(f32[32,4,128]{2,1,0:T(4,128)} %get-tuple-element.132), calls=%async_computation.4 | async-start | bytes 131072 | tf_op jit(solution)/shard_map/all_to_all | solution.py:518
  123.8 3.0 %collective-permute-start.9 = (f32[4,128]{1,0:T(4,128)S(1)}, f32[4,128]{1,0:T(4,128)S(1)}, u32[]{:S(2)}, u32[]{:S(2)}) collective-permute-start(f32[4,128]{1,0:T(4,128)S(1)} %get-tuple-element.138), channel_id=1, source_target_pairs={{0,1},{1,0},{2,3},{3,2},{4,5},{5,4},{6,7},{7,6},{8,9},{9,8},{10,11... | collective-permute-start | bytes 6152 | tf_op jit(solution)/shard_map/ppermute | solution.py:534
  128.1 13.4 %all-to-all-start.5 = ((f32[32,8,128]{2,1,0:T(8,128)}), f32[32,8,128]{2,1,0:T(8,128)S(1)}, u32[]{:S(2)}, u32[]{:S(2)}) async-start(f32[32,8,128]{2,1,0:T(8,128)} %get-tuple-element.140), calls=%async_computation.5 | async-start | bytes 262144 | tf_op jit(solution)/shard_map/all_to_all | solution.py:549
  141.6 5.1 %collective-permute-start.10 = (bf16[256,256]{1,0:T(8,128)(2,1)S(1)}, bf16[256,256]{1,0:T(8,128)(2,1)S(1)}, u32[]{:S(2)}, u32[]{:S(2)}) collective-permute-start(bf16[256,256]{1,0:T(8,128)(2,1)S(1)} %get-tuple-element.165.fine.refs_1_), channel_id=1, source_target_pairs={{0,32},{32,64},{64,96},{128,160},{160,192},{192,224},{1,33},{33,65... | collective-permute-start | bytes 393224 | tf_op jit(solution)/shard_map/ppermute | solution.py:568
  142.9 1.3 collective-permute-start.11
  144.2 11.9 %collective-permute-start.12 = (bf16[64,512]{1,0:T(8,128)(2,1)S(1)}, bf16[64,512]{1,0:T(8,128)(2,1)S(1)}, u32[]{:S(2)}, u32[]{:S(2)}) collective-permute-start(bf16[64,512]{1,0:T(8,128)(2,1)S(1)} %shard_map.191), channel_id=1, source_target_pairs={{0,32},{32,64},{64,96},{96,128},{128,160},{160,192},{192,224},{224... | collective-permute-start | bytes 196616 | tf_op jit(solution)/shard_map/ppermute | solution.py:582
  156.1 10.9 %all-to-all-start.6 = ((f32[32,4,128]{2,1,0:T(4,128)}), f32[32,4,128]{2,1,0:T(4,128)S(1)}, u32[]{:S(2)}, u32[]{:S(2)}) async-start(f32[32,4,128]{2,1,0:T(4,128)} %get-tuple-element.157), calls=%async_computation.6 | async-start | bytes 131072 | tf_op jit(solution)/shard_map/all_to_all | solution.py:518
  163.9 1.2 collective-permute-start.13
  168.2 13.4 %all-to-all-start.7 = ((f32[32,8,128]{2,1,0:T(8,128)}), f32[32,8,128]{2,1,0:T(8,128)S(1)}, u32[]{:S(2)}, u32[]{:S(2)}) async-start(f32[32,8,128]{2,1,0:T(8,128)} %get-tuple-element.164), calls=%async_computation.7 | async-start | bytes 262144 | tf_op jit(solution)/shard_map/all_to_all | solution.py:549
  174.2 17.5 %collective-permute-start.14 = (bf16[2,64,512]{2,1,0:T(8,128)(2,1)S(1)}, bf16[2,64,512]{2,1,0:T(8,128)(2,1)S(1)}, u32[]{:S(2)}, u32[]{:S(2)}) collective-permute-start(bf16[2,64,512]{2,1,0:T(8,128)(2,1)S(1)} %copy-done.5), channel_id=1, source_target_pairs={{128,0},{160,32},{192,64},{224,96},{129,1},{161,33},{193,65},{225,... | collective-permute-start | bytes 393224 | tf_op jit(solution)/shard_map/ppermute | solution.py:557
  (4 other events, 47.6 us)
